TPU v7x, 128 devices: a whole 4x4x4 slice. The times are simulated.
128 devices in a mesh: ctx: 16 (over y, x_hi, core), tp: 8 (over x_lo, z).
Axes of the slice: x: 4 (x_hi: 2, x_lo: 2; x = x_hi * 2 + x_lo), y: 4, z: 4, core: 2. Of those that a mesh axis runs over, the one named last changes fastest.
Arguments:
- tokens: bfloat16 [8192, 4096], P('ctx'), may hold values from -6 to 6
- in_weight: bfloat16 [4096, 3, 4096], P('ctx', None, 'tp'), may hold values from -0.09375 to 0.09375
- short_taps: float32 [3, 3, 4096], P(None, None, 'tp'), may hold values from -3 to 3
- long_filter: float32 [4096, 8192], P(('tp', 'ctx'))
- skip_bias: float32 [4096], P(('tp', 'ctx')), may hold values from -4 to 4
- out_grad: bfloat16 [4096, 8192], P('tp', 'ctx'), may hold values from -1.5 to 1.5
Outputs:
- input_grad: bfloat16 [8192, 4096], P(('ctx', 'tp'))
- weight_grad: bfloat16 [4096, 3, 4096], P('ctx', None, 'tp')
- filter_grad: float32 [4096, 8192], P(('tp', 'ctx'))
All inputs are finite; a program needn't handle non-finite values.
Results may differ from a plain program's by a relative error of at most 0.019.
Values may be sent and summed in bfloat16 or wider, within the bound.
A program may use at most 128 MiB of HBM per device.

v0:
```python
import math

import jax
import jax.numpy as jnp
from jax import lax
from jax.sharding import PartitionSpec as P

HIGH = lax.Precision.HIGHEST


def shifted(value, axis, steps):
    count = lax.axis_size(axis)
    first, last = (max(0, -steps), min(count, count - steps))
    return lax.ppermute(value, axis, [(source, source + steps) for source in range(first, last)])


def dft_tables(length):
    size = 2 * length
    lanes = 128
    inner = size // lanes
    half_rows = length // lanes
    freq_inner = jnp.arange(inner, dtype=jnp.int32)
    pos_inner = jnp.arange(half_rows, dtype=jnp.int32)
    lane_index = jnp.arange(lanes, dtype=jnp.int32)
    angle_inner = (
        2.0
        * math.pi
        / inner
        * (freq_inner[:, None] * pos_inner[None, :] % inner).astype(jnp.float32)
    )
    angle_twist = (
        2.0
        * math.pi
        / size
        * (freq_inner[:, None] * lane_index[None, :] % size).astype(jnp.float32)
    )
    angle_outer = (
        2.0
        * math.pi
        / lanes
        * (lane_index[:, None] * lane_index[None, :] % lanes).astype(jnp.float32)
    )
    return (
        jnp.cos(angle_inner),
        jnp.sin(angle_inner),
        jnp.cos(angle_twist),
        jnp.sin(angle_twist),
        jnp.cos(angle_outer),
        jnp.sin(angle_outer),
    )


def forward_dft(signal, tables):
    cos_inner, sin_inner, cos_twist, sin_twist, cos_outer, sin_outer = tables
    rows = signal.reshape(signal.shape[0], cos_inner.shape[1], cos_outer.shape[0])
    first_re = jnp.einsum("kn,cnm->ckm", cos_inner, rows, precision=HIGH)
    first_im = -jnp.einsum("kn,cnm->ckm", sin_inner, rows, precision=HIGH)
    twist_re = first_re * cos_twist + first_im * sin_twist
    twist_im = first_im * cos_twist - first_re * sin_twist
    spec_re = jnp.einsum("ckn,nj->ckj", twist_re, cos_outer, precision=HIGH) + jnp.einsum(
        "ckn,nj->ckj", twist_im, sin_outer, precision=HIGH
    )
    spec_im = jnp.einsum("ckn,nj->ckj", twist_im, cos_outer, precision=HIGH) - jnp.einsum(
        "ckn,nj->ckj", twist_re, sin_outer, precision=HIGH
    )
    return (spec_re, spec_im)


def inverse_dft(spec_re, spec_im, tables):
    cos_inner, sin_inner, cos_twist, sin_twist, cos_outer, sin_outer = tables
    mid_re = jnp.einsum("ckj,jn->ckn", spec_re, cos_outer, precision=HIGH) - jnp.einsum(
        "ckj,jn->ckn", spec_im, sin_outer, precision=HIGH
    )
    mid_im = jnp.einsum("ckj,jn->ckn", spec_im, cos_outer, precision=HIGH) + jnp.einsum(
        "ckj,jn->ckn", spec_re, sin_outer, precision=HIGH
    )
    turn_re = mid_re * cos_twist - mid_im * sin_twist
    turn_im = mid_im * cos_twist + mid_re * sin_twist
    result = jnp.einsum("kn,ckm->cnm", cos_inner, turn_re, precision=HIGH) - jnp.einsum(
        "kn,ckm->cnm", sin_inner, turn_im, precision=HIGH
    )
    size = 2 * cos_inner.shape[1] * cos_outer.shape[0]
    return (result / size).reshape(spec_re.shape[0], size // 2)


def short_forward(values, before, taps):
    extended = jnp.concatenate([before, values], axis=2).astype(jnp.float32)
    return (
        taps[0][:, :, None] * extended[:, :, 2:]
        + taps[1][:, :, None] * extended[:, :, 1:-1]
        + taps[2][:, :, None] * extended[:, :, :-2]
    ).astype(jnp.bfloat16)


def short_backward(values, after, taps):
    extended = jnp.concatenate([values, after], axis=2).astype(jnp.float32)
    return (
        taps[0][:, :, None] * extended[:, :, :-2]
        + taps[1][:, :, None] * extended[:, :, 1:-1]
        + taps[2][:, :, None] * extended[:, :, 2:]
    ).astype(jnp.bfloat16)


def on_device(tokens, in_weight, short_taps, long_filter, skip_bias, out_grad):
    whole_weight = lax.all_gather(in_weight, "ctx", axis=0, tiled=True)
    projected = jnp.einsum("tr,rpc->pct", tokens, whole_weight, preferred_element_type=jnp.float32)
    projected = projected.astype(jnp.bfloat16)
    before = shifted(projected[:, :, -2:], "ctx", 1)
    outgoing = jnp.concatenate(
        [short_forward(projected, before, short_taps), out_grad[None]], axis=0
    )
    arrived = lax.all_to_all(outgoing, "ctx", split_axis=1, concat_axis=2, tiled=True)
    streams = arrived[:3]
    query = streams[0].astype(jnp.float32)
    key_part = streams[1].astype(jnp.float32)
    value_part = streams[2].astype(jnp.float32)
    cotangent = arrived[3].astype(jnp.float32)
    products = key_part * value_part
    weighted = cotangent * query
    tables = dft_tables(long_filter.shape[1])
    prod_re, prod_im = forward_dft(products, tables)
    filt_re, filt_im = forward_dft(long_filter, tables)
    weig_re, weig_im = forward_dft(weighted, tables)
    conv = inverse_dft(
        prod_re * filt_re - prod_im * filt_im, prod_re * filt_im + prod_im * filt_re, tables
    )
    back_conv = inverse_dft(
        filt_re * weig_re + filt_im * weig_im, filt_re * weig_im - filt_im * weig_re, tables
    )
    filter_grad = inverse_dft(
        prod_re * weig_re + prod_im * weig_im, prod_re * weig_im - prod_im * weig_re, tables
    )
    bias = skip_bias[:, None]
    query_grad = cotangent * (conv + bias * products)
    prod_grad = back_conv + bias * weighted
    conv_grad = jnp.stack(
        [query_grad, prod_grad * value_part, prod_grad * key_part], axis=0
    ).astype(jnp.bfloat16)
    returned = lax.all_to_all(conv_grad, "ctx", split_axis=2, concat_axis=1, tiled=True)
    after = shifted(returned[:, :, :2], "ctx", -1)
    proj_grad = short_backward(returned, after, short_taps)
    weight_grad = lax.psum_scatter(
        jnp.einsum("tr,pct->rpc", tokens, proj_grad, preferred_element_type=jnp.float32).astype(
            jnp.bfloat16
        ),
        "ctx",
        scatter_dimension=0,
        tiled=True,
    )
    input_grad = lax.psum_scatter(
        jnp.einsum(
            "pct,rpc->tr", proj_grad, whole_weight, preferred_element_type=jnp.float32
        ).astype(jnp.bfloat16),
        "tp",
        scatter_dimension=0,
        tiled=True,
    )
    return (input_grad, weight_grad, filter_grad)


def solution(mesh):
    in_specs = (
        P("ctx", None),
        P("ctx", None, "tp"),
        P(None, None, "tp"),
        P(("tp", "ctx"), None),
        P(("tp", "ctx")),
        P("tp", "ctx"),
    )
    out_specs = (P(("ctx", "tp"), None), P("ctx", None, "tp"), P(("tp", "ctx"), None))
    return jax.shard_map(
        on_device, mesh=mesh, in_specs=in_specs, out_specs=out_specs, check_vma=False
    )
```

profile of v0, /device:TPU:1, one launch (start us, length us, event | category | flops | bytes accessed | tf_op | source)
XLA Modules:
  0.0 549.1 jit_solution(678517210027749750)
XLA Ops:
  11.3 93.5 %all-gather.2.cloned.1.call-done = bf16[4096,3,512]{2,0,1:T(8,128)(2,1)} async-done(((bf16[256,3,512]{2,0,1:T(8,128)(2,1)}), bf16[4096,3,512]{2,0,1:T(8,128)(2,1)}) %all-gather.2.cloned.1.call-update) | async-done | bytes 12582928 | tf_op jit(solution)/shard_map/all_gather | solution.py:105
  104.8 10.9 %fusion.45 = bf16[3,512,512]{1,2,0:T(8,128)(2,1)S(1)} fusion(bf16[4096,3,512]{2,0,1:T(8,128)(2,1)} %all-gather.2.cloned.1.call-done, bf16[512,4096]{1,0:T(8,128)(2,1)} %param.6), kind=kOutput, calls=%fused_computation.70 | convolution fusion | flops 6443237376 | bytes 18350080 | tf_op jit(solution)/shard_map/tr,rpc->pct/dot_general | solution.py:106
  125.6 4.5 copy.123
  130.1 5.8 %all-to-all-start = ((bf16[4,512,512]{2,0,1:T(4,128)(2,1)}), bf16[4,512,512]{2,0,1:T(4,128)(2,1)}, u32[]{:S(2)}, u32[]{:S(2)}) async-start(bf16[4,512,512]{2,0,1:T(4,128)(2,1)} %copy.123), calls=%async_computation | async-start | bytes 4194304 | tf_op jit(solution)/shard_map/all_to_all | solution.py:112
  143.4 3.5 fusion.51
  146.9 3.5 fusion.48
  150.3 14.2 %all-to-all-done = bf16[4,512,512]{2,0,1:T(4,128)(2,1)} async-done(((bf16[4,512,512]{2,0,1:T(4,128)(2,1)}), bf16[4,512,512]{2,0,1:T(4,128)(2,1)}, u32[]{:S(2)}, u32[]{:S(2)}) %all-to-all-start) | async-done | bytes 2097184 | tf_op jit(solution)/shard_map/all_to_all | solution.py:112
  169.1 3.4 fusion.148
  172.6 4.8 fusion.157
  180.2 3.5 fusion.153
  183.7 3.7 fusion.162
  187.5 3.9 fusion.90
  191.4 3.9 fusion.94
  195.3 4.2 fusion.96
  199.5 3.8 fusion.100
  205.6 3.9 convolution_add_fusion.4
  209.6 4.0 convolution_subtract_fusion.2
  213.6 3.8 convolution_add_fusion.2
  217.4 7.1 %multiply_subtract_fusion = (f32[32,128,128]{2,1,0:T(8,128)S(1)}, f32[32,128,128]{2,1,0:T(8,128)}, f32[32,128,128]{2,1,0:T(8,128)S(1)}, f32[32,128,128]{2,1,0:T(...) fusion(f32[32,128,128]{2,1,0:T(8,128)S(1)} %convolution_add_fusion.2, ...), kind=kOutput, calls=%fused_computation.46 | convolution fusion | flops 817594368 | bytes 29491200 | tf_op jit(solution)/shard_map/ckn,nj->ckj/dot_general | solution.py:63
  236.4 4.2 fusion.69
  242.1 4.0 fusion.130
  255.8 3.8 fusion.75
  267.0 10.6 %copy.153 = bf16[3,32,8192]{1,0,2:T(4,128)(2,1)} copy(bf16[3,32,8192]{2,1,0:T(8,128)(2,1)} %pad_maximum_fusion.1) | data formatting | bytes 3145728 | tf_op jit(solution)/shard_map/stack | solution.py:136
  277.6 13.2 %reshape.255 = bf16[16,2,24576]{2,1,0:T(2,128)(2,1)} reshape(bf16[8192,3,32]{2,1,0:T(4,128)(2,1)} %bitcast.217) | data formatting | bytes 3145728
  290.8 27.8 %all_to_all.33 = bf16[16,2,24576]{2,1,0:T(2,128)(2,1)} all-to-all(bf16[16,2,24576]{2,1,0:T(2,128)(2,1)} %reshape.255), channel_id=1, replica_groups=mesh['ctx'=16,'tp'=8] {'ctx'}, dimensions={0} | all-to-all | bytes 3145728 | tf_op jit(solution)/shard_map/all_to_all | solution.py:139
  318.6 12.6 %reshape.256 = bf16[8192,3,32]{2,1,0:T(4,128)(2,1)} reshape(bf16[16,2,24576]{2,1,0:T(2,128)(2,1)} %all_to_all.33) | data formatting | bytes 3145728
  331.2 11.8 %copy.194 = bf16[3,32,16,512]{3,1,2,0:T(8,128)(2,1)} copy(bf16[3,32,16,512]{1,0,3,2:T(4,128)(2,1)} %bitcast.218) | data formatting | bytes 3145728 | tf_op jit(solution)/shard_map/all_to_all | solution.py:139
  349.4 3.4 collective-permute-done.1
  357.4 9.7 %convert_bitcast_fusion = bf16[4096,3,512]{0,2,1:T(8,128)(2,1)} fusion(bf16[3,512,512]{1,2,0:T(8,128)(2,1)S(1)} %fusion.4, bf16[512,4096]{1,0:T(8,128)(2,1)S(1)} %copy-done.18), kind=kOutput, calls=%fused_computation | convolution fusion | flops 6448742400 | bytes 18350080 | tf_op jit(solution)/shard_map/tr,pct->rpc/dot_general | solution.py:143
  367.1 11.8 %bitcast_convert_fusion = bf16[512,4096]{1,0:T(8,128)(2,1)} fusion(bf16[3,512,512]{1,2,0:T(8,128)(2,1)} %copy-done.15, bf16[4096,3,512]{2,0,1:T(8,128)(2,1)} %all-gather.2.cloned.1.call-done), kind=kOutput, calls=%fused_computation.1 | convolution fusion | flops 6444548096 | bytes 18350080 | tf_op jit(solution)/shard_map/pct,rpc->tr/dot_general | solution.py:151
  395.2 91.8 %reduce-scatter.5.cloned.1.call-done = bf16[256,3,512]{0,2,1:T(8,128)(2,1)} async-done(((bf16[4096,3,512]{0,2,1:T(8,128)(2,1)}), bf16[256,3,512]{0,2,1:T(8,128)(2,1)}) %reduce-scatter.5.cloned.1.call-update) | async-done | bytes 786448 | tf_op jit(solution)/shard_map/reduce_scatter | solution.py:142
  489.3 53.0 %reduce-scatter.3.cloned.1.call-done = bf16[64,4096]{1,0:T(8,128)(2,1)} async-done(((bf16[512,4096]{1,0:T(8,128)(2,1)}), bf16[64,4096]{1,0:T(8,128)(2,1)}) %reduce-scatter.3.cloned.1.call-update) | async-done | bytes 524304 | tf_op jit(solution)/shard_map/reduce_scatter | solution.py:150
  (98 shorter events, 90.9 us)
Async XLA Ops:
  7.2 97.6 %all-gather.2.cloned.1.call-start = ((), (), s32[]{:S(2)}) async-start(), calls=%async_computation.4 | async-start | bytes 13369344 | tf_op jit(solution)/shard_map/all_gather | solution.py:105
  11.3 107.9 %copy-start.16 = (f32[3,3,512]{2,1,0:T(4,128)S(1)}, f32[3,3,512]{2,1,0:T(4,128)}, u32[]{:S(2)}) copy-start(f32[3,3,512]{2,1,0:T(4,128)} %param.8) | copy-start | bytes 55300
  115.7 1.1 copy-start.14
  116.8 4.4 collective-permute-start
  123.1 1.0 copy-start.13
  130.1 34.4 %all-to-all-start = ((bf16[4,512,512]{2,0,1:T(4,128)(2,1)}), bf16[4,512,512]{2,0,1:T(4,128)(2,1)}, u32[]{:S(2)}, u32[]{:S(2)}) async-start(bf16[4,512,512]{2,0,1:T(4,128)(2,1)} %copy.123), calls=%async_computation | async-start | bytes 4194304 | tf_op jit(solution)/shard_map/all_to_all | solution.py:112
  136.0 351.0 %reduce-scatter.5.cloned.1.call-start = ((), (), s32[]{:S(2)}) async-start(), calls=%async_computation.6 | async-start | bytes 13369344 | tf_op jit(solution)/shard_map/reduce_scatter | solution.py:142
  166.6 1.7 copy-start.4
  172.5 4.8 copy-start.12
  191.4 3.9 copy-start
  199.5 3.8 copy-start.5
  213.6 3.8 copy-start.6
  213.6 3.8 copy-start.7
  242.0 4.0 copy-start.3
  248.3 2.3 copy-start.2
  262.0 1.5 copy-start.11
  262.0 1.9 copy-start.10
  263.5 1.3 copy-start.9
  263.8 1.3 copy-start.8
  263.8 1.3 copy-start.17
  346.4 6.4 %collective-permute-start.1 = (bf16[3,512,2]{1,2,0:T(2,128)(2,1)S(1)}, bf16[3,512,2]{1,2,0:T(2,128)(2,1)S(1)}, u32[]{:S(2)}, u32[]{:S(2)}) collective-permute-start(bf16[3,512,2]{1,2,0:T(2,128)(2,1)S(1)} %slice.80), channel_id=1, source_target_pairs={{8,0},{16,8},{24,16},{32,24},{40,32},{48,40},{56,48},{64,56},{72,6... | collective-permute-start | bytes 18440 | tf_op jit(solution)/shard_map/ppermute | solution.py:14
  354.6 2.7 copy-start.18
  355.7 1.2 copy-start.15
  367.1 175.2 %reduce-scatter.3.cloned.1.call-start = ((), (), s32[]{:S(2)}) async-start(), calls=%async_computation.5 | async-start | bytes 4718592 | tf_op jit(solution)/shard_map/reduce_scatter | solution.py:150
  378.9 2.3 copy-start.1
Sparse Core Ops, SparseCore 0:
  10.5 94.2 all-gather.1
  367.2 119.7 reduce-scatter.4
  490.0 52.2 reduce-scatter.2
where the time goes:
time: 557 us; the launch traced here: 549 us
  waiting for transfers between devices  257 us (46%)
  matrix products  146 us (26%)
  local copies, waits for them, and re-layouts  79.2 us (14%)
  blocking collectives  27.8 us (5%)
  between operations  14.5 us (3%)
  other arithmetic  13.2 us (2%)
  starting transfers between devices  11.8 us (2%)
    all_gather x1, waiting for transfers between devices, on_device(): whole_weight = lax.all_gather(in_weight, 'ctx', axis=0, tiled=True)  93.5 us
    reduce_scatter x1, waiting for transfers between devices, on_device(): lax.psum_scatter(jnp.einsum('tr,pct->rpc', tokens, proj_grad, preferred_e...  91.8 us
    reduce_scatter x1, waiting for transfers between devices, on_device(): lax.psum_scatter(jnp.einsum('pct,rpc->tr', proj_grad, whole_weight, prefe...  53 us
    unnamed x44, local copies, waits for them, and re-layouts  37.5 us
    all_to_all x1, blocking collectives, on_device(): lax.all_to_all(conv_grad, 'ctx', split_axis=2, concat_axis=1, tiled=True)  27.8 us
    dot_general x3, matrix products, forward_dft(): jnp.einsum('ckn,nj->ckj', twist_re, sin_outer, precision=HIGH)  14.6 us
    all_to_all x2, local copies, waits for them, and re-layouts, on_device(): lax.all_to_all(conv_grad, 'ctx', split_axis=2, concat_axis=1, tiled=True)  14.4 us
    all_to_all x1, waiting for transfers between devices, on_device(): lax.all_to_all(outgoing, 'ctx', split_axis=1, concat_axis=2, tiled=True)  14.2 us
  transfers between devices with their start and end apart: 6, of which 5 were waited for; matrix products, arithmetic and copies ran while one was open for 9% of the time, Pallas kernels for 0%

commit v1 on v0

v1 whole, which is shorter than its diff:
```python
import functools
import math

import jax
import jax.numpy as jnp
import numpy as np
from jax import lax
from jax.experimental import pallas as pl
from jax.experimental.pallas import tpu as pltpu
from jax.sharding import PartitionSpec as P

MESH = pl.DeviceIdType.MESH
ANY = pl.BlockSpec(memory_space=pl.ANY)
IN_VMEM = pl.BlockSpec(memory_space=pltpu.VMEM)
N_CTX = 16
LANES = 128
BLOCKS = 64
GROUP = 4


def shifted(value, axis, steps):
    count = lax.axis_size(axis)
    first, last = (max(0, -steps), min(count, count - steps))
    return lax.ppermute(value, axis, [(source, source + steps) for source in range(first, last)])


def exchange_kernel(pick, place, src, out, send_sem, recv_sem, local_sem):
    me = lax.axis_index("ctx")
    barrier = pltpu.get_barrier_semaphore()
    for step in range(1, N_CTX):
        pl.semaphore_signal(
            barrier, inc=1, device_id={"ctx": lax.rem(me + step, N_CTX)}, device_id_type=MESH
        )
    pl.semaphore_wait(barrier, N_CTX - 1)
    copies = []
    for step in range(1, N_CTX):
        peer = lax.rem(me + step, N_CTX)
        copy = pltpu.make_async_remote_copy(
            src_ref=pick(src, peer),
            dst_ref=place(out, me),
            send_sem=send_sem.at[step - 1],
            recv_sem=recv_sem.at[step - 1],
            device_id={"ctx": peer},
            device_id_type=MESH,
        )
        copy.start()
        copies.append(copy)
    own = pltpu.make_async_copy(pick(src, me), place(out, me), local_sem)
    own.start()
    own.wait()
    for copy in copies:
        copy.wait()


def rows_of(ref, index):
    return ref.at[:, pl.ds(pl.multiple_of(index * 32, 32), 32), :]


def positions_of(ref, index):
    return ref.at[:, :, pl.ds(pl.multiple_of(index * 512, 512), 512)]


def exchange(value, shape, pick, place, collective_id):
    return pl.pallas_call(
        functools.partial(exchange_kernel, pick, place),
        out_shape=jax.ShapeDtypeStruct(shape, value.dtype),
        in_specs=[ANY],
        out_specs=ANY,
        scratch_shapes=[
            pltpu.SemaphoreType.DMA((N_CTX - 1,)),
            pltpu.SemaphoreType.DMA((N_CTX - 1,)),
            pltpu.SemaphoreType.DMA,
        ],
        compiler_params=pltpu.CompilerParams(collective_id=collective_id, has_side_effects=True),
    )(value)


def tables():
    size = 2 * BLOCKS * LANES
    half = np.arange(BLOCKS) + 0.5
    n = np.arange(BLOCKS)
    m = np.arange(LANES)
    theta = 2 * np.pi * half[:, None] * n[None, :] / LANES
    phi = 2 * np.pi * half[:, None] * m[None, :] / size
    psi = 2 * np.pi * (m[:, None] * m[None, :] % LANES) / LANES
    first = np.concatenate([np.cos(theta), -np.sin(theta)], axis=0)
    second = np.block([[np.cos(psi), -np.sin(psi)], [np.sin(psi), np.cos(psi)]])
    second_back = np.block([[np.cos(psi), np.sin(psi)], [-np.sin(psi), np.cos(psi)]])
    first_back = np.concatenate([np.cos(theta).T, -np.sin(theta).T], axis=1)
    low = lambda value: jnp.asarray(value, jnp.bfloat16)
    turn = jnp.asarray(np.stack([np.cos(phi), np.sin(phi)]), jnp.float32)
    return low(first), low(second), low(second_back), low(first_back), turn


def convolve_kernel(
    arrived, filters, bias, first, second, second_back, first_back, turn, grad, result, held
):
    f32, bf16 = jnp.float32, jnp.bfloat16
    size = 2 * BLOCKS * LANES
    for n in range(BLOCKS):
        at = slice(n * LANES, (n + 1) * LANES)
        rows = slice(n * 32, (n + 1) * 32)
        held[0, rows, :] = arrived[0, :, at].astype(f32)
        held[1, rows, :] = arrived[1, :, at].astype(f32)
        held[2, rows, :] = filters[:, at]

    def dot(a, b):
        return jnp.dot(a, b, preferred_element_type=f32)

    def some(step, carry):
        cos, sin = turn[0], turn[1]
        pairs = [(j, s) for j in range(GROUP) for s in range(3)]
        signals = [
            held[s, pl.ds(step * GROUP + j, BLOCKS, stride=32), :].astype(bf16) for j, s in pairs
        ]
        mixed = dot(first[...], jnp.concatenate(signals, axis=1))
        turned = []
        for index in range(len(pairs)):
            at = slice(index * LANES, (index + 1) * LANES)
            re, im = mixed[:BLOCKS, at], mixed[BLOCKS:, at]
            turned.append(
                jnp.concatenate([re * cos + im * sin, im * cos - re * sin], axis=1).astype(bf16)
            )
        spectra = dot(jnp.concatenate(turned, axis=0), second[...])
        joined = []
        for j in range(GROUP):
            parts = []
            for s in range(3):
                rows = slice((3 * j + s) * BLOCKS, (3 * j + s + 1) * BLOCKS)
                parts.append((spectra[rows, :LANES], spectra[rows, LANES:]))
            (pr, pi), (wr, wi), (hr, hi) = parts
            joined.append(jnp.concatenate([pr * hr - pi * hi, pr * hi + pi * hr], axis=1))
            joined.append(jnp.concatenate([hr * wr + hi * wi, hr * wi - hi * wr], axis=1))
            joined.append(jnp.concatenate([pr * wr + pi * wi, pr * wi - pi * wr], axis=1))
        back = dot(jnp.concatenate(joined, axis=0).astype(bf16), second_back[...])
        cos, sin = cos * (2.0 / size), sin * (2.0 / size)
        unturned = []
        for index in range(len(pairs)):
            rows = slice(index * BLOCKS, (index + 1) * BLOCKS)
            re, im = back[rows, :LANES], back[rows, LANES:]
            unturned.append(
                jnp.concatenate([re * cos - im * sin, im * cos + re * sin], axis=0).astype(bf16)
            )
        final = dot(first_back[...], jnp.concatenate(unturned, axis=1))
        for index, (j, s) in enumerate(pairs):
            held[s, pl.ds(step * GROUP + j, BLOCKS, stride=32), :] = final[
                :, index * LANES : (index + 1) * LANES
            ]
        return carry

    lax.fori_loop(0, 32 // GROUP, some, 0)
    gain = bias[...]
    for n in range(BLOCKS):
        at = slice(n * LANES, (n + 1) * LANES)
        rows = slice(n * 32, (n + 1) * 32)
        for s in range(2):
            result[s, :, at] = (held[s, rows, :] + gain * arrived[s, :, at].astype(f32)).astype(bf16)
        grad[:, at] = held[2, rows, :]


def convolve(arrived, long_filter, skip_bias):
    bias = jnp.broadcast_to(skip_bias[:, None], (32, LANES))
    return pl.pallas_call(
        convolve_kernel,
        out_shape=(
            jax.ShapeDtypeStruct((32, BLOCKS * LANES), jnp.float32),
            jax.ShapeDtypeStruct((2, 32, BLOCKS * LANES), jnp.bfloat16),
        ),
        in_specs=[IN_VMEM] * 8,
        out_specs=(IN_VMEM, IN_VMEM),
        scratch_shapes=[pltpu.VMEM((3, 32 * BLOCKS, LANES), jnp.float32)],
        compiler_params=pltpu.CompilerParams(vmem_limit_bytes=48 * 1024 * 1024),
    )(arrived, long_filter, bias, *tables())


def short_forward(values, before, taps):
    extended = jnp.concatenate([before, values], axis=2).astype(jnp.float32)
    return (
        taps[0][:, :, None] * extended[:, :, 2:]
        + taps[1][:, :, None] * extended[:, :, 1:-1]
        + taps[2][:, :, None] * extended[:, :, :-2]
    ).astype(jnp.bfloat16)


def short_backward(values, after, taps):
    extended = jnp.concatenate([values, after], axis=2).astype(jnp.float32)
    return (
        taps[0][:, :, None] * extended[:, :, :-2]
        + taps[1][:, :, None] * extended[:, :, 1:-1]
        + taps[2][:, :, None] * extended[:, :, 2:]
    ).astype(jnp.bfloat16)


def on_device(tokens, in_weight, short_taps, long_filter, skip_bias, out_grad):
    f32, bf16 = jnp.float32, jnp.bfloat16
    whole_weight = lax.all_gather(in_weight, "ctx", axis=0, tiled=True)
    projected = jnp.einsum("tr,rpc->pct", tokens, whole_weight, preferred_element_type=f32)
    projected = projected.astype(bf16)
    before = shifted(projected[:, :, -2:], "ctx", 1)
    streams = short_forward(projected, before, short_taps).astype(f32)
    cotangent = out_grad.astype(f32)
    outgoing = jnp.stack([streams[1] * streams[2], cotangent * streams[0]]).astype(bf16)
    arrived = exchange(outgoing, (2, 32, 8192), rows_of, positions_of, 1)
    filter_grad, result = convolve(arrived, long_filter, skip_bias)
    returned = exchange(result, (2, 512, 512), positions_of, rows_of, 2).astype(f32)
    conv_grad = jnp.stack(
        [cotangent * returned[0], returned[1] * streams[2], returned[1] * streams[1]], axis=0
    ).astype(bf16)
    after = shifted(conv_grad[:, :, :2], "ctx", -1)
    proj_grad = short_backward(conv_grad, after, short_taps)
    weight_grad = lax.psum_scatter(
        jnp.einsum("tr,pct->rpc", tokens, proj_grad, preferred_element_type=f32).astype(bf16),
        "ctx",
        scatter_dimension=0,
        tiled=True,
    )
    input_grad = lax.psum_scatter(
        jnp.einsum("pct,rpc->tr", proj_grad, whole_weight, preferred_element_type=f32).astype(
            bf16
        ),
        "tp",
        scatter_dimension=0,
        tiled=True,
    )
    return (input_grad, weight_grad, filter_grad)


def solution(mesh):
    in_specs = (
        P("ctx", None),
        P("ctx", None, "tp"),
        P(None, None, "tp"),
        P(("tp", "ctx"), None),
        P(("tp", "ctx")),
        P("tp", "ctx"),
    )
    out_specs = (P(("ctx", "tp"), None), P("ctx", None, "tp"), P(("tp", "ctx"), None))
    return jax.shard_map(
        on_device, mesh=mesh, in_specs=in_specs, out_specs=out_specs, check_vma=False
    )
```

time: 557 us -> 390 us (0.70); the launches traced: 549 us -> 390 us
  matrix products: 146 us -> 43.2 us
  local copies, waits for them, and re-layouts: 79.2 us -> 6.25 us
  Pallas kernels: 0 us -> 49 us
  blocking collectives: 27.8 us -> 0 us
  starting transfers between devices: 11.8 us -> 4.54 us
  waiting for transfers between devices: 257 us -> 263 us
    dot_general x38 -> x2, matrix products: 134 us -> 20.6 us  [the longest x1 11 us: on_device(): jnp.einsum('tr,rpc->pct', tokens, whole_weight, preferred_element_type=f32)]
    pallas_call x0 -> x3, Pallas kernels: none -> 49 us  [the longest x2 38.2 us: exchange(): pl.pallas_call(functools.partial(exchange_kernel, pick, place), out_shape...]
    unnamed x44 -> x31, local copies, waits for them, and re-layouts: 37.5 us -> 6 us
    all_to_all x1 -> x0, blocking collectives: 27.8 us -> none  [on_device(): lax.all_to_all(conv_grad, 'ctx', split_axis=2, concat_axis=1, tiled=True)]
    all_to_all x3 -> x0, local copies, waits for them, and re-layouts: 16.4 us -> none  [the longest x2 14.4 us: on_device(): lax.all_to_all(conv_grad, 'ctx', split_axis=2, concat_axis=1, tiled=True)]
    all_to_all x1 -> x0, waiting for transfers between devices: 14.2 us -> none  [on_device(): lax.all_to_all(outgoing, 'ctx', split_axis=1, concat_axis=2, tiled=True)]
    dot_general x1, matrix products: 11.8 us -> 22.6 us  [on_device(): jnp.einsum('pct,rpc->tr', proj_grad, whole_weight, preferred_element_type...]
    another operation x1 -> x0, local copies, waits for them, and re-layouts: 10.6 us -> none  [on_device(): jnp.stack([query_grad, prod_grad * value_part, prod_grad * key_part], axi...]
  transfers between devices with their start and end apart: 6 -> 5, of which waited for: 5 -> 5; matrix products, arithmetic and copies ran while one was open for 9% -> 6% of each run, Pallas kernels for 0% -> 0%
where the time goes in v1:
time: 390 us
  waiting for transfers between devices  263 us (67%)
  Pallas kernels  49 us (13%)
  matrix products  43.2 us (11%)
  between operations  14 us (4%)
  other arithmetic  10.2 us (3%)
  local copies, waits for them, and re-layouts  6.25 us (2%)
  starting transfers between devices  4.54 us (1%)
    reduce_scatter x1, waiting for transfers between devices, on_device(): lax.psum_scatter(jnp.einsum('tr,pct->rpc', tokens, proj_grad, preferred_e...  99.1 us
    all_gather x1, waiting for transfers between devices, on_device(): whole_weight = lax.all_gather(in_weight, 'ctx', axis=0, tiled=True)  96.8 us
    reduce_scatter x1, waiting for transfers between devices, on_device(): lax.psum_scatter(jnp.einsum('pct,rpc->tr', proj_grad, whole_weight, prefe...  53.1 us
    pallas_call x2, Pallas kernels, exchange(): pl.pallas_call(functools.partial(exchange_kernel, pick, place), out_shape...  38.2 us
    dot_general x1, matrix products, on_device(): jnp.einsum('pct,rpc->tr', proj_grad, whole_weight, preferred_element_type...  22.6 us
    ppermute x2, waiting for transfers between devices, shifted(): lax.ppermute(value, axis, [(source, source + steps) for source in range(f...  13.2 us
    dot_general x1, matrix products, on_device(): jnp.einsum('tr,rpc->pct', tokens, whole_weight, preferred_element_type=f32)  11 us
    pallas_call x1, Pallas kernels, convolve(): pl.pallas_call(convolve_kernel, out_shape=(jax.ShapeDtypeStruct((32, BLOC...  10.8 us
  transfers between devices with their start and end apart: 5, of which 5 were waited for; matrix products, arithmetic and copies ran while one was open for 6% of the time, Pallas kernels for 0%

profile of v1, /device:TPU:1, one launch (start us, length us, event | category | flops | bytes accessed | tf_op | source)
XLA Modules:
  0.0 390.0 jit_solution(7962835225231016605)
XLA Ops:
  7.2 0.7 all-gather.2.cloned.1.call-update
  8.0 96.8 %all-gather.2.cloned.1.call-done = bf16[4096,3,512]{2,0,1:T(8,128)(2,1)} async-done(((bf16[256,3,512]{2,0,1:T(8,128)(2,1)}), bf16[4096,3,512]{2,0,1:T(8,128)(2,1)}) %all-gather.2.cloned.1.call-update) | async-done | bytes 12582928 | tf_op jit(solution)/shard_map/all_gather | solution.py:196
  104.8 11.0 %fusion.9 = bf16[3,512,512]{2,1,0:T(8,128)(2,1)S(1)} fusion(bf16[4096,3,512]{2,0,1:T(8,128)(2,1)} %all-gather.2.cloned.1.call-done, bf16[512,4096]{1,0:T(8,128)(2,1)} %param.11), kind=kOutput, calls=%fused_computation.19 | convolution fusion | flops 6443237376 | bytes 18350080 | tf_op jit(solution)/shard_map/tr,rpc->pct/dot_general | solution.py:197
  115.7 0.2 slice.70
  115.9 2.3 collective-permute-start
  118.2 4.7 %collective-permute-done = bf16[3,512,2]{2,1,0:T(8,128)(2,1)S(1)} collective-permute-done((bf16[3,512,2]{2,1,0:T(8,128)(2,1)S(1)}, bf16[3,512,2]{2,1,0:T(8,128)(2,1)S(1)}, u32[]{:S(2)}, u32[]{:S(2)}) %collective-permute-start) | collective-permute-done | bytes 6176 | tf_op jit(solution)/shard_map/ppermute | solution.py:24
  122.9 0.9 maximum_convert_fusion
  123.8 2.8 fusion.12
  126.6 0.2 multiply_convert_fusion.2
  126.7 1.5 copy-done.8
  128.3 0.2 fusion.16
  128.4 1.1 pad_maximum_fusion.src
  129.5 21.2 %shard_map.130.arrived = bf16[2,32,8192]{2,1,0:T(8,128)(2,1)} custom-call(bf16[2,512,512]{2,1,0:T(8,128)(2,1)} %pad_maximum_fusion.src), custom_call_target="tpu_custom_call" | custom-call | tf_op jit(solution)/shard_map/pallas_call | solution.py:64
  150.7 0.1 broadcast_in_dim.2.bias
  150.9 1.2 copy-done
  152.1 10.8 %shard_map.131 = (f32[32,8192]{1,0:T(8,128)}, bf16[2,32,8192]{2,1,0:T(8,128)(2,1)S(1)}) custom-call(bf16[2,32,8192]{2,1,0:T(8,128)(2,1)S(1)} %copy-done, f32[32,8192]{1,0:T(8,128)S(1)} %copy-done.1, f32[32,128]{1,0:T(8,128)S(1)} %broadcast_in_dim.2.bias, bf16[128,64]{1,0:T(8,128)(2,1)S(1)} %copy-done.6, bf16[256,256]{1,0:T(8,128)(2,1)S(1)} %copy-done.4, ...), custom_call_target="tpu_custom_call" | custom-call | tf_op jit(solution)/shard_map/pallas_call | solution.py:163
  162.9 1.0 copy-done.2
  163.9 16.9 %shard_map.132 = bf16[2,512,512]{2,1,0:T(8,128)(2,1)} custom-call(bf16[2,32,8192]{2,1,0:T(8,128)(2,1)} %copy-done.2), custom_call_target="tpu_custom_call" | custom-call | tf_op jit(solution)/shard_map/pallas_call | solution.py:64
  180.8 1.6 convert_element_type.40
  182.4 0.4 multiply_convert_fusion.1
  182.8 0.2 fusion.15
  183.0 0.1 pad_maximum_fusion.1
  183.1 2.1 collective-permute-start.1
  185.2 8.5 %collective-permute-done.1 = bf16[3,512,2]{2,1,0:T(8,128)(2,1)S(1)} collective-permute-done((bf16[3,512,2]{2,1,0:T(8,128)(2,1)S(1)}, bf16[3,512,2]{2,1,0:T(8,128)(2,1)S(1)}, u32[]{:S(2)}, u32[]{:S(2)}) %collective-permute-start.1) | collective-permute-done | bytes 6176 | tf_op jit(solution)/shard_map/ppermute | solution.py:24
  193.7 0.3 maximum_convert_fusion.1
  194.0 2.8 fusion.4
  196.7 9.6 %convert_bitcast_fusion = bf16[4096,3,512]{0,2,1:T(8,128)(2,1)} fusion(bf16[3,512,512]{2,1,0:T(8,128)(2,1)S(1)} %fusion.4, bf16[512,4096]{1,0:T(8,128)(2,1)S(1)} %copy-done.14), kind=kOutput, calls=%fused_computation | convolution fusion | flops 6448742400 | bytes 18350080 | tf_op jit(solution)/shard_map/tr,pct->rpc/dot_general | solution.py:212
  206.4 0.0 reduce-scatter.3.cloned.1.call-start
  206.4 22.6 %bitcast_convert_fusion = bf16[512,4096]{1,0:T(8,128)(2,1)} fusion(bf16[3,512,512]{2,1,0:T(8,128)(2,1)S(1)} %fusion.4, bf16[4096,3,512]{2,0,1:T(8,128)(2,1)} %all-gather.2.cloned.1.call-done), kind=kOutput, calls=%fused_computation.1 | convolution fusion | flops 6444548096 | bytes 18350080 | tf_op jit(solution)/shard_map/pct,rpc->tr/dot_general | solution.py:218
  229.1 99.1 %reduce-scatter.5.cloned.1.call-done = bf16[256,3,512]{0,2,1:T(8,128)(2,1)} async-done(((bf16[4096,3,512]{0,2,1:T(8,128)(2,1)}), bf16[256,3,512]{0,2,1:T(8,128)(2,1)}) %reduce-scatter.5.cloned.1.call-update) | async-done | bytes 786448 | tf_op jit(solution)/shard_map/reduce_scatter | solution.py:211
  328.2 2.3 copy.16
  330.4 53.1 %reduce-scatter.3.cloned.1.call-done = bf16[64,4096]{1,0:T(8,128)(2,1)} async-done(((bf16[512,4096]{1,0:T(8,128)(2,1)}), bf16[64,4096]{1,0:T(8,128)(2,1)}) %reduce-scatter.3.cloned.1.call-update) | async-done | bytes 524304 | tf_op jit(solution)/shard_map/reduce_scatter | solution.py:217
  (32 shorter events, 0.2 us)
Async XLA Ops:
  7.2 97.6 %all-gather.2.cloned.1.call-start = ((), (), s32[]{:S(2)}) async-start(), calls=%async_computation.2 | async-start | bytes 13369344 | tf_op jit(solution)/shard_map/all_gather | solution.py:196
  7.9 110.3 %copy-start.12 = (f32[3,3,512]{2,1,0:T(4,128)S(1)}, f32[3,3,512]{2,1,0:T(4,128)}, u32[]{:S(2)}) copy-start(f32[3,3,512]{2,1,0:T(4,128)} %param.13) | copy-start | bytes 55300
  7.9 320.2 %reduce-scatter.5.cloned.1.call-start = ((), (), s32[]{:S(2)}) async-start(), calls=%async_computation.4 | async-start | bytes 13369344 | tf_op jit(solution)/shard_map/reduce_scatter | solution.py:211
  115.9 7.0 %collective-permute-start = (bf16[3,512,2]{2,1,0:T(8,128)(2,1)S(1)}, bf16[3,512,2]{2,1,0:T(8,128)(2,1)S(1)}, u32[]{:S(2)}, u32[]{:S(2)}) collective-permute-start(bf16[3,512,2]{2,1,0:T(8,128)(2,1)S(1)} %slice.70), channel_id=1, source_target_pairs={{0,8},{8,16},{16,24},{24,32},{32,40},{40,48},{48,56},{56,64},{64,7... | collective-permute-start | bytes 18440 | tf_op jit(solution)/shard_map/ppermute | solution.py:24
  123.8 4.4 %copy-start.10 = (bf16[512,512]{1,0:T(8,128)(2,1)S(1)}, bf16[512,512]{1,0:T(8,128)(2,1)}, u32[]{:S(2)}) copy-start(bf16[512,512]{1,0:T(8,128)(2,1)} %param.16) | copy-start | bytes 1572868
  126.6 1.6 copy-start.8
  128.2 22.5 %copy-start.13 = (f32[32]{0:T(128)S(1)}, f32[32]{0:T(128)}, u32[]{:S(2)}) copy-start(f32[32]{0:T(128)} %param.15) | copy-start | bytes 388
  128.2 22.6 %copy-start.1 = (f32[32,8192]{1,0:T(8,128)S(1)}, f32[32,8192]{1,0:T(8,128)}, u32[]{:S(2)}) copy-start(f32[32,8192]{1,0:T(8,128)} %filters.1) | copy-start | bytes 3145732
  128.2 22.6 %copy-start.3 = (bf16[256,256]{1,0:T(8,128)(2,1)S(1)}, bf16[256,256]{1,0:T(8,128)(2,1)}, u32[]{:S(2)}) copy-start(bf16[256,256]{1,0:T(8,128)(2,1)} %constant.13.clone.second_back) | copy-start | bytes 393220
  128.2 22.6 %copy-start.4 = (bf16[256,256]{1,0:T(8,128)(2,1)S(1)}, bf16[256,256]{1,0:T(8,128)(2,1)}, u32[]{:S(2)}) copy-start(bf16[256,256]{1,0:T(8,128)(2,1)} %constant.12.clone.second) | copy-start | bytes 393220
  128.2 22.6 %copy-start.5 = (f32[2,64,128]{2,1,0:T(8,128)S(1)}, f32[2,64,128]{2,1,0:T(8,128)}, u32[]{:S(2)}) copy-start(f32[2,64,128]{2,1,0:T(8,128)} %constant.10.clone.turn) | copy-start | bytes 196612
  128.2 22.6 %copy-start.6 = (bf16[128,64]{1,0:T(8,128)(2,1)S(1)}, bf16[128,64]{1,0:T(8,128)(2,1)}, u32[]{:S(2)}) copy-start(bf16[128,64]{1,0:T(8,128)(2,1)} %constant.11.clone.first) | copy-start | bytes 49156
  128.3 22.6 %copy-start.7 = (bf16[64,128]{1,0:T(8,128)(2,1)S(1)}, bf16[64,128]{1,0:T(8,128)(2,1)}, u32[]{:S(2)}) copy-start(bf16[64,128]{1,0:T(8,128)(2,1)} %constant.14.clone.first_back) | copy-start | bytes 49156
  150.9 1.2 copy-start
  162.9 1.0 copy-start.2
  163.9 18.5 %copy-start.9 = (f32[3,512,512]{2,1,0:T(8,128)S(1)}, f32[3,512,512]{2,1,0:T(8,128)}, u32[]{:S(2)}) copy-start(f32[3,512,512]{2,1,0:T(8,128)} %copy-done.8) | copy-start | bytes 9437188
  180.8 2.0 copy-start.11
  183.1 10.6 %collective-permute-start.1 = (bf16[3,512,2]{2,1,0:T(8,128)(2,1)S(1)}, bf16[3,512,2]{2,1,0:T(8,128)(2,1)S(1)}, u32[]{:S(2)}, u32[]{:S(2)}) collective-permute-start(bf16[3,512,2]{2,1,0:T(8,128)(2,1)S(1)} %pad_maximum_fusion.1), channel_id=1, source_target_pairs={{8,0},{16,8},{24,16},{32,24},{40,32},{48,40},{56,48},{64,56},{72,6... | collective-permute-start | bytes 18440 | tf_op jit(solution)/shard_map/ppermute | solution.py:24
  194.0 2.8 copy-start.14
  206.4 177.1 %reduce-scatter.3.cloned.1.call-start = ((), (), s32[]{:S(2)}) async-start(), calls=%async_computation.3 | async-start | bytes 4718592 | tf_op jit(solution)/shard_map/reduce_scatter | solution.py:217
Sparse Core Ops, SparseCore 0:
  10.5 94.2 all-gather.1
  206.5 121.6 reduce-scatter.4
  331.1 52.3 reduce-scatter.2

commit v2 on v1

--- a/solution.py
+++ b/solution.py
@@ -173,6 +173,227 @@
     )(arrived, long_filter, bias, *tables())
 
 
+def places():
+    me, b = lax.axis_index("ctx"), lax.axis_index("tp")
+    core, xh, y = lax.rem(me, 2), lax.rem(me // 2, 2), me // 4
+    z, xl = lax.rem(b, 4), b // 4
+    ctx_of = lambda y, xh: (y * 2 + xh) * 2 + core
+    return dict(
+        core=core,
+        xh=xh,
+        y=y,
+        z=z,
+        xl=xl,
+        twin={"ctx": me + 1 - 2 * core},
+        up={"ctx": ctx_of(lax.rem(y + 1, 4), xh)},
+        down={"ctx": ctx_of(lax.rem(y + 3, 4), xh)},
+        near={"ctx": me, "tp": (1 - xl) * 4 + z},
+        far={"ctx": ctx_of(y, 1 - xh), "tp": (1 - xl) * 4 + z},
+        above={"tp": xl * 4 + lax.rem(z + 1, 4)},
+        below={"tp": xl * 4 + lax.rem(z + 3, 4)},
+    )
+
+
+def greet(peers):
+    barrier = pltpu.get_barrier_semaphore()
+    for peer in peers:
+        pl.semaphore_signal(barrier, inc=1, device_id=peer, device_id_type=MESH)
+    pl.semaphore_wait(barrier, len(peers))
+
+
+def reduce_kernel(
+    pgc, pgt, tokens, others, weight, ig_out, wg_out,
+    tok, oth, wei, pgo, ig, acc, part, r2, rf, relay, xr, z2, zf, xz, send, recv, load,
+):
+    f32, bf16 = jnp.float32, jnp.bfloat16
+    at = places()
+    core, xh, y, z, xl = at["core"], at["xh"], at["y"], at["z"], at["xl"]
+    loads = [
+        pltpu.make_async_copy(weight.at[pl.ds(0, 2048)], wei.at[pl.ds(0, 2048)], load.at[0]),
+        pltpu.make_async_copy(tokens, tok, load.at[1]),
+        pltpu.make_async_copy(others, oth, load.at[2]),
+        pltpu.make_async_copy(weight.at[pl.ds(2048, 2048)], wei.at[pl.ds(2048, 2048)], load.at[3]),
+    ]
+    for one in loads:
+        one.start()
+    greet([at[name] for name in ("twin", "up", "down", "near", "far", "above", "below")])
+    sent = {}
+
+    def start(name, src, dst, peer):
+        index = len(sent)
+        copy = pltpu.make_async_remote_copy(
+            src_ref=src,
+            dst_ref=dst,
+            send_sem=send.at[index],
+            recv_sem=recv.at[index],
+            device_id=at[peer],
+            device_id_type=MESH,
+        )
+        copy.start()
+        sent[name] = copy
+
+    def arrived(name):
+        sent[name].wait_recv()
+
+    def input_tiles(first):
+        def tile(step, carry):
+            rows = pl.ds(pl.multiple_of((first + step) * 256, 256), 256)
+            ig[:, rows] = lax.dot_general(
+                pgt[...], wei[rows, :], (((1,), (1,)), ((), ())), preferred_element_type=f32
+            ).astype(bf16)
+            return carry
+
+        lax.fori_loop(0, 8, tile, 0)
+
+    def weight_part(block):
+        mine = pl.ds(pl.multiple_of((2 * block + core) * 256, 256), 256)
+        theirs = pl.ds(pl.multiple_of(block * 256, 256), 256)
+
+        def half(step, carry):
+            rows = pl.ds(pl.multiple_of(step * 768, 256), 768)
+            acc[rows, :] = jnp.dot(pgc[rows, :], tok[:, mine], preferred_element_type=f32) + jnp.dot(
+                pgo[rows, :], oth[:, theirs], preferred_element_type=f32
+            )
+            return carry
+
+        lax.fori_loop(0, 2, half, 0)
+
+    def fold(dst, first, last, *terms):
+        def chunk(step, carry):
+            rows = pl.ds(pl.multiple_of(step * 128, 128), 128)
+            total = acc[rows, :]
+            for term, offset in terms:
+                part_rows = pl.ds(pl.multiple_of(step * 128 - offset, 128), 128)
+                total = total + term[part_rows, :].astype(f32)
+            dst[rows, :] = total.astype(bf16)
+            return carry
+
+        lax.fori_loop(first // 128, last // 128, chunk, 0)
+
+    def block_of(y, xh):
+        return y * 2 + xh
+
+    y2, yp, ym = lax.rem(y + 2, 4), lax.rem(y + 1, 4), lax.rem(y + 3, 4)
+    z2i, zp, zm = lax.rem(z + 2, 4), lax.rem(z + 1, 4), lax.rem(z + 3, 4)
+    columns = (1 - xh, xh)
+    sides = (1 - xl, xl)
+    low, high = pl.ds(0, 768), pl.ds(768, 768)
+
+    start("twin", pgc, pgo, "twin")
+    loads[0].wait()
+    input_tiles(0)
+    loads[1].wait()
+    loads[2].wait()
+    arrived("twin")
+    for k in range(2):
+        weight_part(block_of(y2, columns[k]))
+        fold(part.at[k], 0, 1536)
+        start(("2p", k), part.at[k, low], r2.at[k, 0], "up")
+        start(("2m", k), part.at[k, high], r2.at[k, 1], "down")
+    loads[3].wait()
+    input_tiles(8)
+
+    def ig_rows(side, z, first, count):
+        return pl.ds(pl.multiple_of((side * 4 + z) * 64 + first, 32), count)
+
+    for k in range(2):
+        start(("z2p", k), ig.at[ig_rows(sides[k], z2i, 0, 32)], z2.at[k, 0], "above")
+        start(("z2m", k), ig.at[ig_rows(sides[k], z2i, 32, 32)], z2.at[k, 1], "below")
+
+    def ig_add(rows, *terms):
+        total = ig[rows, :].astype(f32)
+        for term in terms:
+            total = total + term[...].astype(f32)
+        return total
+
+    for k in range(2):
+        weight_part(block_of(yp, columns[k]))
+        arrived(("2p", k))
+        fold(part.at[2 + 2 * k], 0, 768, (r2.at[k, 0], 0))
+        fold(part.at[2 + 2 * k], 768, 1536)
+        start(("fp", k), part.at[2 + 2 * k], rf.at[k, 0], "up")
+        weight_part(block_of(ym, columns[k]))
+        arrived(("2m", k))
+        fold(part.at[3 + 2 * k], 0, 768)
+        fold(part.at[3 + 2 * k], 768, 1536, (r2.at[k, 1], 768))
+        start(("fm", k), part.at[3 + 2 * k], rf.at[k, 1], "down")
+        arrived(("z2p", k))
+        rows = ig_rows(sides[k], zp, 0, 32)
+        ig[rows, :] = ig_add(rows, z2.at[k, 0]).astype(bf16)
+        start(("zfp", k), ig.at[ig_rows(sides[k], zp, 0, 64)], zf.at[k, 0], "above")
+        arrived(("z2m", k))
+        rows = ig_rows(sides[k], zm, 32, 32)
+        ig[rows, :] = ig_add(rows, z2.at[k, 1]).astype(bf16)
+        start(("zfm", k), ig.at[ig_rows(sides[k], zm, 0, 64)], zf.at[k, 1], "below")
+
+    weight_part(block_of(y, columns[0]))
+    arrived(("fp", 0))
+    arrived(("fm", 0))
+    fold(part.at[6], 0, 1536, (rf.at[0, 0], 0), (rf.at[0, 1], 0))
+    start("xa", part.at[6, low], relay.at[0], "near")
+    start("xb", part.at[6, high], relay.at[1], "far")
+    arrived(("zfp", 0))
+    arrived(("zfm", 0))
+    rows = ig_rows(sides[0], z, 0, 64)
+    ig[rows, :] = ig_add(rows, zf.at[0, 0], zf.at[0, 1]).astype(bf16)
+    start("xz", ig.at[rows], xz, "near")
+    arrived("xa")
+    start("ya", relay.at[0], xr.at[low], "far")
+    arrived("xb")
+    start("yb", relay.at[1], xr.at[high], "near")
+    weight_part(block_of(y, columns[1]))
+    arrived(("zfp", 1))
+    arrived(("zfm", 1))
+    arrived("xz")
+    ig_out[...] = ig_add(ig_rows(sides[1], z, 0, 64), zf.at[1, 0], zf.at[1, 1], xz).astype(bf16)
+    arrived(("fp", 1))
+    arrived(("fm", 1))
+    arrived("ya")
+    arrived("yb")
+    fold(wg_out, 0, 1536, (rf.at[1, 0], 0), (rf.at[1, 1], 0), (xr, 0))
+    for copy in sent.values():
+        copy.wait_send()
+
+
+def gradients(pgc, pgt, tokens, others, weight):
+    bf16 = jnp.bfloat16
+    vmem = lambda *shape: pltpu.VMEM(shape, bf16)
+    return pl.pallas_call(
+        reduce_kernel,
+        out_shape=(
+            jax.ShapeDtypeStruct((64, 4096), bf16),
+            jax.ShapeDtypeStruct((1536, 256), bf16),
+        ),
+        in_specs=[IN_VMEM, IN_VMEM, ANY, ANY, ANY],
+        out_specs=(IN_VMEM, IN_VMEM),
+        scratch_shapes=[
+            vmem(512, 4096),
+            vmem(512, 2048),
+            vmem(4096, 1536),
+            vmem(1536, 512),
+            vmem(512, 4096),
+            pltpu.VMEM((1536, 256), jnp.float32),
+            vmem(7, 1536, 256),
+            vmem(2, 2, 768, 256),
+            vmem(2, 2, 1536, 256),
+            vmem(2, 768, 256),
+            vmem(1536, 256),
+            vmem(2, 2, 32, 4096),
+            vmem(2, 2, 64, 4096),
+            vmem(64, 4096),
+            pltpu.SemaphoreType.DMA((22,)),
+            pltpu.SemaphoreType.DMA((22,)),
+            pltpu.SemaphoreType.DMA((4,)),
+        ],
+        compiler_params=pltpu.CompilerParams(
+            collective_id=3, has_side_effects=True, vmem_limit_bytes=56 * 1024 * 1024
+        ),
+        cost_estimate=pl.CostEstimate(
+            flops=4 * 512 * 4096 * 1536, bytes_accessed=24 * 1024 * 1024, transcendentals=0
+        ),
+    )(pgc, pgt, tokens, others, weight)
+
+
 def short_forward(values, before, taps):
     extended = jnp.concatenate([before, values], axis=2).astype(jnp.float32)
     return (
@@ -193,9 +414,15 @@
 
 def on_device(tokens, in_weight, short_taps, long_filter, skip_bias, out_grad):
     f32, bf16 = jnp.float32, jnp.bfloat16
-    whole_weight = lax.all_gather(in_weight, "ctx", axis=0, tiled=True)
-    projected = jnp.einsum("tr,rpc->pct", tokens, whole_weight, preferred_element_type=f32)
-    projected = projected.astype(bf16)
+    me = lax.axis_index("ctx")
+    cut = tokens.reshape(512, 8, 2, 256)
+    theirs = lax.dynamic_index_in_dim(cut, 1 - lax.rem(me, 2), 2, keepdims=False).reshape(512, 2048)
+    others = lax.ppermute(theirs, "ctx", [(index, index ^ 1) for index in range(N_CTX)])
+    whole_weight = lax.all_gather(in_weight.reshape(256, 1536), "ctx", axis=0, tiled=True)
+    projected = lax.dot_general(
+        whole_weight, tokens, (((0,), (1,)), ((), ())), preferred_element_type=f32
+    )
+    projected = projected.astype(bf16).reshape(3, 512, 512)
     before = shifted(projected[:, :, -2:], "ctx", 1)
     streams = short_forward(projected, before, short_taps).astype(f32)
     cotangent = out_grad.astype(f32)
@@ -207,22 +434,9 @@
         [cotangent * returned[0], returned[1] * streams[2], returned[1] * streams[1]], axis=0
     ).astype(bf16)
     after = shifted(conv_grad[:, :, :2], "ctx", -1)
-    proj_grad = short_backward(conv_grad, after, short_taps)
-    weight_grad = lax.psum_scatter(
-        jnp.einsum("tr,pct->rpc", tokens, proj_grad, preferred_element_type=f32).astype(bf16),
-        "ctx",
-        scatter_dimension=0,
-        tiled=True,
-    )
-    input_grad = lax.psum_scatter(
-        jnp.einsum("pct,rpc->tr", proj_grad, whole_weight, preferred_element_type=f32).astype(
-            bf16
-        ),
-        "tp",
-        scatter_dimension=0,
-        tiled=True,
-    )
-    return (input_grad, weight_grad, filter_grad)
+    proj_grad = short_backward(conv_grad, after, short_taps).reshape(1536, 512)
+    input_grad, weight_grad = gradients(proj_grad, proj_grad.T, tokens, others, whole_weight)
+    return (input_grad, weight_grad.T.reshape(256, 3, 512), filter_grad)
 
 
 def solution(mesh):

time: 390 us -> 289 us (0.74)
  waiting for transfers between devices: 263 us -> 83.7 us
  Pallas kernels: 49 us -> 127 us
  matrix products: 43.2 us -> 11 us
  local copies, waits for them, and re-layouts: 6.25 us -> 36 us
    reduce_scatter x2 -> x0, waiting for transfers between devices: 152 us -> none  [the longest x1 99.1 us: on_device(): lax.psum_scatter(jnp.einsum('tr,pct->rpc', tokens, proj_grad, preferred_e...]
    pallas_call x0 -> x1, Pallas kernels: none -> 78.1 us  [gradients(): pl.pallas_call(reduce_kernel, out_shape=(jax.ShapeDtypeStruct((64, 4096),...]
    dot_general x3 -> x1, matrix products: 43.2 us -> 11 us  [on_device(): lax.dot_general(whole_weight, tokens, (((0,), (1,)), ((), ())), preferred...]
    all_gather x1, waiting for transfers between devices: 96.8 us -> 70.8 us  [on_device(): lax.all_gather(in_weight.reshape(256, 1536), 'ctx', axis=0, tiled=True)]
    dynamic_slice x0 -> x1, local copies, waits for them, and re-layouts: none -> 13.5 us  [on_device(): lax.dynamic_index_in_dim(cut, 1 - lax.rem(me, 2), 2, keepdims=False)]
    reshape x0 -> x3, local copies, waits for them, and re-layouts: none -> 10.6 us  [the longest x1 7.86 us: on_device(): cut = tokens.reshape(512, 8, 2, 256)]
    unnamed x31 -> x32, local copies, waits for them, and re-layouts: 6 us -> 11.6 us
  transfers between devices with their start and end apart: 5 -> 4, of which waited for: 5 -> 3; matrix products, arithmetic and copies ran while one was open for 6% -> 16% of each run, Pallas kernels for 0% -> 17%
where the time goes in v2:
time: 289 us
  Pallas kernels  127 us (44%)
  waiting for transfers between devices  83.7 us (29%)
  local copies, waits for them, and re-layouts  36 us (12%)
  between operations  14.3 us (5%)
  matrix products  11 us (4%)
  other arithmetic  10.4 us (4%)
  starting transfers between devices  6.1 us (2%)
    pallas_call x1, Pallas kernels, gradients(): pl.pallas_call(reduce_kernel, out_shape=(jax.ShapeDtypeStruct((64, 4096),...  78.1 us
    all_gather x1, waiting for transfers between devices, on_device(): lax.all_gather(in_weight.reshape(256, 1536), 'ctx', axis=0, tiled=True)  70.8 us
    pallas_call x2, Pallas kernels, exchange(): pl.pallas_call(functools.partial(exchange_kernel, pick, place), out_shape...  38.1 us
    dynamic_slice x1, local copies, waits for them, and re-layouts, on_device(): lax.dynamic_index_in_dim(cut, 1 - lax.rem(me, 2), 2, keepdims=False)  13.5 us
    ppermute x2, waiting for transfers between devices, shifted(): lax.ppermute(value, axis, [(source, source + steps) for source in range(f...  12.9 us
    unnamed x32, local copies, waits for them, and re-layouts  11.6 us
    dot_general x1, matrix products, on_device(): lax.dot_general(whole_weight, tokens, (((0,), (1,)), ((), ())), preferred...  11 us
    pallas_call x1, Pallas kernels, convolve(): pl.pallas_call(convolve_kernel, out_shape=(jax.ShapeDtypeStruct((32, BLOC...  10.8 us
  transfers between devices with their start and end apart: 4, of which 3 were waited for; matrix products, arithmetic and copies ran while one was open for 16% of the time, Pallas kernels for 17%

profile of v2, /device:TPU:1, one launch (start us, length us, event | category | flops | bytes accessed | tf_op | source)
XLA Modules:
  0.0 288.6 jit_solution(12300483224480969958)
XLA Ops:
  7.2 1.4 copy.19
  8.6 1.2 copy.20
  9.8 7.9 %reshape.32 = bf16[512,8,2,256]{3,2,1,0:T(2,128)(2,1)} reshape(bf16[512,4096]{1,0:T(8,128)(2,1)} %tokens.1) | data formatting | bytes 8388608 | tf_op jit(solution)/shard_map/reshape | solution.py:418
  17.7 13.5 %dynamic-slice_reduce_fusion = bf16[512,8,256]{2,1,0:T(8,128)(2,1)S(1)} fusion(bf16[512,8,2,256]{3,2,1,0:T(2,128)(2,1)} %reshape.32, s32[]{:T(128)S(6)} %select_n.4), kind=kLoop, calls=%fused_computation | loop fusion | bytes 4194308 | tf_op jit(solution)/shard_map/jit(dynamic_index_in_dim)/dynamic_slice | solution.py:419
  31.2 2.0 copy.25
  33.2 1.4 collective-permute-start.2
  34.6 70.8 %all-gather.2.cloned.1.call-done.weight = bf16[4096,1536]{1,0:T(8,128)(2,1)} async-done(((bf16[256,1536]{1,0:T(8,128)(2,1)}), bf16[4096,1536]{1,0:T(8,128)(2,1)}) %all-gather.2.cloned.1.call-update) | async-done | bytes 12582928 | tf_op jit(solution)/shard_map/all_gather | solution.py:421
  105.3 11.0 %convolution_convert_fusion = bf16[1536,512]{1,0:T(8,128)(2,1)S(1)} fusion(bf16[4096,1536]{1,0:T(8,128)(2,1)} %all-gather.2.cloned.1.call-done.weight, bf16[512,4096]{1,0:T(8,128)(2,1)} %tokens.1), kind=kOutput, calls=%fused_computation.13 | convolution fusion | flops 6443237376 | bytes 18350080 | tf_op jit(solution)/shard_map/dot_general | solution.py:422
  116.3 0.2 slice.70
  116.5 2.5 collective-permute-start
  119.1 4.5 %collective-permute-done = bf16[3,512,2]{2,1,0:T(8,128)(2,1)S(1)} collective-permute-done((bf16[3,512,2]{2,1,0:T(8,128)(2,1)S(1)}, bf16[3,512,2]{2,1,0:T(8,128)(2,1)S(1)}, u32[]{:S(2)}, u32[]{:S(2)}) %collective-permute-start) | collective-permute-done | bytes 6176 | tf_op jit(solution)/shard_map/ppermute | solution.py:24
  123.5 0.9 maximum_convert_fusion
  124.4 2.8 fusion.6
  127.4 1.5 copy-done.8
  128.9 0.2 fusion.10
  129.1 1.1 pad_maximum_fusion.src
  130.2 21.2 %shard_map.130.arrived = bf16[2,32,8192]{2,1,0:T(8,128)(2,1)} custom-call(bf16[2,512,512]{2,1,0:T(8,128)(2,1)} %pad_maximum_fusion.src), custom_call_target="tpu_custom_call" | custom-call | tf_op jit(solution)/shard_map/pallas_call | solution.py:64
  151.5 1.2 copy-done
  152.7 10.8 %shard_map.131 = (f32[32,8192]{1,0:T(8,128)}, bf16[2,32,8192]{2,1,0:T(8,128)(2,1)S(1)}) custom-call(bf16[2,32,8192]{2,1,0:T(8,128)(2,1)S(1)} %copy-done, f32[32,8192]{1,0:T(8,128)S(1)} %copy-done.1, f32[32,128]{1,0:T(8,128)S(1)} %broadcast_in_dim.2.bias, bf16[128,64]{1,0:T(8,128)(2,1)S(1)} %copy-done.6, bf16[256,256]{1,0:T(8,128)(2,1)S(1)} %copy-done.4, ...), custom_call_target="tpu_custom_call" | custom-call | tf_op jit(solution)/shard_map/pallas_call | solution.py:163
  163.6 1.0 copy-done.2
  164.6 16.9 %shard_map.132 = bf16[2,512,512]{2,1,0:T(8,128)(2,1)} custom-call(bf16[2,32,8192]{2,1,0:T(8,128)(2,1)} %copy-done.2), custom_call_target="tpu_custom_call" | custom-call | tf_op jit(solution)/shard_map/pallas_call | solution.py:64
  181.5 1.7 convert_element_type.31
  183.3 0.4 copy-done.9
  183.7 0.4 multiply_convert_fusion.1
  184.2 2.1 collective-permute-start.1
  186.4 8.5 %collective-permute-done.1 = bf16[3,512,2]{2,1,0:T(8,128)(2,1)S(1)} collective-permute-done((bf16[3,512,2]{2,1,0:T(8,128)(2,1)S(1)}, bf16[3,512,2]{2,1,0:T(8,128)(2,1)S(1)}, u32[]{:S(2)}, u32[]{:S(2)}) %collective-permute-start.1) | collective-permute-done | bytes 6176 | tf_op jit(solution)/shard_map/ppermute | solution.py:24
  194.8 0.3 maximum_convert_fusion.1
  195.1 2.8 fusion.1
  197.9 1.6 copy.21
  199.5 78.1 %shard_map.133 = (bf16[64,4096]{1,0:T(8,128)(2,1)}, bf16[1536,256]{1,0:T(8,128)(2,1)}) custom-call(bf16[1536,512]{1,0:T(8,128)(2,1)} %bitcast.35, bf16[512,1536]{1,0:T(8,128)(2,1)} %bitcast.39, bf16[512,4096]{1,0:T(8,128)(2,1)} %tokens.1, bf16[512,2048]{1,0:T(8,128)(2,1)} %collective-permute-done.2.others, bf16[4096,1536]{1,0:T(8,128)(2,1)} %all-gather.2.cloned.1.call-done.weight), custom_call_target="tpu_custom_call" | custom-call | flops 12884901888 | bytes 25165824 | tf_op jit(solution)/shard_map/pallas_call | solution.py:361
  277.6 2.3 copy.23
  279.9 1.9 copy.27
  (32 shorter events, 0.6 us)
Async XLA Ops:
  7.2 98.2 %all-gather.2.cloned.1.call-start = ((), (), s32[]{:S(2)}) async-start(), calls=%async_computation | async-start | bytes 13369344 | tf_op jit(solution)/shard_map/all_gather | solution.py:421
  33.2 85.9 %copy-start.12 = (f32[3,3,512]{2,1,0:T(4,128)S(1)}, f32[3,3,512]{2,1,0:T(4,128)}, u32[]{:S(2)}) copy-start(f32[3,3,512]{2,1,0:T(4,128)} %param.13) | copy-start | bytes 55300
  33.2 166.3 %collective-permute-start.2 = (bf16[512,2048]{1,0:T(8,128)(2,1)}, bf16[512,2048]{1,0:T(8,128)(2,1)}, u32[]{:S(2)}, u32[]{:S(2)}) collective-permute-start(bf16[512,2048]{1,0:T(8,128)(2,1)} %bitcast.15), channel_id=1, source_target_pairs={{0,8},{8,0},{16,24},{24,16},{32,40},{40,32},{48,56},{56,48},{64,72... | collective-permute-start | bytes 6291464 | tf_op jit(solution)/shard_map/ppermute | solution.py:420
  116.5 7.0 %collective-permute-start = (bf16[3,512,2]{2,1,0:T(8,128)(2,1)S(1)}, bf16[3,512,2]{2,1,0:T(8,128)(2,1)S(1)}, u32[]{:S(2)}, u32[]{:S(2)}) collective-permute-start(bf16[3,512,2]{2,1,0:T(8,128)(2,1)S(1)} %slice.70), channel_id=1, source_target_pairs={{0,8},{8,16},{16,24},{24,32},{32,40},{40,48},{48,56},{56,64},{64,7... | collective-permute-start | bytes 18440 | tf_op jit(solution)/shard_map/ppermute | solution.py:24
  124.4 4.4 %copy-start.11 = (bf16[512,512]{1,0:T(8,128)(2,1)S(1)}, bf16[512,512]{1,0:T(8,128)(2,1)}, u32[]{:S(2)}) copy-start(bf16[512,512]{1,0:T(8,128)(2,1)} %param.16) | copy-start | bytes 1572868
  127.2 1.6 copy-start.8
  128.8 22.6 %copy-start.13 = (f32[32]{0:T(128)S(1)}, f32[32]{0:T(128)}, u32[]{:S(2)}) copy-start(f32[32]{0:T(128)} %param.15) | copy-start | bytes 388
  128.8 22.6 %copy-start.1 = (f32[32,8192]{1,0:T(8,128)S(1)}, f32[32,8192]{1,0:T(8,128)}, u32[]{:S(2)}) copy-start(f32[32,8192]{1,0:T(8,128)} %filters.1) | copy-start | bytes 3145732
  128.8 22.6 %copy-start.3 = (bf16[256,256]{1,0:T(8,128)(2,1)S(1)}, bf16[256,256]{1,0:T(8,128)(2,1)}, u32[]{:S(2)}) copy-start(bf16[256,256]{1,0:T(8,128)(2,1)} %constant.31.clone.second_back) | copy-start | bytes 393220
  128.8 22.6 %copy-start.4 = (bf16[256,256]{1,0:T(8,128)(2,1)S(1)}, bf16[256,256]{1,0:T(8,128)(2,1)}, u32[]{:S(2)}) copy-start(bf16[256,256]{1,0:T(8,128)(2,1)} %constant.30.clone.second) | copy-start | bytes 393220
  128.9 22.6 %copy-start.5 = (f32[2,64,128]{2,1,0:T(8,128)S(1)}, f32[2,64,128]{2,1,0:T(8,128)}, u32[]{:S(2)}) copy-start(f32[2,64,128]{2,1,0:T(8,128)} %constant.28.clone.turn) | copy-start | bytes 196612
  128.9 22.6 %copy-start.6 = (bf16[128,64]{1,0:T(8,128)(2,1)S(1)}, bf16[128,64]{1,0:T(8,128)(2,1)}, u32[]{:S(2)}) copy-start(bf16[128,64]{1,0:T(8,128)(2,1)} %constant.29.clone.first) | copy-start | bytes 49156
  128.9 22.6 %copy-start.7 = (bf16[64,128]{1,0:T(8,128)(2,1)S(1)}, bf16[64,128]{1,0:T(8,128)(2,1)}, u32[]{:S(2)}) copy-start(bf16[64,128]{1,0:T(8,128)(2,1)} %constant.32.clone.first_back) | copy-start | bytes 49156
  151.5 1.2 copy-start
  163.6 1.0 copy-start.2
  181.5 2.2 copy-start.9
  184.2 10.6 %collective-permute-start.1 = (bf16[3,512,2]{2,1,0:T(8,128)(2,1)S(1)}, bf16[3,512,2]{2,1,0:T(8,128)(2,1)S(1)}, u32[]{:S(2)}, u32[]{:S(2)}) collective-permute-start(bf16[3,512,2]{2,1,0:T(8,128)(2,1)S(1)} %pad_maximum_fusion.1), channel_id=1, source_target_pairs={{8,0},{16,8},{24,16},{32,24},{40,32},{48,40},{56,48},{64,56},{72,6... | collective-permute-start | bytes 18440 | tf_op jit(solution)/shard_map/ppermute | solution.py:24
  197.8 1.6 copy-start.10
Sparse Core Ops, SparseCore 0:
  11.0 94.2 all-gather.1

commit v3 on v2

--- a/solution.py
+++ b/solution.py
@@ -394,6 +394,180 @@
     )(pgc, pgt, tokens, others, weight)
 
 
+def project_kernel(tokens, weight, projected, whole, others, tok, wall, acc, send, recv, load):
+    f32, bf16 = jnp.float32, jnp.bfloat16
+    at = places()
+    core, xh, y = at["core"], at["xh"], at["y"]
+    me = lax.axis_index("ctx")
+    at["across"] = {"ctx": (y * 2 + 1 - xh) * 2 + core}
+    at["next"] = {"ctx": lax.rem(me + 1, N_CTX)}
+    at["last"] = {"ctx": lax.rem(me + N_CTX - 1, N_CTX)}
+    loads = [
+        pltpu.make_async_copy(weight, wall.at[me], load.at[0]),
+        pltpu.make_async_copy(tokens, tok.at[pl.ds(16, 512)], load.at[1]),
+    ]
+    for one in loads:
+        one.start()
+    greet([at[name] for name in ("twin", "up", "down", "across", "next", "last")])
+    sent = {}
+
+    def start(name, src, dst, peer):
+        index = len(sent)
+        copy = pltpu.make_async_remote_copy(
+            src_ref=src,
+            dst_ref=dst,
+            send_sem=send.at[index],
+            recv_sem=recv.at[index],
+            device_id=at[peer],
+            device_id_type=MESH,
+        )
+        copy.start()
+        sent[name] = copy
+
+    def arrived(*names):
+        for name in names:
+            sent[name].wait_recv()
+
+    halves = (pl.ds(0, 128), pl.ds(128, 128))
+
+    def half_of(index, half):
+        return wall.at[index, halves[half]]
+
+    def pass_on(name, index, half, peer):
+        start(name, half_of(index, half), half_of(index, half), peer)
+
+    def hand_over(name, index):
+        start(name, wall.at[index], wall.at[index], "twin")
+
+    stored = []
+
+    def multiply(index, fresh=False):
+        pair = index // 2
+        columns = pl.ds(pl.multiple_of(pair * 512, 512), 512)
+        store = pltpu.make_async_copy(
+            wall.at[pl.ds(pair * 2, 2)], whole.at[pl.ds(pair * 2, 2)], load.at[2 + len(stored)]
+        )
+        store.start()
+        stored.append(store)
+
+        def tile(step, carry):
+            place = pl.ds(pl.multiple_of(step * 512, 512), 512)
+            value = jnp.dot(
+                tok[:, columns],
+                wall[pl.ds(pair * 2, 2), :, place].reshape(512, 512),
+                preferred_element_type=f32,
+            )
+            acc[:, place] = value if fresh else acc[:, place] + value
+            return carry
+
+        lax.fori_loop(0, 3, tile, 0)
+
+    def ctx_of(y, xh):
+        return (lax.rem(y, 4) * 2 + xh) * 2 + core
+
+    below, above, beyond = ctx_of(y + 3, xh), ctx_of(y + 1, xh), ctx_of(y + 2, xh)
+    side = ctx_of(y, 1 - xh)
+    side_below, side_above = ctx_of(y + 3, 1 - xh), ctx_of(y + 1, 1 - xh)
+    side_beyond = ctx_of(y + 2, 1 - xh)
+
+    start("up0", weight.at[halves[0]], half_of(me, 0), "up")
+    start("down1", weight.at[halves[1]], half_of(me, 1), "down")
+    start("across", weight, wall.at[me], "across")
+    start("twin", weight, wall.at[me], "twin")
+    start("halo", tokens.at[pl.ds(496, 16)], tok.at[pl.ds(0, 16)], "next")
+    for j in range(8):
+        columns = pl.ds(pl.multiple_of((2 * j + 1 - core) * 256, 256), 256)
+        start(("swap", j), tokens.at[:, columns], others.at[:, pl.ds(j * 256, 256)], "twin")
+    arrived("up0")
+    pass_on("on0", below, 0, "up")
+    arrived("down1")
+    pass_on("on1", above, 1, "down")
+    start("up1", weight.at[halves[1]], half_of(me, 1), "up")
+    start("down0", weight.at[halves[0]], half_of(me, 0), "down")
+    for one in loads:
+        one.wait()
+    arrived("halo", "twin")
+    multiply(me, fresh=True)
+    arrived("across")
+    pass_on("side_up0", side, 0, "up")
+    pass_on("side_down1", side, 1, "down")
+    hand_over("twin_side", side)
+    arrived("on0", "on1")
+    start("across_beyond", wall.at[beyond], wall.at[beyond], "across")
+    hand_over("twin_beyond", beyond)
+    pass_on("side_up1", side, 1, "up")
+    pass_on("side_down0", side, 0, "down")
+    arrived("twin_side")
+    multiply(side)
+    arrived("up1")
+    hand_over("twin_below", below)
+    arrived("down0")
+    hand_over("twin_above", above)
+    arrived("twin_beyond")
+    multiply(beyond)
+    arrived("twin_below")
+    multiply(below)
+    arrived("twin_above")
+    multiply(above)
+    arrived("side_up0")
+    pass_on("twin_sb0", side_below, 0, "twin")
+    arrived("side_down1")
+    pass_on("twin_sa1", side_above, 1, "twin")
+    arrived("across_beyond")
+    hand_over("twin_across", side_beyond)
+    arrived("twin_across")
+    multiply(side_beyond)
+    arrived("side_up1")
+    pass_on("twin_sb1", side_below, 1, "twin")
+    arrived("side_down0")
+    pass_on("twin_sa0", side_above, 0, "twin")
+    arrived("twin_sb0", "twin_sb1")
+    multiply(side_below)
+    arrived("twin_sa0", "twin_sa1")
+    multiply(side_above)
+
+    def finish(step, carry):
+        rows = pl.ds(pl.multiple_of(step * 48, 16), 48)
+        projected[rows, :] = acc[rows, :].astype(bf16)
+        return carry
+
+    lax.fori_loop(0, 11, finish, 0)
+    for j in range(8):
+        arrived(("swap", j))
+    for store in stored:
+        store.wait()
+    for copy in sent.values():
+        copy.wait_send()
+
+
+def project(tokens, weight):
+    bf16 = jnp.bfloat16
+    return pl.pallas_call(
+        project_kernel,
+        out_shape=(
+            jax.ShapeDtypeStruct((528, 1536), bf16),
+            jax.ShapeDtypeStruct((N_CTX, 256, 1536), bf16),
+            jax.ShapeDtypeStruct((512, 2048), bf16),
+        ),
+        in_specs=[ANY, ANY],
+        out_specs=(IN_VMEM, ANY, ANY),
+        scratch_shapes=[
+            pltpu.VMEM((528, 4096), bf16),
+            pltpu.VMEM((N_CTX, 256, 1536), bf16),
+            pltpu.VMEM((528, 1536), jnp.float32),
+            pltpu.SemaphoreType.DMA((34,)),
+            pltpu.SemaphoreType.DMA((34,)),
+            pltpu.SemaphoreType.DMA((10,)),
+        ],
+        compiler_params=pltpu.CompilerParams(
+            collective_id=4, has_side_effects=True, vmem_limit_bytes=48 * 1024 * 1024
+        ),
+        cost_estimate=pl.CostEstimate(
+            flops=2 * 512 * 4096 * 1536, bytes_accessed=24 * 1024 * 1024, transcendentals=0
+        ),
+    )(tokens, weight)
+
+
 def short_forward(values, before, taps):
     extended = jnp.concatenate([before, values], axis=2).astype(jnp.float32)
     return (
@@ -414,16 +588,11 @@
 
 def on_device(tokens, in_weight, short_taps, long_filter, skip_bias, out_grad):
     f32, bf16 = jnp.float32, jnp.bfloat16
-    me = lax.axis_index("ctx")
-    cut = tokens.reshape(512, 8, 2, 256)
-    theirs = lax.dynamic_index_in_dim(cut, 1 - lax.rem(me, 2), 2, keepdims=False).reshape(512, 2048)
-    others = lax.ppermute(theirs, "ctx", [(index, index ^ 1) for index in range(N_CTX)])
-    whole_weight = lax.all_gather(in_weight.reshape(256, 1536), "ctx", axis=0, tiled=True)
-    projected = lax.dot_general(
-        whole_weight, tokens, (((0,), (1,)), ((), ())), preferred_element_type=f32
-    )
-    projected = projected.astype(bf16).reshape(3, 512, 512)
-    before = shifted(projected[:, :, -2:], "ctx", 1)
+    projected, whole_weight, others = project(tokens, in_weight.reshape(256, 1536))
+    whole_weight = whole_weight.reshape(4096, 1536)
+    projected = projected.T.reshape(3, 512, 528)
+    before = jnp.where(lax.axis_index("ctx") == 0, jnp.zeros((), bf16), projected[:, :, 14:16])
+    projected = projected[:, :, 16:]
     streams = short_forward(projected, before, short_taps).astype(f32)
     cotangent = out_grad.astype(f32)
     outgoing = jnp.stack([streams[1] * streams[2], cotangent * streams[0]]).astype(bf16)

time: 289 us -> 224 us (0.78)
  waiting for transfers between devices: 83.7 us -> 8.49 us
  Pallas kernels: 127 us -> 183 us
  local copies, waits for them, and re-layouts: 36 us -> 17.9 us
  between operations: 14.3 us -> 0.9 us
  matrix products: 11 us -> 0 us
  starting transfers between devices: 6.1 us -> 2.1 us
    all_gather x1 -> x0, waiting for transfers between devices: 70.8 us -> none  [on_device(): lax.all_gather(in_weight.reshape(256, 1536), 'ctx', axis=0, tiled=True)]
    pallas_call x0 -> x1, Pallas kernels: none -> 58.4 us  [project(): pl.pallas_call(project_kernel, out_shape=(jax.ShapeDtypeStruct((528, 1536...]
    dynamic_slice x1 -> x0, local copies, waits for them, and re-layouts: 13.5 us -> none  [on_device(): lax.dynamic_index_in_dim(cut, 1 - lax.rem(me, 2), 2, keepdims=False)]
    dot_general x1 -> x0, matrix products: 11 us -> none  [on_device(): lax.dot_general(whole_weight, tokens, (((0,), (1,)), ((), ())), preferred...]
    reshape x1 -> x0, local copies, waits for them, and re-layouts: 7.86 us -> none  [on_device(): cut = tokens.reshape(512, 8, 2, 256)]
    ppermute x2 -> x1, waiting for transfers between devices: 12.9 us -> 8.49 us  [shifted(): lax.ppermute(value, axis, [(source, source + steps) for source in range(f...]
    pallas_call x2, Pallas kernels: 38.1 us -> 34.7 us  [exchange(): pl.pallas_call(functools.partial(exchange_kernel, pick, place), out_shape...]
    unnamed x32 -> x33, local copies, waits for them, and re-layouts: 11.6 us -> 10.6 us
  transfers between devices with their start and end apart: 4 -> 1, of which waited for: 3 -> 1; matrix products, arithmetic and copies ran while one was open for 16% -> 0% of each run, Pallas kernels for 17% -> 0%
where the time goes in v3:
time: 224 us; the launch traced here: 223 us
  Pallas kernels  183 us (82%)
  local copies, waits for them, and re-layouts  17.9 us (8%)
  other arithmetic  11.4 us (5%)
  waiting for transfers between devices  8.49 us (4%)
    pallas_call x1, Pallas kernels, gradients(): pl.pallas_call(reduce_kernel, out_shape=(jax.ShapeDtypeStruct((64, 4096),...  78.8 us
    pallas_call x1, Pallas kernels, project(): pl.pallas_call(project_kernel, out_shape=(jax.ShapeDtypeStruct((528, 1536...  58.4 us
    pallas_call x2, Pallas kernels, exchange(): pl.pallas_call(functools.partial(exchange_kernel, pick, place), out_shape...  34.7 us
    pallas_call x1, Pallas kernels, convolve(): pl.pallas_call(convolve_kernel, out_shape=(jax.ShapeDtypeStruct((32, BLOC...  10.8 us
    unnamed x33, local copies, waits for them, and re-layouts  10.6 us
    ppermute x1, waiting for transfers between devices, shifted(): lax.ppermute(value, axis, [(source, source + steps) for source in range(f...  8.49 us
  transfers between devices with their start and end apart: 1, of which 1 were waited for; matrix products, arithmetic and copies ran while one was open for 0% of the time, Pallas kernels for 0%

profile of v3, /device:TPU:1, one launch (start us, length us, event | category | flops | bytes accessed | tf_op | source)
XLA Modules:
  0.0 223.4 jit_solution(14779128716326535906)
XLA Ops:
  0.6 0.7 slice_bitcast_fusion.4
  1.4 1.4 copy.19
  2.8 0.3 copy.20.weight
  3.1 58.4 %shard_map.130 = (bf16[528,1536]{1,0:T(8,128)(2,1)S(1)}, bf16[16,256,1536]{2,1,0:T(8,128)(2,1)}, bf16[512,2048]{1,0:T(8,128)(2,1)S(1)}) custom-call(bf16[512,4096]{1,0:T(8,128)(2,1)} %tokens.3, bf16[256,1536]{1,0:T(8,128)(2,1)S(1)} %copy.20.weight), custom_call_target="tpu_custom_call" | custom-call | flops 6442450944 | bytes 25165824 | tf_op jit(solution)/shard_map/pallas_call | solution.py:545
  61.5 1.3 copy-done.8
  62.8 2.3 %copy.21 = bf16[1536,528]{1,0:T(8,128)(2,1)} copy(bf16[1536,528]{0,1:T(8,128)(2,1)S(1)} %bitcast.31) | data formatting | bytes 3244032 | tf_op jit(solution)/shard_map/transpose | solution.py:593
  65.1 2.3 %slice.75 = bf16[3,512,512]{2,1,0:T(8,128)(2,1)S(1)} slice(bf16[3,512,528]{2,1,0:T(8,128)(2,1)} %bitcast.32), slice={[0:3], [0:512], [16:528]} | slice | bytes 3145728 | tf_op jit(solution)/shard_map/slice | solution.py:595
  67.4 1.2 slice_select_fusion
  68.6 0.9 maximum_convert_fusion
  69.4 2.8 %fusion.6 = f32[3,512,512]{2,1,0:T(8,128)S(1)} fusion(f32[3,512,514]{2,1,0:T(8,128)S(1)} %maximum_convert_fusion, f32[3,512]{1,0:T(4,128)S(1)} %get-tuple-element.26, f32[3,512]{1,0:T(4,128)S(1)} %get-tuple-element.27, f32[3,512]{1,0:T(4,128)S(1)} %get-tuple-element.25), kind=kLoop, calls=%fused_computation.14 | loop fusion | flops 5505024 | bytes 12601344 | tf_op jit(solution)/shard_map/convert_element_type | solution.py:596
  72.2 0.2 multiply_convert_fusion.2
  72.4 1.5 copy-done.9
  73.9 0.2 fusion.10
  74.1 1.1 pad_maximum_fusion.src
  75.1 16.6 %shard_map.131.arrived = bf16[2,32,8192]{2,1,0:T(8,128)(2,1)} custom-call(bf16[2,512,512]{2,1,0:T(8,128)(2,1)} %pad_maximum_fusion.src), custom_call_target="tpu_custom_call" | custom-call | tf_op jit(solution)/shard_map/pallas_call | solution.py:64
  91.7 0.1 broadcast_in_dim.11.bias
  91.8 1.2 copy-done
  93.0 10.8 %shard_map.132 = (f32[32,8192]{1,0:T(8,128)}, bf16[2,32,8192]{2,1,0:T(8,128)(2,1)S(1)}) custom-call(bf16[2,32,8192]{2,1,0:T(8,128)(2,1)S(1)} %copy-done, f32[32,8192]{1,0:T(8,128)S(1)} %copy-done.1, f32[32,128]{1,0:T(8,128)S(1)} %broadcast_in_dim.11.bias, bf16[128,64]{1,0:T(8,128)(2,1)S(1)} %copy-done.6, bf16[256,256]{1,0:T(8,128)(2,1)S(1)} %copy-done.4, ...), custom_call_target="tpu_custom_call" | custom-call | tf_op jit(solution)/shard_map/pallas_call | solution.py:163
  103.8 1.0 copy-done.2
  104.8 18.1 %shard_map.133 = bf16[2,512,512]{2,1,0:T(8,128)(2,1)} custom-call(bf16[2,32,8192]{2,1,0:T(8,128)(2,1)} %copy-done.2), custom_call_target="tpu_custom_call" | custom-call | tf_op jit(solution)/shard_map/pallas_call | solution.py:64
  123.0 1.6 convert_element_type.27
  124.5 0.4 multiply_convert_fusion.1
  125.0 0.2 fusion.9
  125.1 0.1 pad_maximum_fusion.1
  125.2 2.1 collective-permute-start
  127.3 8.5 %collective-permute-done = bf16[3,512,2]{2,1,0:T(8,128)(2,1)S(1)} collective-permute-done((bf16[3,512,2]{2,1,0:T(8,128)(2,1)S(1)}, bf16[3,512,2]{2,1,0:T(8,128)(2,1)S(1)}, u32[]{:S(2)}, u32[]{:S(2)}) %collective-permute-start) | collective-permute-done | bytes 6176 | tf_op jit(solution)/shard_map/ppermute | solution.py:24
  135.8 0.3 maximum_convert_fusion.1
  136.1 2.8 %fusion.1 = bf16[3,512,512]{2,1,0:T(8,128)(2,1)S(1)} fusion(f32[3,512,514]{2,1,0:T(8,128)S(1)} %maximum_convert_fusion.1, f32[3,512]{1,0:T(4,128)S(1)} %get-tuple-element.26, f32[3,512]{1,0:T(4,128)S(1)} %get-tuple-element.27, f32[3,512]{1,0:T(4,128)S(1)} %get-tuple-element.25), kind=kLoop, calls=%fused_computation.2 | loop fusion | flops 4718592 | bytes 11028480 | tf_op jit(solution)/shard_map/convert_element_type | solution.py:586
  138.9 1.6 copy.22
  140.5 78.8 %shard_map.134 = (bf16[64,4096]{1,0:T(8,128)(2,1)}, bf16[1536,256]{1,0:T(8,128)(2,1)}) custom-call(bf16[1536,512]{1,0:T(8,128)(2,1)} %bitcast.35, bf16[512,1536]{1,0:T(8,128)(2,1)} %bitcast.37, bf16[512,4096]{1,0:T(8,128)(2,1)} %tokens.3, bf16[512,2048]{1,0:T(8,128)(2,1)} %copy-done.8, bf16[4096,1536]{1,0:T(8,128)(2,1)} %bitcast.39), custom_call_target="tpu_custom_call" | custom-call | flops 12884901888 | bytes 25165824 | tf_op jit(solution)/shard_map/pallas_call | solution.py:361
  219.3 2.3 %copy.23 = bf16[256,3,512]{2,0,1:T(8,128)(2,1)} copy(bf16[256,3,512]{0,2,1:T(8,128)(2,1)} %bitcast.38) | data formatting | bytes 1572864
  221.6 1.9 copy.25
  (26 shorter events, 0.1 us)
Async XLA Ops:
  61.5 1.3 copy-start.8
  69.4 4.4 %copy-start.12 = (bf16[512,512]{1,0:T(8,128)(2,1)S(1)}, bf16[512,512]{1,0:T(8,128)(2,1)}, u32[]{:S(2)}) copy-start(bf16[512,512]{1,0:T(8,128)(2,1)} %param.16) | copy-start | bytes 1572868
  72.2 1.6 copy-start.9
  73.8 17.9 %copy-start.14 = (f32[32]{0:T(128)S(1)}, f32[32]{0:T(128)}, u32[]{:S(2)}) copy-start(f32[32]{0:T(128)} %param.15) | copy-start | bytes 388
  73.9 17.9 %copy-start.1 = (f32[32,8192]{1,0:T(8,128)S(1)}, f32[32,8192]{1,0:T(8,128)}, u32[]{:S(2)}) copy-start(f32[32,8192]{1,0:T(8,128)} %filters.1) | copy-start | bytes 3145732
  73.9 17.9 %copy-start.3 = (bf16[256,256]{1,0:T(8,128)(2,1)S(1)}, bf16[256,256]{1,0:T(8,128)(2,1)}, u32[]{:S(2)}) copy-start(bf16[256,256]{1,0:T(8,128)(2,1)} %constant.23.clone.second_back) | copy-start | bytes 393220
  73.9 17.9 %copy-start.4 = (bf16[256,256]{1,0:T(8,128)(2,1)S(1)}, bf16[256,256]{1,0:T(8,128)(2,1)}, u32[]{:S(2)}) copy-start(bf16[256,256]{1,0:T(8,128)(2,1)} %constant.22.clone.second) | copy-start | bytes 393220
  73.9 17.9 %copy-start.5 = (f32[2,64,128]{2,1,0:T(8,128)S(1)}, f32[2,64,128]{2,1,0:T(8,128)}, u32[]{:S(2)}) copy-start(f32[2,64,128]{2,1,0:T(8,128)} %constant.20.clone.turn) | copy-start | bytes 196612
  73.9 17.9 %copy-start.6 = (bf16[128,64]{1,0:T(8,128)(2,1)S(1)}, bf16[128,64]{1,0:T(8,128)(2,1)}, u32[]{:S(2)}) copy-start(bf16[128,64]{1,0:T(8,128)(2,1)} %constant.21.clone.first) | copy-start | bytes 49156
  73.9 17.9 %copy-start.7 = (bf16[64,128]{1,0:T(8,128)(2,1)S(1)}, bf16[64,128]{1,0:T(8,128)(2,1)}, u32[]{:S(2)}) copy-start(bf16[64,128]{1,0:T(8,128)(2,1)} %constant.24.clone.first_back) | copy-start | bytes 49156
  91.8 1.2 copy-start
  103.8 1.0 copy-start.2
  104.8 19.7 %copy-start.10 = (f32[3,512,512]{2,1,0:T(8,128)S(1)}, f32[3,512,512]{2,1,0:T(8,128)}, u32[]{:S(2)}) copy-start(f32[3,512,512]{2,1,0:T(8,128)} %copy-done.9) | copy-start | bytes 9437188
  122.9 2.0 copy-start.13
  125.2 10.6 %collective-permute-start = (bf16[3,512,2]{2,1,0:T(8,128)(2,1)S(1)}, bf16[3,512,2]{2,1,0:T(8,128)(2,1)S(1)}, u32[]{:S(2)}, u32[]{:S(2)}) collective-permute-start(bf16[3,512,2]{2,1,0:T(8,128)(2,1)S(1)} %pad_maximum_fusion.1), channel_id=1, source_target_pairs={{8,0},{16,8},{24,16},{32,24},{40,32},{48,40},{56,48},{64,56},{72,6... | collective-permute-start | bytes 18440 | tf_op jit(solution)/shard_map/ppermute | solution.py:24
  138.8 1.6 copy-start.11

commit v4 on v3

--- a/solution.py
+++ b/solution.py
@@ -16,12 +16,6 @@
 LANES = 128
 BLOCKS = 64
 GROUP = 4
-
-
-def shifted(value, axis, steps):
-    count = lax.axis_size(axis)
-    first, last = (max(0, -steps), min(count, count - steps))
-    return lax.ppermute(value, axis, [(source, source + steps) for source in range(first, last)])
 
 
 def exchange_kernel(pick, place, src, out, send_sem, recv_sem, local_sem):
@@ -201,22 +195,26 @@
     pl.semaphore_wait(barrier, len(peers))
 
 
-def reduce_kernel(
-    pgc, pgt, tokens, others, weight, ig_out, wg_out,
-    tok, oth, wei, pgo, ig, acc, part, r2, rf, relay, xr, z2, zf, xz, send, recv, load,
+def tail_kernel(
+    result, cotangent, keys, values, taps, tokens, others, weight, ig_out, wg_out,
+    tok, oth, wei, ret, cgx, hout, hin, pgc, pgt, pgo, ig, acc, part, xin, r2, rf, xr, z2, zf, xz,
+    send, recv, load,
 ):
     f32, bf16 = jnp.float32, jnp.bfloat16
     at = places()
     core, xh, y, z, xl = at["core"], at["xh"], at["y"], at["z"], at["xl"]
+    me = lax.axis_index("ctx")
+    at["across"] = {"ctx": (y * 2 + 1 - xh) * 2 + core}
+    for step in range(1, N_CTX):
+        at[step] = {"ctx": lax.rem(me + step, N_CTX)}
     loads = [
         pltpu.make_async_copy(weight.at[pl.ds(0, 2048)], wei.at[pl.ds(0, 2048)], load.at[0]),
         pltpu.make_async_copy(tokens, tok, load.at[1]),
         pltpu.make_async_copy(others, oth, load.at[2]),
         pltpu.make_async_copy(weight.at[pl.ds(2048, 2048)], wei.at[pl.ds(2048, 2048)], load.at[3]),
+        pltpu.make_async_copy(positions_of(result, me), rows_of(ret, me), load.at[4]),
     ]
-    for one in loads:
-        one.start()
-    greet([at[name] for name in ("twin", "up", "down", "near", "far", "above", "below")])
+    greet([at[name] for name in (*range(1, N_CTX), "near", "above", "below")])
     sent = {}
 
     def start(name, src, dst, peer):
@@ -232,36 +230,95 @@
         copy.start()
         sent[name] = copy
 
-    def arrived(name):
-        sent[name].wait_recv()
+    def arrived(*names):
+        for name in names:
+            sent[name].wait_recv()
+
+    for step in range(1, N_CTX):
+        peer = lax.rem(me + step, N_CTX)
+        start(step, positions_of(result, peer), rows_of(ret, me), step)
+    for one in loads:
+        one.start()
+    loads[4].wait()
+    arrived(*range(1, N_CTX))
+
+    def lanes(p, chunk):
+        return pl.ds(pl.multiple_of(p * 512 + chunk * 128, 128), 128)
+
+    def stream_grads(chunk, carry):
+        rows = pl.ds(pl.multiple_of(chunk * 128, 128), 128)
+        one, two = ret[0, rows, :].astype(f32), ret[1, rows, :].astype(f32)
+        factors = ((one, cotangent), (two, values), (two, keys))
+        for p, (value, factor) in enumerate(factors):
+            grad = (value * factor[rows, :].astype(f32)).astype(bf16)
+            cgx[p, rows, 0:512] = grad
+            hout[:, lanes(p, chunk)] = grad[:, 0:128].T[0:16, :]
+        return carry
+
+    lax.fori_loop(0, 4, stream_grads, 0)
+    start("halo", hout, hin, N_CTX - 1)
+
+    def tapped(p, rows, first, width, kept):
+        x = cgx[p, rows, first : first + width].astype(f32)
+        total = taps[rows, p : p + 1] * x
+        for j in (1, 2):
+            total = total + taps[rows, 3 * j + p : 3 * j + p + 1] * pltpu.roll(x, width - j, 1)
+        return total[:, :kept].astype(bf16)
+
+    def front(chunk, carry):
+        rows = pl.ds(pl.multiple_of(chunk * 128, 128), 128)
+        for p in range(3):
+            grad = tapped(p, rows, 0, 512, 384)
+            pgc[lanes(p, chunk), 0:384] = grad
+            pgt[0:384, lanes(p, chunk)] = grad.T
+        return carry
+
+    lax.fori_loop(0, 4, front, 0)
+    start("twin0", pgc.at[:, pl.ds(0, 384)], pgo.at[:, pl.ds(0, 384)], "twin")
+    arrived("halo")
+
+    def rest(chunk, carry):
+        rows = pl.ds(pl.multiple_of(chunk * 128, 128), 128)
+        for p in range(3):
+            first = hin[:, lanes(p, chunk)].astype(f32)
+            first = jnp.where(me == N_CTX - 1, jnp.zeros_like(first), first)
+            first = jnp.concatenate([first, jnp.zeros((112, 128), f32)], axis=0)
+            cgx[p, rows, 512:640] = first.T.astype(bf16)
+            grad = tapped(p, rows, 384, 256, 128)
+            pgc[lanes(p, chunk), 384:512] = grad
+            pgt[384:512, lanes(p, chunk)] = grad.T
+        return carry
+
+    lax.fori_loop(0, 4, rest, 0)
+    start("twin1", pgc.at[:, pl.ds(384, 128)], pgo.at[:, pl.ds(384, 128)], "twin")
 
     def input_tiles(first):
         def tile(step, carry):
-            rows = pl.ds(pl.multiple_of((first + step) * 256, 256), 256)
+            rows = pl.ds(pl.multiple_of((first + step) * 512, 512), 512)
             ig[:, rows] = lax.dot_general(
                 pgt[...], wei[rows, :], (((1,), (1,)), ((), ())), preferred_element_type=f32
             ).astype(bf16)
             return carry
 
-        lax.fori_loop(0, 8, tile, 0)
-
-    def weight_part(block):
+        lax.fori_loop(0, 4, tile, 0)
+
+    def weight_part(slot, block):
         mine = pl.ds(pl.multiple_of((2 * block + core) * 256, 256), 256)
         theirs = pl.ds(pl.multiple_of(block * 256, 256), 256)
 
         def half(step, carry):
             rows = pl.ds(pl.multiple_of(step * 768, 256), 768)
-            acc[rows, :] = jnp.dot(pgc[rows, :], tok[:, mine], preferred_element_type=f32) + jnp.dot(
-                pgo[rows, :], oth[:, theirs], preferred_element_type=f32
-            )
+            acc[slot, rows, :] = jnp.dot(
+                pgc[rows, :], tok[:, mine], preferred_element_type=f32
+            ) + jnp.dot(pgo[rows, :], oth[:, theirs], preferred_element_type=f32)
             return carry
 
         lax.fori_loop(0, 2, half, 0)
 
-    def fold(dst, first, last, *terms):
+    def fold(dst, slot, first, last, *terms):
         def chunk(step, carry):
             rows = pl.ds(pl.multiple_of(step * 128, 128), 128)
-            total = acc[rows, :]
+            total = acc[slot, rows, :]
             for term, offset in terms:
                 part_rows = pl.ds(pl.multiple_of(step * 128 - offset, 128), 128)
                 total = total + term[part_rows, :].astype(f32)
@@ -274,124 +331,147 @@
         return y * 2 + xh
 
     y2, yp, ym = lax.rem(y + 2, 4), lax.rem(y + 1, 4), lax.rem(y + 3, 4)
-    z2i, zp, zm = lax.rem(z + 2, 4), lax.rem(z + 1, 4), lax.rem(z + 3, 4)
-    columns = (1 - xh, xh)
+    ztwo, zp, zm = lax.rem(z + 2, 4), lax.rem(z + 1, 4), lax.rem(z + 3, 4)
+    xo = 1 - xh
     sides = (1 - xl, xl)
     low, high = pl.ds(0, 768), pl.ds(768, 768)
-
-    start("twin", pgc, pgo, "twin")
+    parts = (slice(0, 2048), slice(2048, 4096))
+
+    def ig_rows(side, z, first, count):
+        return pl.ds(pl.multiple_of((side * 4 + z) * 64 + first, 32), count)
+
+    def ig_add(rows, h, *terms):
+        total = ig[rows, parts[h]].astype(f32)
+        for term in terms:
+            total = total + term[...].astype(f32)
+        return total.astype(bf16)
+
+    def z_first(h):
+        for k in range(2):
+            src = ig.at[ig_rows(sides[k], ztwo, 0, 32), parts[h]]
+            start(("z2p", h, k), src, z2.at[h, k, 0], "above")
+            src = ig.at[ig_rows(sides[k], ztwo, 32, 32), parts[h]]
+            start(("z2m", h, k), src, z2.at[h, k, 1], "below")
+
+    def z_second(h):
+        for k in range(2):
+            arrived(("z2p", h, k))
+            rows = ig_rows(sides[k], zp, 0, 32)
+            ig[rows, parts[h]] = ig_add(rows, h, z2.at[h, k, 0])
+            src = ig.at[ig_rows(sides[k], zp, 0, 64), parts[h]]
+            start(("zfp", h, k), src, zf.at[h, k, 0], "above")
+            arrived(("z2m", h, k))
+            rows = ig_rows(sides[k], zm, 32, 32)
+            ig[rows, parts[h]] = ig_add(rows, h, z2.at[h, k, 1])
+            src = ig.at[ig_rows(sides[k], zm, 0, 64), parts[h]]
+            start(("zfm", h, k), src, zf.at[h, k, 1], "below")
+
+    def z_across(h):
+        arrived(("zfp", h, 0), ("zfm", h, 0))
+        rows = ig_rows(sides[0], z, 0, 64)
+        ig[rows, parts[h]] = ig_add(rows, h, zf.at[h, 0, 0], zf.at[h, 0, 1])
+        start(("xz", h), ig.at[rows, parts[h]], xz.at[h], "near")
+
+    def z_last(h):
+        arrived(("zfp", h, 1), ("zfm", h, 1), ("xz", h))
+        rows = ig_rows(sides[1], z, 0, 64)
+        ig_out[:, parts[h]] = ig_add(rows, h, zf.at[h, 1, 0], zf.at[h, 1, 1], xz.at[h])
+
     loads[0].wait()
     input_tiles(0)
+    z_first(0)
     loads[1].wait()
     loads[2].wait()
-    arrived("twin")
-    for k in range(2):
-        weight_part(block_of(y2, columns[k]))
-        fold(part.at[k], 0, 1536)
-        start(("2p", k), part.at[k, low], r2.at[k, 0], "up")
-        start(("2m", k), part.at[k, high], r2.at[k, 1], "down")
+    arrived("twin0", "twin1")
+    weight_part(0, block_of(y2, xo))
+    fold(part.at[0], 0, 0, 1536)
+    start("across0", part.at[0], xin, "across")
+    weight_part(0, block_of(yp, xo))
+    fold(part.at[1], 0, 0, 1536)
+    start("up0", part.at[1], rf.at[0, 0], "up")
+    weight_part(0, block_of(ym, xo))
+    fold(part.at[2], 0, 0, 1536)
+    start("down0", part.at[2], rf.at[0, 1], "down")
     loads[3].wait()
-    input_tiles(8)
-
-    def ig_rows(side, z, first, count):
-        return pl.ds(pl.multiple_of((side * 4 + z) * 64 + first, 32), count)
-
-    for k in range(2):
-        start(("z2p", k), ig.at[ig_rows(sides[k], z2i, 0, 32)], z2.at[k, 0], "above")
-        start(("z2m", k), ig.at[ig_rows(sides[k], z2i, 32, 32)], z2.at[k, 1], "below")
-
-    def ig_add(rows, *terms):
-        total = ig[rows, :].astype(f32)
-        for term in terms:
-            total = total + term[...].astype(f32)
-        return total
-
-    for k in range(2):
-        weight_part(block_of(yp, columns[k]))
-        arrived(("2p", k))
-        fold(part.at[2 + 2 * k], 0, 768, (r2.at[k, 0], 0))
-        fold(part.at[2 + 2 * k], 768, 1536)
-        start(("fp", k), part.at[2 + 2 * k], rf.at[k, 0], "up")
-        weight_part(block_of(ym, columns[k]))
-        arrived(("2m", k))
-        fold(part.at[3 + 2 * k], 0, 768)
-        fold(part.at[3 + 2 * k], 768, 1536, (r2.at[k, 1], 768))
-        start(("fm", k), part.at[3 + 2 * k], rf.at[k, 1], "down")
-        arrived(("z2p", k))
-        rows = ig_rows(sides[k], zp, 0, 32)
-        ig[rows, :] = ig_add(rows, z2.at[k, 0]).astype(bf16)
-        start(("zfp", k), ig.at[ig_rows(sides[k], zp, 0, 64)], zf.at[k, 0], "above")
-        arrived(("z2m", k))
-        rows = ig_rows(sides[k], zm, 32, 32)
-        ig[rows, :] = ig_add(rows, z2.at[k, 1]).astype(bf16)
-        start(("zfm", k), ig.at[ig_rows(sides[k], zm, 0, 64)], zf.at[k, 1], "below")
-
-    weight_part(block_of(y, columns[0]))
-    arrived(("fp", 0))
-    arrived(("fm", 0))
-    fold(part.at[6], 0, 1536, (rf.at[0, 0], 0), (rf.at[0, 1], 0))
-    start("xa", part.at[6, low], relay.at[0], "near")
-    start("xb", part.at[6, high], relay.at[1], "far")
-    arrived(("zfp", 0))
-    arrived(("zfm", 0))
-    rows = ig_rows(sides[0], z, 0, 64)
-    ig[rows, :] = ig_add(rows, zf.at[0, 0], zf.at[0, 1]).astype(bf16)
-    start("xz", ig.at[rows], xz, "near")
-    arrived("xa")
-    start("ya", relay.at[0], xr.at[low], "far")
-    arrived("xb")
-    start("yb", relay.at[1], xr.at[high], "near")
-    weight_part(block_of(y, columns[1]))
-    arrived(("zfp", 1))
-    arrived(("zfm", 1))
-    arrived("xz")
-    ig_out[...] = ig_add(ig_rows(sides[1], z, 0, 64), zf.at[1, 0], zf.at[1, 1], xz).astype(bf16)
-    arrived(("fp", 1))
-    arrived(("fm", 1))
-    arrived("ya")
-    arrived("yb")
-    fold(wg_out, 0, 1536, (rf.at[1, 0], 0), (rf.at[1, 1], 0), (xr, 0))
+    input_tiles(4)
+    z_first(1)
+    z_second(0)
+    weight_part(1, block_of(yp, xh))
+    weight_part(2, block_of(ym, xh))
+    z_second(1)
+    weight_part(0, block_of(y2, xh))
+    arrived("across0")
+    fold(part.at[3], 0, 0, 1536, (xin, 0))
+    start("up2", part.at[3, low], r2.at[0], "up")
+    start("down2", part.at[3, high], r2.at[1], "down")
+    weight_part(0, block_of(y, xo))
+    arrived("up0", "down0")
+    fold(part.at[6], 0, 0, 1536, (rf.at[0, 0], 0), (rf.at[0, 1], 0))
+    start("across1", part.at[6], xr, "across")
+    fold(part.at[4], 1, 768, 1536)
+    start("up1b", part.at[4, high], rf.at[1, 0, high], "up")
+    fold(part.at[5], 2, 0, 768)
+    start("down1a", part.at[5, low], rf.at[1, 1, low], "down")
+    weight_part(0, block_of(y, xh))
+    z_across(0)
+    z_across(1)
+    arrived("up2")
+    fold(part.at[4], 1, 0, 768, (r2.at[0], 0))
+    start("up1a", part.at[4, low], rf.at[1, 0, low], "up")
+    arrived("down2")
+    fold(part.at[5], 2, 768, 1536, (r2.at[1], 768))
+    start("down1b", part.at[5, high], rf.at[1, 1, high], "down")
+    z_last(0)
+    z_last(1)
+    arrived("across1", "up1a", "up1b", "down1a", "down1b")
+    fold(wg_out, 0, 0, 1536, (rf.at[1, 0], 0), (rf.at[1, 1], 0), (xr, 0))
     for copy in sent.values():
         copy.wait_send()
 
 
-def gradients(pgc, pgt, tokens, others, weight):
+def gradients(result, cotangent, keys, values, taps, tokens, others, weight):
     bf16 = jnp.bfloat16
     vmem = lambda *shape: pltpu.VMEM(shape, bf16)
     return pl.pallas_call(
-        reduce_kernel,
+        tail_kernel,
         out_shape=(
             jax.ShapeDtypeStruct((64, 4096), bf16),
             jax.ShapeDtypeStruct((1536, 256), bf16),
         ),
-        in_specs=[IN_VMEM, IN_VMEM, ANY, ANY, ANY],
+        in_specs=[ANY] + [IN_VMEM] * 4 + [ANY] * 3,
         out_specs=(IN_VMEM, IN_VMEM),
         scratch_shapes=[
             vmem(512, 4096),
             vmem(512, 2048),
             vmem(4096, 1536),
+            vmem(2, 512, 512),
+            vmem(3, 512, 640),
+            vmem(16, 1536),
+            vmem(16, 1536),
+            vmem(1536, 512),
+            vmem(512, 1536),
             vmem(1536, 512),
             vmem(512, 4096),
-            pltpu.VMEM((1536, 256), jnp.float32),
+            pltpu.VMEM((3, 1536, 256), jnp.float32),
             vmem(7, 1536, 256),
-            vmem(2, 2, 768, 256),
+            vmem(1536, 256),
+            vmem(2, 768, 256),
             vmem(2, 2, 1536, 256),
-            vmem(2, 768, 256),
             vmem(1536, 256),
-            vmem(2, 2, 32, 4096),
-            vmem(2, 2, 64, 4096),
-            vmem(64, 4096),
-            pltpu.SemaphoreType.DMA((22,)),
-            pltpu.SemaphoreType.DMA((22,)),
-            pltpu.SemaphoreType.DMA((4,)),
+            vmem(2, 2, 2, 32, 2048),
+            vmem(2, 2, 2, 64, 2048),
+            vmem(2, 64, 2048),
+            pltpu.SemaphoreType.DMA((48,)),
+            pltpu.SemaphoreType.DMA((48,)),
+            pltpu.SemaphoreType.DMA((5,)),
         ],
         compiler_params=pltpu.CompilerParams(
-            collective_id=3, has_side_effects=True, vmem_limit_bytes=56 * 1024 * 1024
+            collective_id=3, has_side_effects=True, vmem_limit_bytes=60 * 1024 * 1024
         ),
         cost_estimate=pl.CostEstimate(
             flops=4 * 512 * 4096 * 1536, bytes_accessed=24 * 1024 * 1024, transcendentals=0
         ),
-    )(pgc, pgt, tokens, others, weight)
+    )(result, cotangent, keys, values, taps, tokens, others, weight)
 
 
 def project_kernel(tokens, weight, projected, whole, others, tok, wall, acc, send, recv, load):
@@ -577,15 +657,6 @@
     ).astype(jnp.bfloat16)
 
 
-def short_backward(values, after, taps):
-    extended = jnp.concatenate([values, after], axis=2).astype(jnp.float32)
-    return (
-        taps[0][:, :, None] * extended[:, :, :-2]
-        + taps[1][:, :, None] * extended[:, :, 1:-1]
-        + taps[2][:, :, None] * extended[:, :, 2:]
-    ).astype(jnp.bfloat16)
-
-
 def on_device(tokens, in_weight, short_taps, long_filter, skip_bias, out_grad):
     f32, bf16 = jnp.float32, jnp.bfloat16
     projected, whole_weight, others = project(tokens, in_weight.reshape(256, 1536))
@@ -598,13 +669,11 @@
     outgoing = jnp.stack([streams[1] * streams[2], cotangent * streams[0]]).astype(bf16)
     arrived = exchange(outgoing, (2, 32, 8192), rows_of, positions_of, 1)
     filter_grad, result = convolve(arrived, long_filter, skip_bias)
-    returned = exchange(result, (2, 512, 512), positions_of, rows_of, 2).astype(f32)
-    conv_grad = jnp.stack(
-        [cotangent * returned[0], returned[1] * streams[2], returned[1] * streams[1]], axis=0
-    ).astype(bf16)
-    after = shifted(conv_grad[:, :, :2], "ctx", -1)
-    proj_grad = short_backward(conv_grad, after, short_taps).reshape(1536, 512)
-    input_grad, weight_grad = gradients(proj_grad, proj_grad.T, tokens, others, whole_weight)
+    streams = streams.astype(bf16)
+    taps = short_taps.reshape(9, 512).T
+    input_grad, weight_grad = gradients(
+        result, out_grad, streams[1], streams[2], taps, tokens, others, whole_weight
+    )
     return (input_grad, weight_grad.T.reshape(256, 3, 512), filter_grad)
 
 

time: 224 us -> 194 us (0.87)
  Pallas kernels: 183 us -> 170 us
  waiting for transfers between devices: 8.49 us -> 0 us
  other arithmetic: 11.4 us -> 6.1 us
    pallas_call x2 -> x1, Pallas kernels: 34.7 us -> 16.6 us  [exchange(): pl.pallas_call(functools.partial(exchange_kernel, pick, place), out_shape...]
    ppermute x1 -> x0, waiting for transfers between devices: 8.49 us -> none  [shifted(): lax.ppermute(value, axis, [(source, source + steps) for source in range(f...]
    pallas_call x1, Pallas kernels: 78.8 us -> 83.8 us  [gradients(): pl.pallas_call(tail_kernel, out_shape=(jax.ShapeDtypeStruct((64, 4096), b...]
    convert_element_type x3 -> x0, other arithmetic: 4.58 us -> none  [the longest x1 2.75 us: short_backward(): return (taps[0][:, :, None] * extended[:, :, :-2] + taps[1][:, :, None] *...]
    unnamed x33 -> x27, local copies, waits for them, and re-layouts: 10.6 us -> 9.17 us
  transfers between devices with their start and end apart: 1 -> 0, of which waited for: 1 -> 0; matrix products, arithmetic and copies ran while one was open for 0% -> 0% of each run, Pallas kernels for 0% -> 0%
where the time goes in v4:
time: 194 us; the launch traced here: 192 us
  Pallas kernels  170 us (88%)
  local copies, waits for them, and re-layouts  16 us (8%)
  other arithmetic  6.1 us (3%)
    pallas_call x1, Pallas kernels, gradients(): pl.pallas_call(tail_kernel, out_shape=(jax.ShapeDtypeStruct((64, 4096), b...  83.8 us
    pallas_call x1, Pallas kernels, project(): pl.pallas_call(project_kernel, out_shape=(jax.ShapeDtypeStruct((528, 1536...  58.4 us
    pallas_call x1, Pallas kernels, exchange(): pl.pallas_call(functools.partial(exchange_kernel, pick, place), out_shape...  16.6 us
    pallas_call x1, Pallas kernels, convolve(): pl.pallas_call(convolve_kernel, out_shape=(jax.ShapeDtypeStruct((32, BLOC...  10.8 us
    unnamed x27, local copies, waits for them, and re-layouts  9.17 us

profile of v4, /device:TPU:1, one launch (start us, length us, event | category | flops | bytes accessed | tf_op | source)
XLA Modules:
  0.0 192.4 jit_solution(8004563604728464291)
XLA Ops:
  0.6 1.4 copy.18
  2.0 0.3 copy.19.weight
  2.3 58.4 %shard_map.130 = (bf16[528,1536]{1,0:T(8,128)(2,1)S(1)}, bf16[16,256,1536]{2,1,0:T(8,128)(2,1)}, bf16[512,2048]{1,0:T(8,128)(2,1)S(1)}) custom-call(bf16[512,4096]{1,0:T(8,128)(2,1)} %tokens.3, bf16[256,1536]{1,0:T(8,128)(2,1)S(1)} %copy.19.weight), custom_call_target="tpu_custom_call" | custom-call | flops 6442450944 | bytes 25165824 | tf_op jit(solution)/shard_map/pallas_call | solution.py:625
  60.7 1.3 copy-done.8
  62.1 2.3 %copy.20 = bf16[1536,528]{1,0:T(8,128)(2,1)} copy(bf16[1536,528]{0,1:T(8,128)(2,1)S(1)} %bitcast.28) | data formatting | bytes 3244032 | tf_op jit(solution)/shard_map/transpose | solution.py:664
  64.3 2.3 %slice.53 = bf16[3,512,512]{2,1,0:T(8,128)(2,1)S(1)} slice(bf16[3,512,528]{2,1,0:T(8,128)(2,1)} %bitcast.29), slice={[0:3], [0:512], [16:528]} | slice | bytes 3145728 | tf_op jit(solution)/shard_map/slice | solution.py:666
  66.6 1.2 slice_select_fusion
  67.8 0.0 copy-start.10
  67.8 0.9 maximum_convert_fusion
  68.7 0.0 copy-start.9
  68.7 2.7 %fusion.7 = (f32[3,512,512]{2,1,0:T(8,128)S(1)}, bf16[3,512,512]{2,1,0:T(8,128)(2,1)S(1)}) fusion(f32[3,512,514]{2,1,0:T(8,128)S(1)} %maximum_convert_fusion, f32[3,512]{1,0:T(4,128)S(1)} %get-tuple-element.29, f32[3,512]{1,0:T(4,128)S(1)} %get-tuple-element.28, f32[3,512]{1,0:T(4,128)S(1)} %get-tuple-element.27), kind=kLoop, calls=%fused_computation.20 | loop fusion | flops 5505024 | bytes 14174208 | tf_op jit(solution)/shard_map/convert_element_type | solution.py:667
  71.4 0.2 fusion.5
  71.6 0.0 copy-start.11
  71.6 0.0 copy-start.1
  71.6 0.0 copy-start.2
  71.6 0.0 copy-start.3
  71.6 0.0 copy-start.4
  71.6 0.0 copy-start.5
  71.7 0.0 copy-start.6
  71.7 0.2 fusion.6
  71.8 1.1 pad_maximum_fusion.src
  72.9 16.6 %shard_map.131.arrived = bf16[2,32,8192]{2,1,0:T(8,128)(2,1)} custom-call(bf16[2,512,512]{2,1,0:T(8,128)(2,1)} %pad_maximum_fusion.src), custom_call_target="tpu_custom_call" | custom-call | tf_op jit(solution)/shard_map/pallas_call | solution.py:58
  89.5 0.1 broadcast_in_dim.11.bias
  89.5 0.0 copy-done.1
  89.6 1.2 copy-done
  90.8 10.8 %shard_map.132 = (f32[32,8192]{1,0:T(8,128)}, bf16[2,32,8192]{2,1,0:T(8,128)(2,1)S(1)}) custom-call(bf16[2,32,8192]{2,1,0:T(8,128)(2,1)S(1)} %copy-done, f32[32,8192]{1,0:T(8,128)S(1)} %copy-done.1, f32[32,128]{1,0:T(8,128)S(1)} %broadcast_in_dim.11.bias, bf16[128,64]{1,0:T(8,128)(2,1)S(1)} %copy-done.5, bf16[256,256]{1,0:T(8,128)(2,1)S(1)} %copy-done.2, ...), custom_call_target="tpu_custom_call" | custom-call | tf_op jit(solution)/shard_map/pallas_call | solution.py:157
  101.6 1.0 copy-done.7
  102.6 1.0 slice_bitcast_fusion.1
  103.6 0.8 copy.21
  104.5 83.8 %shard_map.133 = (bf16[64,4096]{1,0:T(8,128)(2,1)}, bf16[1536,256]{1,0:T(8,128)(2,1)}) custom-call(bf16[2,32,8192]{2,1,0:T(8,128)(2,1)} %copy-done.7, bf16[512,512]{1,0:T(8,128)(2,1)} %cotangent.1, bf16[512,512]{1,0:T(8,128)(2,1)} %get-tuple-element.26.keys, bf16[512,512]{1,0:T(8,128)(2,1)} %get-tuple-element.25.values, f32[512,9]{1,0:T(8,128)} %bitcast.33, ...), custom_call_target="tpu_custom_call" | custom-call | flops 12884901888 | bytes 25165824 | tf_op jit(solution)/shard_map/pallas_call | solution.py:435
  188.3 2.3 %copy.22 = bf16[256,3,512]{2,0,1:T(8,128)(2,1)} copy(bf16[256,3,512]{0,2,1:T(8,128)(2,1)} %bitcast.32) | data formatting | bytes 1572864
  190.6 1.9 copy.24
  (13 shorter events, 0.0 us)
Async XLA Ops:
  60.7 1.3 copy-start.8
  67.8 0.9 copy-start.10
  68.7 2.9 %copy-start.9 = (bf16[512,512]{1,0:T(8,128)(2,1)S(1)}, bf16[512,512]{1,0:T(8,128)(2,1)}, u32[]{:S(2)}) copy-start(bf16[512,512]{1,0:T(8,128)(2,1)} %cotangent.1) | copy-start | bytes 1572868
  71.6 17.9 %copy-start.11 = (f32[32]{0:T(128)S(1)}, f32[32]{0:T(128)}, u32[]{:S(2)}) copy-start(f32[32]{0:T(128)} %param.15) | copy-start | bytes 388
  71.6 17.9 %copy-start.1 = (f32[32,8192]{1,0:T(8,128)S(1)}, f32[32,8192]{1,0:T(8,128)}, u32[]{:S(2)}) copy-start(f32[32,8192]{1,0:T(8,128)} %filters.1) | copy-start | bytes 3145732
  71.6 17.9 %copy-start.2 = (bf16[256,256]{1,0:T(8,128)(2,1)S(1)}, bf16[256,256]{1,0:T(8,128)(2,1)}, u32[]{:S(2)}) copy-start(bf16[256,256]{1,0:T(8,128)(2,1)} %constant.22.clone.second) | copy-start | bytes 393220
  71.6 17.9 %copy-start.3 = (bf16[256,256]{1,0:T(8,128)(2,1)S(1)}, bf16[256,256]{1,0:T(8,128)(2,1)}, u32[]{:S(2)}) copy-start(bf16[256,256]{1,0:T(8,128)(2,1)} %constant.23.clone.second_back) | copy-start | bytes 393220
  71.6 17.9 %copy-start.4 = (f32[2,64,128]{2,1,0:T(8,128)S(1)}, f32[2,64,128]{2,1,0:T(8,128)}, u32[]{:S(2)}) copy-start(f32[2,64,128]{2,1,0:T(8,128)} %constant.20.clone.turn) | copy-start | bytes 196612
  71.6 17.9 %copy-start.5 = (bf16[128,64]{1,0:T(8,128)(2,1)S(1)}, bf16[128,64]{1,0:T(8,128)(2,1)}, u32[]{:S(2)}) copy-start(bf16[128,64]{1,0:T(8,128)(2,1)} %constant.21.clone.first) | copy-start | bytes 49156
  71.7 17.9 %copy-start.6 = (bf16[64,128]{1,0:T(8,128)(2,1)S(1)}, bf16[64,128]{1,0:T(8,128)(2,1)}, u32[]{:S(2)}) copy-start(bf16[64,128]{1,0:T(8,128)(2,1)} %constant.24.clone.first_back) | copy-start | bytes 49156
  89.6 1.2 copy-start
  101.6 1.0 copy-start.7

commit v5 on v4

--- a/solution.py
+++ b/solution.py
@@ -16,57 +16,6 @@
 LANES = 128
 BLOCKS = 64
 GROUP = 4
-
-
-def exchange_kernel(pick, place, src, out, send_sem, recv_sem, local_sem):
-    me = lax.axis_index("ctx")
-    barrier = pltpu.get_barrier_semaphore()
-    for step in range(1, N_CTX):
-        pl.semaphore_signal(
-            barrier, inc=1, device_id={"ctx": lax.rem(me + step, N_CTX)}, device_id_type=MESH
-        )
-    pl.semaphore_wait(barrier, N_CTX - 1)
-    copies = []
-    for step in range(1, N_CTX):
-        peer = lax.rem(me + step, N_CTX)
-        copy = pltpu.make_async_remote_copy(
-            src_ref=pick(src, peer),
-            dst_ref=place(out, me),
-            send_sem=send_sem.at[step - 1],
-            recv_sem=recv_sem.at[step - 1],
-            device_id={"ctx": peer},
-            device_id_type=MESH,
-        )
-        copy.start()
-        copies.append(copy)
-    own = pltpu.make_async_copy(pick(src, me), place(out, me), local_sem)
-    own.start()
-    own.wait()
-    for copy in copies:
-        copy.wait()
-
-
-def rows_of(ref, index):
-    return ref.at[:, pl.ds(pl.multiple_of(index * 32, 32), 32), :]
-
-
-def positions_of(ref, index):
-    return ref.at[:, :, pl.ds(pl.multiple_of(index * 512, 512), 512)]
-
-
-def exchange(value, shape, pick, place, collective_id):
-    return pl.pallas_call(
-        functools.partial(exchange_kernel, pick, place),
-        out_shape=jax.ShapeDtypeStruct(shape, value.dtype),
-        in_specs=[ANY],
-        out_specs=ANY,
-        scratch_shapes=[
-            pltpu.SemaphoreType.DMA((N_CTX - 1,)),
-            pltpu.SemaphoreType.DMA((N_CTX - 1,)),
-            pltpu.SemaphoreType.DMA,
-        ],
-        compiler_params=pltpu.CompilerParams(collective_id=collective_id, has_side_effects=True),
-    )(value)
 
 
 def tables():
@@ -86,85 +35,26 @@
     return low(first), low(second), low(second_back), low(first_back), turn
 
 
-def convolve_kernel(
-    arrived, filters, bias, first, second, second_back, first_back, turn, grad, result, held
-):
-    f32, bf16 = jnp.float32, jnp.bfloat16
+def turned(mixed, count, cos, sin):
+    result = []
+    for index in range(count):
+        at = slice(index * LANES, (index + 1) * LANES)
+        re, im = mixed[:BLOCKS, at], mixed[BLOCKS:, at]
+        both = jnp.concatenate([re * cos + im * sin, im * cos - re * sin], axis=1)
+        result.append(both.astype(jnp.bfloat16))
+    return jnp.concatenate(result, axis=0)
+
+
+def unturned(back, count, cos, sin):
     size = 2 * BLOCKS * LANES
-    for n in range(BLOCKS):
-        at = slice(n * LANES, (n + 1) * LANES)
-        rows = slice(n * 32, (n + 1) * 32)
-        held[0, rows, :] = arrived[0, :, at].astype(f32)
-        held[1, rows, :] = arrived[1, :, at].astype(f32)
-        held[2, rows, :] = filters[:, at]
-
-    def dot(a, b):
-        return jnp.dot(a, b, preferred_element_type=f32)
-
-    def some(step, carry):
-        cos, sin = turn[0], turn[1]
-        pairs = [(j, s) for j in range(GROUP) for s in range(3)]
-        signals = [
-            held[s, pl.ds(step * GROUP + j, BLOCKS, stride=32), :].astype(bf16) for j, s in pairs
-        ]
-        mixed = dot(first[...], jnp.concatenate(signals, axis=1))
-        turned = []
-        for index in range(len(pairs)):
-            at = slice(index * LANES, (index + 1) * LANES)
-            re, im = mixed[:BLOCKS, at], mixed[BLOCKS:, at]
-            turned.append(
-                jnp.concatenate([re * cos + im * sin, im * cos - re * sin], axis=1).astype(bf16)
-            )
-        spectra = dot(jnp.concatenate(turned, axis=0), second[...])
-        joined = []
-        for j in range(GROUP):
-            parts = []
-            for s in range(3):
-                rows = slice((3 * j + s) * BLOCKS, (3 * j + s + 1) * BLOCKS)
-                parts.append((spectra[rows, :LANES], spectra[rows, LANES:]))
-            (pr, pi), (wr, wi), (hr, hi) = parts
-            joined.append(jnp.concatenate([pr * hr - pi * hi, pr * hi + pi * hr], axis=1))
-            joined.append(jnp.concatenate([hr * wr + hi * wi, hr * wi - hi * wr], axis=1))
-            joined.append(jnp.concatenate([pr * wr + pi * wi, pr * wi - pi * wr], axis=1))
-        back = dot(jnp.concatenate(joined, axis=0).astype(bf16), second_back[...])
-        cos, sin = cos * (2.0 / size), sin * (2.0 / size)
-        unturned = []
-        for index in range(len(pairs)):
-            rows = slice(index * BLOCKS, (index + 1) * BLOCKS)
-            re, im = back[rows, :LANES], back[rows, LANES:]
-            unturned.append(
-                jnp.concatenate([re * cos - im * sin, im * cos + re * sin], axis=0).astype(bf16)
-            )
-        final = dot(first_back[...], jnp.concatenate(unturned, axis=1))
-        for index, (j, s) in enumerate(pairs):
-            held[s, pl.ds(step * GROUP + j, BLOCKS, stride=32), :] = final[
-                :, index * LANES : (index + 1) * LANES
-            ]
-        return carry
-
-    lax.fori_loop(0, 32 // GROUP, some, 0)
-    gain = bias[...]
-    for n in range(BLOCKS):
-        at = slice(n * LANES, (n + 1) * LANES)
-        rows = slice(n * 32, (n + 1) * 32)
-        for s in range(2):
-            result[s, :, at] = (held[s, rows, :] + gain * arrived[s, :, at].astype(f32)).astype(bf16)
-        grad[:, at] = held[2, rows, :]
-
-
-def convolve(arrived, long_filter, skip_bias):
-    bias = jnp.broadcast_to(skip_bias[:, None], (32, LANES))
-    return pl.pallas_call(
-        convolve_kernel,
-        out_shape=(
-            jax.ShapeDtypeStruct((32, BLOCKS * LANES), jnp.float32),
-            jax.ShapeDtypeStruct((2, 32, BLOCKS * LANES), jnp.bfloat16),
-        ),
-        in_specs=[IN_VMEM] * 8,
-        out_specs=(IN_VMEM, IN_VMEM),
-        scratch_shapes=[pltpu.VMEM((3, 32 * BLOCKS, LANES), jnp.float32)],
-        compiler_params=pltpu.CompilerParams(vmem_limit_bytes=48 * 1024 * 1024),
-    )(arrived, long_filter, bias, *tables())
+    cos, sin = cos * (2.0 / size), sin * (2.0 / size)
+    result = []
+    for index in range(count):
+        rows = slice(index * BLOCKS, (index + 1) * BLOCKS)
+        re, im = back[rows, :LANES], back[rows, LANES:]
+        both = jnp.concatenate([re * cos - im * sin, im * cos + re * sin], axis=0)
+        result.append(both.astype(jnp.bfloat16))
+    return jnp.concatenate(result, axis=1)
 
 
 def places():
@@ -195,9 +85,20 @@
     pl.semaphore_wait(barrier, len(peers))
 
 
+def rows_of(ref, index, group):
+    first = pl.multiple_of(index * 32 + group * 16, 16)
+    return ref.at[:, pl.ds(first, 16), :]
+
+
+def positions_of(ref, index, group):
+    return ref.at[:, pl.ds(group * 16, 16), pl.ds(pl.multiple_of(index * 512, 512), 512)]
+
+
 def tail_kernel(
-    result, cotangent, keys, values, taps, tokens, others, weight, ig_out, wg_out,
-    tok, oth, wei, ret, cgx, hout, hin, pgc, pgt, pgo, ig, acc, part, xin, r2, rf, xr, z2, zf, xz,
+    projected, cotangent, rowtaps, taps, filters, bias, first, second, second_back, first_back,
+    turn, tokens, others, weight, ig_out, wg_out, grad,
+    tok, oth, wei, keys, values, out, arr, held, fgs,
+    ret, cgx, hout, hin, pgc, pgt, pgo, ig, acc, part, xin, r2, rf, xr, z2, zf, xz,
     send, recv, load,
 ):
     f32, bf16 = jnp.float32, jnp.bfloat16
@@ -205,16 +106,30 @@
     core, xh, y, z, xl = at["core"], at["xh"], at["y"], at["z"], at["xl"]
     me = lax.axis_index("ctx")
     at["across"] = {"ctx": (y * 2 + 1 - xh) * 2 + core}
-    for step in range(1, N_CTX):
-        at[step] = {"ctx": lax.rem(me + step, N_CTX)}
+    steps = [(s, i) for s in range(4) for i in range(4)][1:]
+    fourth = lax.rem(me, 4)
+
+    def peer_of(s, i):
+        return lax.rem(y + s, 4) * 4 + lax.rem(fourth + i, 4)
+
+    for step in steps:
+        at[step] = {"ctx": peer_of(*step)}
+    at["last"] = {"ctx": lax.rem(me + N_CTX - 1, N_CTX)}
     loads = [
         pltpu.make_async_copy(weight.at[pl.ds(0, 2048)], wei.at[pl.ds(0, 2048)], load.at[0]),
-        pltpu.make_async_copy(tokens, tok, load.at[1]),
-        pltpu.make_async_copy(others, oth, load.at[2]),
-        pltpu.make_async_copy(weight.at[pl.ds(2048, 2048)], wei.at[pl.ds(2048, 2048)], load.at[3]),
-        pltpu.make_async_copy(positions_of(result, me), rows_of(ret, me), load.at[4]),
+        pltpu.make_async_copy(others, oth, load.at[1]),
+        pltpu.make_async_copy(weight.at[pl.ds(2048, 2048)], wei.at[pl.ds(2048, 2048)], load.at[2]),
     ]
-    greet([at[name] for name in (*range(1, N_CTX), "near", "above", "below")])
+    for j in range(8):
+        columns = pl.ds(pl.multiple_of((2 * j + core) * 256, 256), 256)
+        loads.append(
+            pltpu.make_async_copy(
+                tokens.at[:, columns], tok.at[:, pl.ds(j * 256, 256)], load.at[3 + j]
+            )
+        )
+    for one in loads:
+        one.start()
+    greet([at[name] for name in (*steps, "near", "above", "below")])
     sent = {}
 
     def start(name, src, dst, peer):
@@ -234,13 +149,131 @@
         for name in names:
             sent[name].wait_recv()
 
-    for step in range(1, N_CTX):
-        peer = lax.rem(me + step, N_CTX)
-        start(step, positions_of(result, peer), rows_of(ret, me), step)
-    for one in loads:
-        one.start()
-    loads[4].wait()
-    arrived(*range(1, N_CTX))
+    def head(x):
+        edge = x[0:16]
+        return jnp.concatenate([jnp.where(me == 0, jnp.zeros_like(edge), edge), x[16:]], axis=0)
+
+    def filtered(p, chunk):
+        columns = pl.ds(pl.multiple_of(p * 512 + chunk * 128, 128), 128)
+        own = pl.ds(pl.multiple_of(chunk * 128, 128), 128)
+        x = head(projected[:, columns].astype(f32))
+        total = rowtaps[p : p + 1, own] * x
+        for j in (1, 2):
+            total = total + rowtaps[3 * j + p : 3 * j + p + 1, own] * pltpu.roll(x, j, 0)
+        return total[16:].astype(bf16).T
+
+    def start_out(step, group):
+        peer = peer_of(*step)
+        start(("out", step, group), rows_of(out, peer, group), positions_of(arr, me, group), step)
+
+    for s in range(4):
+        chunk = lax.rem(y + s, 4)
+        rows = pl.ds(pl.multiple_of(chunk * 128, 128), 128)
+        query, key, value = (filtered(p, chunk) for p in range(3))
+        keys[rows, :] = key
+        values[rows, :] = value
+        out[0, rows, :] = (key.astype(f32) * value.astype(f32)).astype(bf16)
+        out[1, rows, :] = (cotangent[rows, :].astype(f32) * query.astype(f32)).astype(bf16)
+        for step in steps:
+            if step[0] == s:
+                start_out(step, 0)
+    for step in steps:
+        start_out(step, 1)
+    kept = []
+    for group in range(2):
+        copy = pltpu.make_async_copy(
+            rows_of(out, me, group), positions_of(arr, me, group), load.at[11 + group]
+        )
+        copy.start()
+        kept.append(copy)
+
+    def dot(a, b):
+        return jnp.dot(a, b, preferred_element_type=f32)
+
+    def channel(index):
+        return pl.ds(index, BLOCKS, stride=32)
+
+    def block(n):
+        return slice(n * LANES, (n + 1) * LANES)
+
+    for n in range(BLOCKS):
+        held[2, n * 32 : (n + 1) * 32, :] = filters[:, block(n)]
+
+    def filter_spectra(step, carry):
+        signals = [held[2, channel(step * 8 + j), :].astype(bf16) for j in range(8)]
+        mixed = dot(first[...], jnp.concatenate(signals, axis=1))
+        rows = pl.ds(pl.multiple_of(step * 512, 512), 512)
+        acc[rows, :] = dot(turned(mixed, 8, turn[0], turn[1]), second[...])
+        return carry
+
+    lax.fori_loop(0, 4, filter_spectra, 0)
+
+    def both_ways(start_at, step, carry):
+        index = start_at + step * 4
+        signals = [held[s, channel(index + j), :].astype(bf16) for j in range(4) for s in range(2)]
+        mixed = dot(first[...], jnp.concatenate(signals, axis=1))
+        spectra = dot(turned(mixed, 8, turn[0], turn[1]), second[...])
+        rows = pl.ds(pl.multiple_of(index * 64, 256), 256)
+        filt = acc[rows, :]
+        joined, kept = [], []
+        for j in range(4):
+            parts = []
+            for value in (
+                spectra[j * 128 : j * 128 + 64],
+                spectra[j * 128 + 64 : j * 128 + 128],
+                filt[j * 64 : j * 64 + 64],
+            ):
+                parts.append((value[:, :LANES], value[:, LANES:]))
+            (pr, pi), (wr, wi), (hr, hi) = parts
+            joined.append(jnp.concatenate([pr * hr - pi * hi, pr * hi + pi * hr], axis=1))
+            joined.append(jnp.concatenate([hr * wr + hi * wi, hr * wi - hi * wr], axis=1))
+            kept.append(jnp.concatenate([pr * wr + pi * wi, pr * wi - pi * wr], axis=1))
+        fgs[rows, :] = jnp.concatenate(kept, axis=0).astype(bf16)
+        back = dot(jnp.concatenate(joined, axis=0).astype(bf16), second_back[...])
+        final = dot(first_back[...], unturned(back, 8, turn[0], turn[1]))
+        for j in range(4):
+            for s in range(2):
+                held[s, channel(index + j), :] = final[:, block(2 * j + s)]
+        return carry
+
+    for group in range(2):
+        arrived(*(("out", step, group) for step in steps))
+        kept[group].wait()
+        own = slice(group * 16, group * 16 + 16)
+        for n in range(BLOCKS):
+            for s in range(2):
+                rows = slice(n * 32 + group * 16, n * 32 + group * 16 + 16)
+                held[s, rows, :] = arr[s, own, block(n)].astype(f32)
+        lax.fori_loop(0, 4, functools.partial(both_ways, group * 16), 0)
+        gain = bias[own, :]
+        for n in range(BLOCKS):
+            for s in range(2):
+                rows = slice(n * 32 + group * 16, n * 32 + group * 16 + 16)
+                direct = gain * arr[s, own, block(n)].astype(f32)
+                arr[s, own, block(n)] = (held[s, rows, :] + direct).astype(bf16)
+        for step in steps:
+            src = positions_of(arr, peer_of(*step), group)
+            start(("back", step, group), src, rows_of(ret, me, group), step)
+        copy = pltpu.make_async_copy(
+            positions_of(arr, me, group), rows_of(ret, me, group), load.at[13 + group]
+        )
+        copy.start()
+        kept.append(copy)
+
+    def filter_grads(step, carry):
+        rows = pl.ds(pl.multiple_of(step * 512, 512), 512)
+        back = dot(fgs[rows, :], second_back[...])
+        final = dot(first_back[...], unturned(back, 8, turn[0], turn[1]))
+        for j in range(8):
+            held[2, channel(step * 8 + j), :] = final[:, block(j)]
+        return carry
+
+    lax.fori_loop(0, 4, filter_grads, 0)
+    for n in range(BLOCKS):
+        grad[:, block(n)] = held[2, n * 32 : (n + 1) * 32, :]
+    for group in range(2):
+        arrived(*(("back", step, group) for step in steps))
+        kept[2 + group].wait()
 
     def lanes(p, chunk):
         return pl.ds(pl.multiple_of(p * 512 + chunk * 128, 128), 128)
@@ -256,7 +289,7 @@
         return carry
 
     lax.fori_loop(0, 4, stream_grads, 0)
-    start("halo", hout, hin, N_CTX - 1)
+    start("halo", hout, hin, "last")
 
     def tapped(p, rows, first, width, kept):
         x = cgx[p, rows, first : first + width].astype(f32)
@@ -302,15 +335,16 @@
 
         lax.fori_loop(0, 4, tile, 0)
 
+    def acc_rows(slot, row, count):
+        return pl.ds(pl.multiple_of(slot * 1536 + row, 128), count)
+
     def weight_part(slot, block):
-        mine = pl.ds(pl.multiple_of((2 * block + core) * 256, 256), 256)
-        theirs = pl.ds(pl.multiple_of(block * 256, 256), 256)
+        columns = pl.ds(pl.multiple_of(block * 256, 256), 256)
 
         def half(step, carry):
             rows = pl.ds(pl.multiple_of(step * 768, 256), 768)
-            acc[slot, rows, :] = jnp.dot(
-                pgc[rows, :], tok[:, mine], preferred_element_type=f32
-            ) + jnp.dot(pgo[rows, :], oth[:, theirs], preferred_element_type=f32)
+            value = dot(pgc[rows, :], tok[:, columns]) + dot(pgo[rows, :], oth[:, columns])
+            acc[acc_rows(slot, step * 768, 768), :] = value
             return carry
 
         lax.fori_loop(0, 2, half, 0)
@@ -318,7 +352,7 @@
     def fold(dst, slot, first, last, *terms):
         def chunk(step, carry):
             rows = pl.ds(pl.multiple_of(step * 128, 128), 128)
-            total = acc[slot, rows, :]
+            total = acc[acc_rows(slot, step * 128, 128), :]
             for term, offset in terms:
                 part_rows = pl.ds(pl.multiple_of(step * 128 - offset, 128), 128)
                 total = total + term[part_rows, :].astype(f32)
@@ -380,8 +414,8 @@
     loads[0].wait()
     input_tiles(0)
     z_first(0)
-    loads[1].wait()
-    loads[2].wait()
+    for one in (loads[1], *loads[3:]):
+        one.wait()
     arrived("twin0", "twin1")
     weight_part(0, block_of(y2, xo))
     fold(part.at[0], 0, 0, 1536)
@@ -392,7 +426,7 @@
     weight_part(0, block_of(ym, xo))
     fold(part.at[2], 0, 0, 1536)
     start("down0", part.at[2], rf.at[0, 1], "down")
-    loads[3].wait()
+    loads[2].wait()
     input_tiles(4)
     z_first(1)
     z_second(0)
@@ -406,8 +440,9 @@
     start("down2", part.at[3, high], r2.at[1], "down")
     weight_part(0, block_of(y, xo))
     arrived("up0", "down0")
-    fold(part.at[6], 0, 0, 1536, (rf.at[0, 0], 0), (rf.at[0, 1], 0))
-    start("across1", part.at[6], xr, "across")
+    sent["across0"].wait_send()
+    fold(part.at[0], 0, 0, 1536, (rf.at[0, 0], 0), (rf.at[0, 1], 0))
+    start("across1", part.at[0], xr, "across")
     fold(part.at[4], 1, 768, 1536)
     start("up1b", part.at[4, high], rf.at[1, 0, high], "up")
     fold(part.at[5], 2, 0, 768)
@@ -425,25 +460,35 @@
     z_last(1)
     arrived("across1", "up1a", "up1b", "down1a", "down1b")
     fold(wg_out, 0, 0, 1536, (rf.at[1, 0], 0), (rf.at[1, 1], 0), (xr, 0))
-    for copy in sent.values():
-        copy.wait_send()
-
-
-def gradients(result, cotangent, keys, values, taps, tokens, others, weight):
-    bf16 = jnp.bfloat16
+    for name, copy in sent.items():
+        if name != "across0":
+            copy.wait_send()
+
+
+def gradients(projected, out_grad, short_taps, long_filter, skip_bias, tokens, others, weight):
+    bf16, f32 = jnp.bfloat16, jnp.float32
     vmem = lambda *shape: pltpu.VMEM(shape, bf16)
+    rowtaps = short_taps.reshape(9, 512)
+    bias = jnp.broadcast_to(skip_bias[:, None], (32, LANES))
     return pl.pallas_call(
         tail_kernel,
         out_shape=(
             jax.ShapeDtypeStruct((64, 4096), bf16),
             jax.ShapeDtypeStruct((1536, 256), bf16),
+            jax.ShapeDtypeStruct((32, BLOCKS * LANES), f32),
         ),
-        in_specs=[ANY] + [IN_VMEM] * 4 + [ANY] * 3,
-        out_specs=(IN_VMEM, IN_VMEM),
+        in_specs=[IN_VMEM] * 11 + [ANY] * 3,
+        out_specs=(IN_VMEM,) * 3,
         scratch_shapes=[
-            vmem(512, 4096),
+            vmem(512, 2048),
             vmem(512, 2048),
             vmem(4096, 1536),
+            vmem(512, 512),
+            vmem(512, 512),
+            vmem(2, 512, 512),
+            vmem(2, 32, BLOCKS * LANES),
+            pltpu.VMEM((3, 32 * BLOCKS, LANES), f32),
+            vmem(32 * BLOCKS, 2 * LANES),
             vmem(2, 512, 512),
             vmem(3, 512, 640),
             vmem(16, 1536),
@@ -452,8 +497,8 @@
             vmem(512, 1536),
             vmem(1536, 512),
             vmem(512, 4096),
-            pltpu.VMEM((3, 1536, 256), jnp.float32),
-            vmem(7, 1536, 256),
+            pltpu.VMEM((4608, 256), f32),
+            vmem(6, 1536, 256),
             vmem(1536, 256),
             vmem(2, 768, 256),
             vmem(2, 2, 1536, 256),
@@ -461,17 +506,19 @@
             vmem(2, 2, 2, 32, 2048),
             vmem(2, 2, 2, 64, 2048),
             vmem(2, 64, 2048),
-            pltpu.SemaphoreType.DMA((48,)),
-            pltpu.SemaphoreType.DMA((48,)),
-            pltpu.SemaphoreType.DMA((5,)),
+            pltpu.SemaphoreType.DMA((91,)),
+            pltpu.SemaphoreType.DMA((91,)),
+            pltpu.SemaphoreType.DMA((15,)),
         ],
         compiler_params=pltpu.CompilerParams(
-            collective_id=3, has_side_effects=True, vmem_limit_bytes=60 * 1024 * 1024
+            collective_id=3, has_side_effects=True, vmem_limit_bytes=62 * 1024 * 1024
         ),
         cost_estimate=pl.CostEstimate(
             flops=4 * 512 * 4096 * 1536, bytes_accessed=24 * 1024 * 1024, transcendentals=0
         ),
-    )(result, cotangent, keys, values, taps, tokens, others, weight)
+    )(
+        projected, out_grad, rowtaps, rowtaps.T, long_filter, bias, *tables(), tokens, others, weight
+    )
 
 
 def project_kernel(tokens, weight, projected, whole, others, tok, wall, acc, send, recv, load):
@@ -648,31 +695,17 @@
     )(tokens, weight)
 
 
-def short_forward(values, before, taps):
-    extended = jnp.concatenate([before, values], axis=2).astype(jnp.float32)
-    return (
-        taps[0][:, :, None] * extended[:, :, 2:]
-        + taps[1][:, :, None] * extended[:, :, 1:-1]
-        + taps[2][:, :, None] * extended[:, :, :-2]
-    ).astype(jnp.bfloat16)
-
-
 def on_device(tokens, in_weight, short_taps, long_filter, skip_bias, out_grad):
-    f32, bf16 = jnp.float32, jnp.bfloat16
     projected, whole_weight, others = project(tokens, in_weight.reshape(256, 1536))
-    whole_weight = whole_weight.reshape(4096, 1536)
-    projected = projected.T.reshape(3, 512, 528)
-    before = jnp.where(lax.axis_index("ctx") == 0, jnp.zeros((), bf16), projected[:, :, 14:16])
-    projected = projected[:, :, 16:]
-    streams = short_forward(projected, before, short_taps).astype(f32)
-    cotangent = out_grad.astype(f32)
-    outgoing = jnp.stack([streams[1] * streams[2], cotangent * streams[0]]).astype(bf16)
-    arrived = exchange(outgoing, (2, 32, 8192), rows_of, positions_of, 1)
-    filter_grad, result = convolve(arrived, long_filter, skip_bias)
-    streams = streams.astype(bf16)
-    taps = short_taps.reshape(9, 512).T
-    input_grad, weight_grad = gradients(
-        result, out_grad, streams[1], streams[2], taps, tokens, others, whole_weight
+    input_grad, weight_grad, filter_grad = gradients(
+        projected,
+        out_grad,
+        short_taps,
+        long_filter,
+        skip_bias,
+        tokens,
+        others,
+        whole_weight.reshape(4096, 1536),
     )
     return (input_grad, weight_grad.T.reshape(256, 3, 512), filter_grad)
 

time: 194 us -> 173 us (0.89)
  Pallas kernels: 170 us -> 158 us
  other arithmetic: 6.1 us -> 0 us
  local copies, waits for them, and re-layouts: 16 us -> 13.5 us
    pallas_call x2 -> x0, Pallas kernels: 27.3 us -> none  [the longest x1 16.6 us: exchange(): pl.pallas_call(functools.partial(exchange_kernel, pick, place), out_shape...]
    pallas_call x1, Pallas kernels: 83.8 us -> 99.9 us  [gradients(): pl.pallas_call(tail_kernel, out_shape=(jax.ShapeDtypeStruct((64, 4096), b...]
    convert_element_type x2 -> x0, other arithmetic: 3.55 us -> none  [the longest x1 2.69 us: on_device(): streams = short_forward(projected, before, short_taps).astype(f32)]
    slice x1 -> x0, local copies, waits for them, and re-layouts: 2.29 us -> none  [on_device(): projected = projected[:, :, 16:]]
    transpose x1 -> x0, local copies, waits for them, and re-layouts: 2.25 us -> none  [on_device(): projected = projected.T.reshape(3, 512, 528)]
    unnamed x27 -> x10, local copies, waits for them, and re-layouts: 9.17 us -> 10.3 us
where the time goes in v5:
time: 173 us; the launch traced here: 172 us
  Pallas kernels  158 us (91%)
  local copies, waits for them, and re-layouts  13.5 us (8%)
    pallas_call x1, Pallas kernels, gradients(): pl.pallas_call(tail_kernel, out_shape=(jax.ShapeDtypeStruct((64, 4096), b...  99.9 us
    pallas_call x1, Pallas kernels, project(): pl.pallas_call(project_kernel, out_shape=(jax.ShapeDtypeStruct((528, 1536...  58.4 us
    unnamed x10, local copies, waits for them, and re-layouts  10.3 us

profile of v5, /device:TPU:1, one launch (start us, length us, event | category | flops | bytes accessed | tf_op | source)
XLA Modules:
  0.0 172.5 jit_solution(14437657154623436438)
XLA Ops:
  0.6 1.3 broadcast_in_dim.2.bias
  2.0 0.8 reshape.20.rowtaps
  2.7 0.0 copy-start.2
  2.7 0.9 copy.20
  3.6 1.4 copy.18
  5.0 0.3 copy.19.weight
  5.3 58.4 %shard_map.130 = (bf16[528,1536]{1,0:T(8,128)(2,1)S(1)}, bf16[16,256,1536]{2,1,0:T(8,128)(2,1)}, bf16[512,2048]{1,0:T(8,128)(2,1)S(1)}) custom-call(bf16[512,4096]{1,0:T(8,128)(2,1)} %tokens.3, bf16[256,1536]{1,0:T(8,128)(2,1)S(1)} %copy.19.weight), custom_call_target="tpu_custom_call" | custom-call | flops 6442450944 | bytes 25165824 | tf_op jit(solution)/shard_map/pallas_call | solution.py:672
  63.7 0.0 copy-done.2
  63.7 0.0 copy-start
  63.7 1.3 copy-done
  65.0 0.0 copy-start.1
  65.0 1.2 copy-done.1
  66.2 99.9 %shard_map.131 = (bf16[64,4096]{1,0:T(8,128)(2,1)}, bf16[1536,256]{1,0:T(8,128)(2,1)}, f32[32,8192]{1,0:T(8,128)}) custom-call(bf16[528,1536]{1,0:T(8,128)(2,1)} %copy-done.1, bf16[512,512]{1,0:T(8,128)(2,1)} %cotangent.1, f32[9,512]{1,0:T(8,128)} %copy-done.2, f32[512,9]{1,0:T(8,128)} %bitcast.8, f32[32,8192]{1,0:T(8,128)} %filters.1, ...), custom_call_target="tpu_custom_call" | custom-call | flops 12884901888 | bytes 25165824 | tf_op jit(solution)/shard_map/pallas_call | solution.py:473
  166.1 2.3 %copy.21 = bf16[256,3,512]{2,0,1:T(8,128)(2,1)} copy(bf16[256,3,512]{0,2,1:T(8,128)(2,1)} %bitcast.7) | data formatting | bytes 1572864
  168.4 1.9 %copy.24 = bf16[64,4096]{1,0:T(8,128)(2,1)} copy(bf16[64,4096]{1,0:T(8,128)(2,1)} %get-tuple-element.24) | data formatting | bytes 1048576
  170.2 2.3 %copy.25 = f32[32,8192]{1,0:T(8,128)} copy(f32[32,8192]{1,0:T(8,128)} %get-tuple-element.26) | data formatting | bytes 2097152
Async XLA Ops:
  2.7 60.9 %copy-start.2 = (f32[9,512]{1,0:T(8,128)}, f32[9,512]{1,0:T(8,128)S(1)}, u32[]{:S(2)}) copy-start(f32[9,512]{1,0:T(8,128)S(1)} %reshape.20.rowtaps) | copy-start | bytes 55300
  63.7 1.3 copy-start
  65.0 1.2 copy-start.1

commit v6 on v5

--- a/solution.py
+++ b/solution.py
@@ -94,18 +94,19 @@
     return ref.at[:, pl.ds(group * 16, 16), pl.ds(pl.multiple_of(index * 512, 512), 512)]
 
 
-def tail_kernel(
-    projected, cotangent, rowtaps, taps, filters, bias, first, second, second_back, first_back,
-    turn, tokens, others, weight, ig_out, wg_out, grad,
-    tok, oth, wei, keys, values, out, arr, held, fgs,
-    ret, cgx, hout, hin, pgc, pgt, pgo, ig, acc, part, xin, r2, rf, xr, z2, zf, xz,
-    send, recv, load,
+def mixer_kernel(
+    tokens, weight, cotangent_in, taps_in, filters_in, bias_in, first_in, second_in,
+    second_back_in, first_back_in, turn_in, ig_out, wg_out, grad,
+    tok, oth, wall, cotangent, taps, coltaps, filters, bias, gains, first, second, second_back, first_back,
+    turn, keys, values, out, arr, held, fgs, ret, cgx, hout, hin, pgc, pgt, pgo, ig, acc, part,
+    xin, r2, rf, xr, z2, zf, xz, send, recv, load,
 ):
     f32, bf16 = jnp.float32, jnp.bfloat16
     at = places()
     core, xh, y, z, xl = at["core"], at["xh"], at["y"], at["z"], at["xl"]
     me = lax.axis_index("ctx")
     at["across"] = {"ctx": (y * 2 + 1 - xh) * 2 + core}
+    at["next"] = {"ctx": lax.rem(me + 1, N_CTX)}
     steps = [(s, i) for s in range(4) for i in range(4)][1:]
     fourth = lax.rem(me, 4)
 
@@ -115,18 +116,22 @@
     for step in steps:
         at[step] = {"ctx": peer_of(*step)}
     at["last"] = {"ctx": lax.rem(me + N_CTX - 1, N_CTX)}
+    fetched = [
+        (weight, wall.at[me]),
+        (tokens, tok.at[pl.ds(16, 512)]),
+        (cotangent_in, cotangent),
+        (taps_in, taps),
+        (filters_in, filters),
+        (bias_in, bias),
+        (first_in, first),
+        (second_in, second),
+        (second_back_in, second_back),
+        (first_back_in, first_back),
+        (turn_in, turn),
+    ]
     loads = [
-        pltpu.make_async_copy(weight.at[pl.ds(0, 2048)], wei.at[pl.ds(0, 2048)], load.at[0]),
-        pltpu.make_async_copy(others, oth, load.at[1]),
-        pltpu.make_async_copy(weight.at[pl.ds(2048, 2048)], wei.at[pl.ds(2048, 2048)], load.at[2]),
+        pltpu.make_async_copy(src, dst, load.at[index]) for index, (src, dst) in enumerate(fetched)
     ]
-    for j in range(8):
-        columns = pl.ds(pl.multiple_of((2 * j + core) * 256, 256), 256)
-        loads.append(
-            pltpu.make_async_copy(
-                tokens.at[:, columns], tok.at[:, pl.ds(j * 256, 256)], load.at[3 + j]
-            )
-        )
     for one in loads:
         one.start()
     greet([at[name] for name in (*steps, "near", "above", "below")])
@@ -149,17 +154,121 @@
         for name in names:
             sent[name].wait_recv()
 
+    halves = (pl.ds(0, 128), pl.ds(128, 128))
+
+    def half_of(index, half):
+        return wall.at[index, halves[half]]
+
+    def pass_on(name, index, half, peer):
+        start(name, half_of(index, half), half_of(index, half), peer)
+
+    def hand_over(name, index):
+        start(name, wall.at[index], wall.at[index], "twin")
+
+    def multiply(index, fresh=False):
+        pair = index // 2
+        columns = pl.ds(pl.multiple_of(pair * 512, 512), 512)
+
+        def tile(step, carry):
+            place = pl.ds(pl.multiple_of(step * 512, 512), 512)
+            value = jnp.dot(
+                tok[:, columns],
+                wall[pl.ds(pair * 2, 2), :, place].reshape(512, 512),
+                preferred_element_type=f32,
+            )
+            for half in range(2):
+                rows = pl.ds(pl.multiple_of(step * 1056 + half * 528, 16), 528)
+                piece = value[:, half * 256 : half * 256 + 256]
+                acc[rows, :] = piece if fresh else acc[rows, :] + piece
+            return carry
+
+        lax.fori_loop(0, 3, tile, 0)
+
+    def ctx_of(y, xh):
+        return (lax.rem(y, 4) * 2 + xh) * 2 + core
+
+    below, above, beyond = ctx_of(y + 3, xh), ctx_of(y + 1, xh), ctx_of(y + 2, xh)
+    side = ctx_of(y, 1 - xh)
+    side_below, side_above = ctx_of(y + 3, 1 - xh), ctx_of(y + 1, 1 - xh)
+    side_beyond = ctx_of(y + 2, 1 - xh)
+
+    start("w_up0", weight.at[halves[0]], half_of(me, 0), "up")
+    start("w_down1", weight.at[halves[1]], half_of(me, 1), "down")
+    start("w_across", weight, wall.at[me], "across")
+    start("w_twin", weight, wall.at[me], "twin")
+    start("w_halo", tokens.at[pl.ds(496, 16)], tok.at[pl.ds(0, 16)], "next")
+    for j in range(8):
+        columns = pl.ds(pl.multiple_of((2 * j + 1 - core) * 256, 256), 256)
+        start(("swap", j), tokens.at[:, columns], oth.at[:, pl.ds(j * 256, 256)], "twin")
+    arrived("w_up0")
+    pass_on("w_on0", below, 0, "up")
+    arrived("w_down1")
+    pass_on("w_on1", above, 1, "down")
+    start("w_up1", weight.at[halves[1]], half_of(me, 1), "up")
+    start("w_down0", weight.at[halves[0]], half_of(me, 0), "down")
+    for one in loads:
+        one.wait()
+    arrived("w_halo", "w_twin")
+    multiply(me, fresh=True)
+    arrived("w_across")
+    pass_on("w_side_up0", side, 0, "up")
+    pass_on("w_side_down1", side, 1, "down")
+    hand_over("w_twin_side", side)
+    arrived("w_on0", "w_on1")
+    start("w_across_beyond", wall.at[beyond], wall.at[beyond], "across")
+    hand_over("w_twin_beyond", beyond)
+    pass_on("w_side_up1", side, 1, "up")
+    pass_on("w_side_down0", side, 0, "down")
+    arrived("w_twin_side")
+    multiply(side)
+    arrived("w_up1")
+    hand_over("w_twin_below", below)
+    arrived("w_down0")
+    hand_over("w_twin_above", above)
+    arrived("w_twin_beyond")
+    multiply(beyond)
+    arrived("w_twin_below")
+    multiply(below)
+    arrived("w_twin_above")
+    multiply(above)
+    arrived("w_side_up0")
+    pass_on("w_twin_sb0", side_below, 0, "twin")
+    arrived("w_side_down1")
+    pass_on("w_twin_sa1", side_above, 1, "twin")
+    arrived("w_across_beyond")
+    hand_over("w_twin_across", side_beyond)
+    arrived("w_twin_across")
+    multiply(side_beyond)
+    arrived("w_side_up1")
+    pass_on("w_twin_sb1", side_below, 1, "twin")
+    arrived("w_side_down0")
+    pass_on("w_twin_sa0", side_above, 0, "twin")
+    arrived("w_twin_sb0", "w_twin_sb1")
+    multiply(side_below)
+    arrived("w_twin_sa0", "w_twin_sa1")
+    multiply(side_above)
+
+    for j in range(8):
+        arrived(("swap", j))
+    coltaps[...] = jnp.concatenate([taps[0], taps[1], taps[2], jnp.zeros((7, 512), f32)], axis=0).T
+    diagonal = lax.broadcasted_iota(jnp.int32, (32, 32), 0) == lax.broadcasted_iota(
+        jnp.int32, (32, 32), 1
+    )
+    gain = jnp.where(diagonal, jnp.broadcast_to(bias[...], (32, 32)), 0.0)
+    gains[...] = jnp.broadcast_to(jnp.sum(gain, axis=1, keepdims=True), (32, LANES))
+
     def head(x):
         edge = x[0:16]
         return jnp.concatenate([jnp.where(me == 0, jnp.zeros_like(edge), edge), x[16:]], axis=0)
 
     def filtered(p, chunk):
-        columns = pl.ds(pl.multiple_of(p * 512 + chunk * 128, 128), 128)
+        rows = pl.ds(pl.multiple_of((p * 2 + chunk // 2) * 528, 16), 528)
+        columns = pl.ds(pl.multiple_of(lax.rem(chunk, 2) * 128, 128), 128)
         own = pl.ds(pl.multiple_of(chunk * 128, 128), 128)
-        x = head(projected[:, columns].astype(f32))
-        total = rowtaps[p : p + 1, own] * x
+        x = head(acc[rows, columns].astype(bf16).astype(f32))
+        total = taps[0, p : p + 1, own] * x
         for j in (1, 2):
-            total = total + rowtaps[3 * j + p : 3 * j + p + 1, own] * pltpu.roll(x, j, 0)
+            total = total + taps[j, p : p + 1, own] * pltpu.roll(x, j, 0)
         return total[16:].astype(bf16).T
 
     def start_out(step, group):
@@ -245,7 +354,7 @@
                 rows = slice(n * 32 + group * 16, n * 32 + group * 16 + 16)
                 held[s, rows, :] = arr[s, own, block(n)].astype(f32)
         lax.fori_loop(0, 4, functools.partial(both_ways, group * 16), 0)
-        gain = bias[own, :]
+        gain = gains[own, :]
         for n in range(BLOCKS):
             for s in range(2):
                 rows = slice(n * 32 + group * 16, n * 32 + group * 16 + 16)
@@ -293,9 +402,9 @@
 
     def tapped(p, rows, first, width, kept):
         x = cgx[p, rows, first : first + width].astype(f32)
-        total = taps[rows, p : p + 1] * x
+        total = coltaps[rows, p : p + 1] * x
         for j in (1, 2):
-            total = total + taps[rows, 3 * j + p : 3 * j + p + 1] * pltpu.roll(x, width - j, 1)
+            total = total + coltaps[rows, 3 * j + p : 3 * j + p + 1] * pltpu.roll(x, width - j, 1)
         return total[:, :kept].astype(bf16)
 
     def front(chunk, carry):
@@ -329,7 +438,10 @@
         def tile(step, carry):
             rows = pl.ds(pl.multiple_of((first + step) * 512, 512), 512)
             ig[:, rows] = lax.dot_general(
-                pgt[...], wei[rows, :], (((1,), (1,)), ((), ())), preferred_element_type=f32
+                pgt[...],
+                wall[pl.ds((first + step) * 2, 2)].reshape(512, 1536),
+                (((1,), (1,)), ((), ())),
+                preferred_element_type=f32,
             ).astype(bf16)
             return carry
 
@@ -338,13 +450,17 @@
     def acc_rows(slot, row, count):
         return pl.ds(pl.multiple_of(slot * 1536 + row, 128), count)
 
-    def weight_part(slot, block):
+    def weight_part(slot, block, own=True, theirs=True):
+        mine = pl.ds(pl.multiple_of((2 * block + core) * 256, 256), 256)
         columns = pl.ds(pl.multiple_of(block * 256, 256), 256)
 
         def half(step, carry):
             rows = pl.ds(pl.multiple_of(step * 768, 256), 768)
-            value = dot(pgc[rows, :], tok[:, columns]) + dot(pgo[rows, :], oth[:, columns])
-            acc[acc_rows(slot, step * 768, 768), :] = value
+            kept = acc_rows(slot, step * 768, 768)
+            value = dot(pgc[rows, :], tok[16:528, mine]) if own else acc[kept, :]
+            if theirs:
+                value = value + dot(pgo[rows, :], oth[:, columns])
+            acc[kept, :] = value
             return carry
 
         lax.fori_loop(0, 2, half, 0)
@@ -411,22 +527,17 @@
         rows = ig_rows(sides[1], z, 0, 64)
         ig_out[:, parts[h]] = ig_add(rows, h, zf.at[h, 1, 0], zf.at[h, 1, 1], xz.at[h])
 
-    loads[0].wait()
+    early = ((y2, xo), (yp, xo), (ym, xo))
+    for slot, place in enumerate(early):
+        weight_part(slot, block_of(*place), theirs=False)
+    arrived("twin0", "twin1")
+    for slot, place in enumerate(early):
+        weight_part(slot, block_of(*place), own=False)
+        fold(part.at[slot], slot, 0, 1536)
+        dst, peer = ((xin, "across"), (rf.at[0, 0], "up"), (rf.at[0, 1], "down"))[slot]
+        start((peer, 0), part.at[slot], dst, peer)
     input_tiles(0)
     z_first(0)
-    for one in (loads[1], *loads[3:]):
-        one.wait()
-    arrived("twin0", "twin1")
-    weight_part(0, block_of(y2, xo))
-    fold(part.at[0], 0, 0, 1536)
-    start("across0", part.at[0], xin, "across")
-    weight_part(0, block_of(yp, xo))
-    fold(part.at[1], 0, 0, 1536)
-    start("up0", part.at[1], rf.at[0, 0], "up")
-    weight_part(0, block_of(ym, xo))
-    fold(part.at[2], 0, 0, 1536)
-    start("down0", part.at[2], rf.at[0, 1], "down")
-    loads[2].wait()
     input_tiles(4)
     z_first(1)
     z_second(0)
@@ -434,13 +545,13 @@
     weight_part(2, block_of(ym, xh))
     z_second(1)
     weight_part(0, block_of(y2, xh))
-    arrived("across0")
+    arrived(("across", 0))
     fold(part.at[3], 0, 0, 1536, (xin, 0))
     start("up2", part.at[3, low], r2.at[0], "up")
     start("down2", part.at[3, high], r2.at[1], "down")
     weight_part(0, block_of(y, xo))
-    arrived("up0", "down0")
-    sent["across0"].wait_send()
+    arrived(("up", 0), ("down", 0))
+    sent[("across", 0)].wait_send()
     fold(part.at[0], 0, 0, 1536, (rf.at[0, 0], 0), (rf.at[0, 1], 0))
     start("across1", part.at[0], xr, "across")
     fold(part.at[4], 1, 768, 1536)
@@ -461,33 +572,43 @@
     arrived("across1", "up1a", "up1b", "down1a", "down1b")
     fold(wg_out, 0, 0, 1536, (rf.at[1, 0], 0), (rf.at[1, 1], 0), (xr, 0))
     for name, copy in sent.items():
-        if name != "across0":
+        if name != ("across", 0):
             copy.wait_send()
 
 
-def gradients(projected, out_grad, short_taps, long_filter, skip_bias, tokens, others, weight):
+def mixer(tokens, weight, out_grad, short_taps, long_filter, skip_bias):
     bf16, f32 = jnp.bfloat16, jnp.float32
     vmem = lambda *shape: pltpu.VMEM(shape, bf16)
-    rowtaps = short_taps.reshape(9, 512)
-    bias = jnp.broadcast_to(skip_bias[:, None], (32, LANES))
+    wide = lambda *shape: pltpu.VMEM(shape, f32)
     return pl.pallas_call(
-        tail_kernel,
+        mixer_kernel,
         out_shape=(
             jax.ShapeDtypeStruct((64, 4096), bf16),
             jax.ShapeDtypeStruct((1536, 256), bf16),
             jax.ShapeDtypeStruct((32, BLOCKS * LANES), f32),
         ),
-        in_specs=[IN_VMEM] * 11 + [ANY] * 3,
+        in_specs=[ANY] * 11,
         out_specs=(IN_VMEM,) * 3,
         scratch_shapes=[
+            vmem(528, 4096),
             vmem(512, 2048),
-            vmem(512, 2048),
-            vmem(4096, 1536),
+            vmem(N_CTX, 256, 1536),
+            vmem(512, 512),
+            wide(3, 3, 512),
+            wide(512, 16),
+            wide(32, BLOCKS * LANES),
+            wide(1, 32),
+            wide(32, LANES),
+            vmem(128, 64),
+            vmem(256, 256),
+            vmem(256, 256),
+            vmem(64, 128),
+            wide(2, 64, LANES),
             vmem(512, 512),
             vmem(512, 512),
             vmem(2, 512, 512),
             vmem(2, 32, BLOCKS * LANES),
-            pltpu.VMEM((3, 32 * BLOCKS, LANES), f32),
+            wide(3, 32 * BLOCKS, LANES),
             vmem(32 * BLOCKS, 2 * LANES),
             vmem(2, 512, 512),
             vmem(3, 512, 640),
@@ -497,7 +618,7 @@
             vmem(512, 1536),
             vmem(1536, 512),
             vmem(512, 4096),
-            pltpu.VMEM((4608, 256), f32),
+            wide(4608, 256),
             vmem(6, 1536, 256),
             vmem(1536, 256),
             vmem(2, 768, 256),
@@ -506,208 +627,53 @@
             vmem(2, 2, 2, 32, 2048),
             vmem(2, 2, 2, 64, 2048),
             vmem(2, 64, 2048),
-            pltpu.SemaphoreType.DMA((91,)),
-            pltpu.SemaphoreType.DMA((91,)),
+            pltpu.SemaphoreType.DMA((125,)),
+            pltpu.SemaphoreType.DMA((125,)),
             pltpu.SemaphoreType.DMA((15,)),
         ],
         compiler_params=pltpu.CompilerParams(
-            collective_id=3, has_side_effects=True, vmem_limit_bytes=62 * 1024 * 1024
-        ),
-        cost_estimate=pl.CostEstimate(
-            flops=4 * 512 * 4096 * 1536, bytes_accessed=24 * 1024 * 1024, transcendentals=0
+            collective_id=1, has_side_effects=True, vmem_limit_bytes=63 * 1024 * 1024
         ),
     )(
-        projected, out_grad, rowtaps, rowtaps.T, long_filter, bias, *tables(), tokens, others, weight
+        tokens, weight, out_grad, short_taps, long_filter, skip_bias.reshape(1, 32), *tables()
     )
 
 
-def project_kernel(tokens, weight, projected, whole, others, tok, wall, acc, send, recv, load):
-    f32, bf16 = jnp.float32, jnp.bfloat16
-    at = places()
-    core, xh, y = at["core"], at["xh"], at["y"]
-    me = lax.axis_index("ctx")
-    at["across"] = {"ctx": (y * 2 + 1 - xh) * 2 + core}
-    at["next"] = {"ctx": lax.rem(me + 1, N_CTX)}
-    at["last"] = {"ctx": lax.rem(me + N_CTX - 1, N_CTX)}
-    loads = [
-        pltpu.make_async_copy(weight, wall.at[me], load.at[0]),
-        pltpu.make_async_copy(tokens, tok.at[pl.ds(16, 512)], load.at[1]),
+def hand_out_kernel(ig_in, wg_in, grad_in, ig_out, wg_out, grad_out, wg, sem):
+    copies = [
+        pltpu.make_async_copy(wg_in, wg, sem.at[0]),
+        pltpu.make_async_copy(ig_in, ig_out, sem.at[1]),
+        pltpu.make_async_copy(grad_in, grad_out, sem.at[2]),
     ]
-    for one in loads:
-        one.start()
-    greet([at[name] for name in ("twin", "up", "down", "across", "next", "last")])
-    sent = {}
-
-    def start(name, src, dst, peer):
-        index = len(sent)
-        copy = pltpu.make_async_remote_copy(
-            src_ref=src,
-            dst_ref=dst,
-            send_sem=send.at[index],
-            recv_sem=recv.at[index],
-            device_id=at[peer],
-            device_id_type=MESH,
-        )
+    for copy in copies:
         copy.start()
-        sent[name] = copy
-
-    def arrived(*names):
-        for name in names:
-            sent[name].wait_recv()
-
-    halves = (pl.ds(0, 128), pl.ds(128, 128))
-
-    def half_of(index, half):
-        return wall.at[index, halves[half]]
-
-    def pass_on(name, index, half, peer):
-        start(name, half_of(index, half), half_of(index, half), peer)
-
-    def hand_over(name, index):
-        start(name, wall.at[index], wall.at[index], "twin")
-
-    stored = []
-
-    def multiply(index, fresh=False):
-        pair = index // 2
-        columns = pl.ds(pl.multiple_of(pair * 512, 512), 512)
-        store = pltpu.make_async_copy(
-            wall.at[pl.ds(pair * 2, 2)], whole.at[pl.ds(pair * 2, 2)], load.at[2 + len(stored)]
-        )
-        store.start()
-        stored.append(store)
-
-        def tile(step, carry):
-            place = pl.ds(pl.multiple_of(step * 512, 512), 512)
-            value = jnp.dot(
-                tok[:, columns],
-                wall[pl.ds(pair * 2, 2), :, place].reshape(512, 512),
-                preferred_element_type=f32,
-            )
-            acc[:, place] = value if fresh else acc[:, place] + value
-            return carry
-
-        lax.fori_loop(0, 3, tile, 0)
-
-    def ctx_of(y, xh):
-        return (lax.rem(y, 4) * 2 + xh) * 2 + core
-
-    below, above, beyond = ctx_of(y + 3, xh), ctx_of(y + 1, xh), ctx_of(y + 2, xh)
-    side = ctx_of(y, 1 - xh)
-    side_below, side_above = ctx_of(y + 3, 1 - xh), ctx_of(y + 1, 1 - xh)
-    side_beyond = ctx_of(y + 2, 1 - xh)
-
-    start("up0", weight.at[halves[0]], half_of(me, 0), "up")
-    start("down1", weight.at[halves[1]], half_of(me, 1), "down")
-    start("across", weight, wall.at[me], "across")
-    start("twin", weight, wall.at[me], "twin")
-    start("halo", tokens.at[pl.ds(496, 16)], tok.at[pl.ds(0, 16)], "next")
-    for j in range(8):
-        columns = pl.ds(pl.multiple_of((2 * j + 1 - core) * 256, 256), 256)
-        start(("swap", j), tokens.at[:, columns], others.at[:, pl.ds(j * 256, 256)], "twin")
-    arrived("up0")
-    pass_on("on0", below, 0, "up")
-    arrived("down1")
-    pass_on("on1", above, 1, "down")
-    start("up1", weight.at[halves[1]], half_of(me, 1), "up")
-    start("down0", weight.at[halves[0]], half_of(me, 0), "down")
-    for one in loads:
-        one.wait()
-    arrived("halo", "twin")
-    multiply(me, fresh=True)
-    arrived("across")
-    pass_on("side_up0", side, 0, "up")
-    pass_on("side_down1", side, 1, "down")
-    hand_over("twin_side", side)
-    arrived("on0", "on1")
-    start("across_beyond", wall.at[beyond], wall.at[beyond], "across")
-    hand_over("twin_beyond", beyond)
-    pass_on("side_up1", side, 1, "up")
-    pass_on("side_down0", side, 0, "down")
-    arrived("twin_side")
-    multiply(side)
-    arrived("up1")
-    hand_over("twin_below", below)
-    arrived("down0")
-    hand_over("twin_above", above)
-    arrived("twin_beyond")
-    multiply(beyond)
-    arrived("twin_below")
-    multiply(below)
-    arrived("twin_above")
-    multiply(above)
-    arrived("side_up0")
-    pass_on("twin_sb0", side_below, 0, "twin")
-    arrived("side_down1")
-    pass_on("twin_sa1", side_above, 1, "twin")
-    arrived("across_beyond")
-    hand_over("twin_across", side_beyond)
-    arrived("twin_across")
-    multiply(side_beyond)
-    arrived("side_up1")
-    pass_on("twin_sb1", side_below, 1, "twin")
-    arrived("side_down0")
-    pass_on("twin_sa0", side_above, 0, "twin")
-    arrived("twin_sb0", "twin_sb1")
-    multiply(side_below)
-    arrived("twin_sa0", "twin_sa1")
-    multiply(side_above)
-
-    def finish(step, carry):
-        rows = pl.ds(pl.multiple_of(step * 48, 16), 48)
-        projected[rows, :] = acc[rows, :].astype(bf16)
-        return carry
-
-    lax.fori_loop(0, 11, finish, 0)
-    for j in range(8):
-        arrived(("swap", j))
-    for store in stored:
-        store.wait()
-    for copy in sent.values():
-        copy.wait_send()
-
-
-def project(tokens, weight):
+    copies[0].wait()
+    for p in range(3):
+        wg_out[:, p, :] = wg[p * 512 : (p + 1) * 512, :].T
+    for copy in copies[1:]:
+        copy.wait()
+
+
+def hand_out(input_grad, weight_grad, filter_grad):
     bf16 = jnp.bfloat16
     return pl.pallas_call(
-        project_kernel,
+        hand_out_kernel,
         out_shape=(
-            jax.ShapeDtypeStruct((528, 1536), bf16),
-            jax.ShapeDtypeStruct((N_CTX, 256, 1536), bf16),
-            jax.ShapeDtypeStruct((512, 2048), bf16),
+            jax.ShapeDtypeStruct((64, 4096), bf16),
+            jax.ShapeDtypeStruct((256, 3, 512), bf16),
+            jax.ShapeDtypeStruct((32, BLOCKS * LANES), jnp.float32),
         ),
-        in_specs=[ANY, ANY],
-        out_specs=(IN_VMEM, ANY, ANY),
-        scratch_shapes=[
-            pltpu.VMEM((528, 4096), bf16),
-            pltpu.VMEM((N_CTX, 256, 1536), bf16),
-            pltpu.VMEM((528, 1536), jnp.float32),
-            pltpu.SemaphoreType.DMA((34,)),
-            pltpu.SemaphoreType.DMA((34,)),
-            pltpu.SemaphoreType.DMA((10,)),
-        ],
-        compiler_params=pltpu.CompilerParams(
-            collective_id=4, has_side_effects=True, vmem_limit_bytes=48 * 1024 * 1024
-        ),
-        cost_estimate=pl.CostEstimate(
-            flops=2 * 512 * 4096 * 1536, bytes_accessed=24 * 1024 * 1024, transcendentals=0
-        ),
-    )(tokens, weight)
+        in_specs=[ANY] * 3,
+        out_specs=(ANY, IN_VMEM, ANY),
+        scratch_shapes=[pltpu.VMEM((1536, 256), bf16), pltpu.SemaphoreType.DMA((3,))],
+        compiler_params=pltpu.CompilerParams(vmem_limit_bytes=32 * 1024 * 1024),
+    )(input_grad, weight_grad, filter_grad)
 
 
 def on_device(tokens, in_weight, short_taps, long_filter, skip_bias, out_grad):
-    projected, whole_weight, others = project(tokens, in_weight.reshape(256, 1536))
-    input_grad, weight_grad, filter_grad = gradients(
-        projected,
-        out_grad,
-        short_taps,
-        long_filter,
-        skip_bias,
-        tokens,
-        others,
-        whole_weight.reshape(4096, 1536),
-    )
-    return (input_grad, weight_grad.T.reshape(256, 3, 512), filter_grad)
+    weight = in_weight.reshape(256, 1536)
+    results = mixer(tokens, weight, out_grad, short_taps, long_filter, skip_bias)
+    return hand_out(*results)
 
 
 def solution(mesh):

time: 173 us -> 164 us (0.948)
  local copies, waits for them, and re-layouts: 13.5 us -> 7 us
  Pallas kernels: 158 us -> 156 us
    unnamed x10 -> x7, local copies, waits for them, and re-layouts: 10.3 us -> 4.79 us
    pallas_call x2, Pallas kernels: 158 us -> 156 us  [the longest x1 155 us: mixer(): pl.pallas_call(mixer_kernel, out_shape=(jax.ShapeDtypeStruct((64, 4096),...]
where the time goes in v6:
time: 164 us
  Pallas kernels  156 us (95%)
  local copies, waits for them, and re-layouts  7 us (4%)
    pallas_call x1, Pallas kernels, mixer(): pl.pallas_call(mixer_kernel, out_shape=(jax.ShapeDtypeStruct((64, 4096),...  155 us
    unnamed x7, local copies, waits for them, and re-layouts  4.79 us

profile of v6, /device:TPU:1, one launch (start us, length us, event | category | flops | bytes accessed | tf_op | source)
XLA Modules:
  0.0 163.8 jit_solution(12382519529253024838)
XLA Ops:
  0.6 1.4 copy.16
  2.0 1.2 copy.17.weight
  3.2 154.9 %shard_map.130 = (bf16[64,4096]{1,0:T(8,128)(2,1)}, bf16[1536,256]{1,0:T(8,128)(2,1)}, f32[32,8192]{1,0:T(8,128)}) custom-call(bf16[512,4096]{1,0:T(8,128)(2,1)} %tokens.1, bf16[256,1536]{1,0:T(8,128)(2,1)} %copy.17.weight, bf16[512,512]{1,0:T(8,128)(2,1)} %cotangent_in.1, f32[3,3,512]{2,1,0:T(4,128)} %taps_in.1, f32[32,8192]{1,0:T(8,128)} %filters_in.1, ...), custom_call_target="tpu_custom_call" | custom-call | tf_op jit(solution)/shard_map/pallas_call | solution.py:583
  158.1 0.0 copy-start
  158.1 1.2 copy-done
  159.4 0.0 copy-start.1
  159.4 1.1 copy-done.1
  160.5 0.0 copy-start.2
  160.5 1.0 copy-done.2
  161.5 1.2 shard_map.131
  162.8 1.1 copy.18
Async XLA Ops:
  158.1 1.2 copy-start
  159.4 1.1 copy-start.1
  160.5 1.0 copy-start.2

commit v7 on v6

--- a/solution.py
+++ b/solution.py
@@ -117,7 +117,6 @@
         at[step] = {"ctx": peer_of(*step)}
     at["last"] = {"ctx": lax.rem(me + N_CTX - 1, N_CTX)}
     fetched = [
-        (weight, wall.at[me]),
         (tokens, tok.at[pl.ds(16, 512)]),
         (cotangent_in, cotangent),
         (taps_in, taps),
@@ -132,7 +131,13 @@
     loads = [
         pltpu.make_async_copy(src, dst, load.at[index]) for index, (src, dst) in enumerate(fetched)
     ]
-    for one in loads:
+    own_weight = [
+        pltpu.make_async_copy(
+            weight.at[p], wall.at[me, :, pl.ds(p * 512, 512)], load.at[15 + p]
+        )
+        for p in range(3)
+    ]
+    for one in (*own_weight, *loads):
         one.start()
     greet([at[name] for name in (*steps, "near", "above", "below")])
     sent = {}
@@ -192,10 +197,12 @@
     side_below, side_above = ctx_of(y + 3, 1 - xh), ctx_of(y + 1, 1 - xh)
     side_beyond = ctx_of(y + 2, 1 - xh)
 
-    start("w_up0", weight.at[halves[0]], half_of(me, 0), "up")
-    start("w_down1", weight.at[halves[1]], half_of(me, 1), "down")
-    start("w_across", weight, wall.at[me], "across")
-    start("w_twin", weight, wall.at[me], "twin")
+    for one in own_weight:
+        one.wait()
+    pass_on("w_up0", me, 0, "up")
+    pass_on("w_down1", me, 1, "down")
+    start("w_across", wall.at[me], wall.at[me], "across")
+    hand_over("w_twin", me)
     start("w_halo", tokens.at[pl.ds(496, 16)], tok.at[pl.ds(0, 16)], "next")
     for j in range(8):
         columns = pl.ds(pl.multiple_of((2 * j + 1 - core) * 256, 256), 256)
@@ -204,8 +211,8 @@
     pass_on("w_on0", below, 0, "up")
     arrived("w_down1")
     pass_on("w_on1", above, 1, "down")
-    start("w_up1", weight.at[halves[1]], half_of(me, 1), "up")
-    start("w_down0", weight.at[halves[0]], half_of(me, 0), "down")
+    pass_on("w_up1", me, 1, "up")
+    pass_on("w_down0", me, 0, "down")
     for one in loads:
         one.wait()
     arrived("w_halo", "w_twin")
@@ -570,7 +577,17 @@
     z_last(0)
     z_last(1)
     arrived("across1", "up1a", "up1b", "down1a", "down1b")
-    fold(wg_out, 0, 0, 1536, (rf.at[1, 0], 0), (rf.at[1, 1], 0), (xr, 0))
+
+    def last_fold(step, carry):
+        rows = pl.ds(pl.multiple_of(step * 128, 128), 128)
+        total = acc[rows, :]
+        for term in (rf.at[1, 0], rf.at[1, 1], xr):
+            total = total + term[rows, :].astype(f32)
+        columns = pl.ds(pl.multiple_of(lax.rem(step, 4) * 128, 128), 128)
+        wg_out[step // 4, :, columns] = total.T.astype(bf16)
+        return carry
+
+    lax.fori_loop(0, 12, last_fold, 0)
     for name, copy in sent.items():
         if name != ("across", 0):
             copy.wait_send()
@@ -584,7 +601,7 @@
         mixer_kernel,
         out_shape=(
             jax.ShapeDtypeStruct((64, 4096), bf16),
-            jax.ShapeDtypeStruct((1536, 256), bf16),
+            jax.ShapeDtypeStruct((3, 256, 512), bf16),
             jax.ShapeDtypeStruct((32, BLOCKS * LANES), f32),
         ),
         in_specs=[ANY] * 11,
@@ -629,7 +646,7 @@
             vmem(2, 64, 2048),
             pltpu.SemaphoreType.DMA((125,)),
             pltpu.SemaphoreType.DMA((125,)),
-            pltpu.SemaphoreType.DMA((15,)),
+            pltpu.SemaphoreType.DMA((18,)),
         ],
         compiler_params=pltpu.CompilerParams(
             collective_id=1, has_side_effects=True, vmem_limit_bytes=63 * 1024 * 1024
@@ -639,41 +656,35 @@
     )
 
 
-def hand_out_kernel(ig_in, wg_in, grad_in, ig_out, wg_out, grad_out, wg, sem):
+def hand_out_kernel(*refs):
+    count = len(refs) // 2
     copies = [
-        pltpu.make_async_copy(wg_in, wg, sem.at[0]),
-        pltpu.make_async_copy(ig_in, ig_out, sem.at[1]),
-        pltpu.make_async_copy(grad_in, grad_out, sem.at[2]),
+        pltpu.make_async_copy(refs[index], refs[count + index], refs[-1].at[index])
+        for index in range(count)
     ]
     for copy in copies:
         copy.start()
-    copies[0].wait()
-    for p in range(3):
-        wg_out[:, p, :] = wg[p * 512 : (p + 1) * 512, :].T
-    for copy in copies[1:]:
+    for copy in copies:
         copy.wait()
 
 
-def hand_out(input_grad, weight_grad, filter_grad):
-    bf16 = jnp.bfloat16
+def hand_out(results):
+    in_hbm = pl.BlockSpec(memory_space=pltpu.HBM)
     return pl.pallas_call(
         hand_out_kernel,
-        out_shape=(
-            jax.ShapeDtypeStruct((64, 4096), bf16),
-            jax.ShapeDtypeStruct((256, 3, 512), bf16),
-            jax.ShapeDtypeStruct((32, BLOCKS * LANES), jnp.float32),
-        ),
-        in_specs=[ANY] * 3,
-        out_specs=(ANY, IN_VMEM, ANY),
-        scratch_shapes=[pltpu.VMEM((1536, 256), bf16), pltpu.SemaphoreType.DMA((3,))],
-        compiler_params=pltpu.CompilerParams(vmem_limit_bytes=32 * 1024 * 1024),
-    )(input_grad, weight_grad, filter_grad)
+        out_shape=[jax.ShapeDtypeStruct(value.shape, value.dtype) for value in results],
+        in_specs=[in_hbm] * len(results),
+        out_specs=[in_hbm] * len(results),
+        scratch_shapes=[pltpu.SemaphoreType.DMA((len(results),))],
+        compiler_params=pltpu.CompilerParams(vmem_limit_bytes=63 * 1024 * 1024),
+    )(*results)
 
 
 def on_device(tokens, in_weight, short_taps, long_filter, skip_bias, out_grad):
-    weight = in_weight.reshape(256, 1536)
+    weight = jnp.transpose(in_weight, (1, 0, 2))
     results = mixer(tokens, weight, out_grad, short_taps, long_filter, skip_bias)
-    return hand_out(*results)
+    input_grad, weight_grad, filter_grad = hand_out(results)
+    return input_grad, jnp.transpose(weight_grad, (1, 0, 2)), filter_grad
 
 
 def solution(mesh):

time: 164 us -> 229 us (1.40)
  Pallas kernels: 156 us -> 228 us
  local copies, waits for them, and re-layouts: 7 us -> 0 us
    pallas_call x1, Pallas kernels: 1.22 us -> 72.6 us  [hand_out(): pl.pallas_call(hand_out_kernel, out_shape=[jax.ShapeDtypeStruct(value.sha...]
    unnamed x7 -> x0, local copies, waits for them, and re-layouts: 4.79 us -> none
where the time goes in v7:
time: 229 us
  Pallas kernels  228 us (100%)
    pallas_call x1, Pallas kernels, mixer(): pl.pallas_call(mixer_kernel, out_shape=(jax.ShapeDtypeStruct((64, 4096),...  156 us
    pallas_call x1, Pallas kernels, hand_out(): pl.pallas_call(hand_out_kernel, out_shape=[jax.ShapeDtypeStruct(value.sha...  72.6 us

profile of v7, /device:TPU:1, one launch (start us, length us, event | category | flops | bytes accessed | tf_op | source)
XLA Modules:
  0.0 229.2 jit_solution(3537623162609565241)
XLA Ops:
  0.6 155.8 %shard_map.130 = (bf16[64,4096]{1,0:T(8,128)(2,1)}, bf16[3,256,512]{2,1,0:T(8,128)(2,1)}, f32[32,8192]{1,0:T(8,128)}) custom-call(bf16[512,4096]{1,0:T(8,128)(2,1)} %tokens.1, bf16[3,256,512]{2,1,0:T(8,128)(2,1)} %bitcast.3, bf16[512,512]{1,0:T(8,128)(2,1)} %cotangent_in.1, f32[3,3,512]{2,1,0:T(4,128)} %taps_in.1, f32[32,8192]{1,0:T(8,128)} %filters_in.1, ...), custom_call_target="tpu_custom_call" | custom-call | tf_op jit(solution)/shard_map/pallas_call | solution.py:600
  156.5 72.6 %shard_map.131 = (bf16[64,4096]{1,0:T(8,128)(2,1)}, bf16[3,256,512]{2,1,0:T(8,128)(2,1)}, f32[32,8192]{1,0:T(8,128)}) custom-call(bf16[64,4096]{1,0:T(8,128)(2,1)} %get-tuple-element.9.refs_0_, bf16[3,256,512]{2,1,0:T(8,128)(2,1)} %get-tuple-element.10.refs_1_, f32[32,8192]{1,0:T(8,128)} %get-tuple-element.11.refs_2_), custom_call_target="tpu_custom_call" | custom-call | tf_op jit(solution)/shard_map/pallas_call | solution.py:673

commit v8 on v7

--- a/solution.py
+++ b/solution.py
@@ -257,7 +257,10 @@
 
     for j in range(8):
         arrived(("swap", j))
-    coltaps[...] = jnp.concatenate([taps[0], taps[1], taps[2], jnp.zeros((7, 512), f32)], axis=0).T
+    columns = jnp.concatenate([taps[0], taps[1], taps[2], jnp.zeros((7, 512), f32)], axis=0).T
+    for group in range(2):
+        pieces = [columns[i * 32 + group * 16 : i * 32 + group * 16 + 16] for i in range(N_CTX)]
+        coltaps[group] = jnp.concatenate(pieces, axis=0)
     diagonal = lax.broadcasted_iota(jnp.int32, (32, 32), 0) == lax.broadcasted_iota(
         jnp.int32, (32, 32), 1
     )
@@ -286,8 +289,11 @@
         chunk = lax.rem(y + s, 4)
         rows = pl.ds(pl.multiple_of(chunk * 128, 128), 128)
         query, key, value = (filtered(p, chunk) for p in range(3))
-        keys[rows, :] = key
-        values[rows, :] = value
+        for group in range(2):
+            compact = pl.ds(pl.multiple_of(chunk * 64, 16), 64)
+            for dst, src in ((keys, key), (values, value)):
+                pieces = [src[i * 32 + group * 16 : i * 32 + group * 16 + 16] for i in range(4)]
+                dst[group, compact, :] = jnp.concatenate(pieces, axis=0)
         out[0, rows, :] = (key.astype(f32) * value.astype(f32)).astype(bf16)
         out[1, rows, :] = (cotangent[rows, :].astype(f32) * query.astype(f32)).astype(bf16)
         for step in steps:
@@ -352,6 +358,9 @@
                 held[s, channel(index + j), :] = final[:, block(2 * j + s)]
         return carry
 
+    def compact_of(group):
+        return ret.at[group, :, pl.ds(pl.multiple_of(me * 16, 16), 16), :]
+
     for group in range(2):
         arrived(*(("out", step, group) for step in steps))
         kept[group].wait()
@@ -369,9 +378,9 @@
                 arr[s, own, block(n)] = (held[s, rows, :] + direct).astype(bf16)
         for step in steps:
             src = positions_of(arr, peer_of(*step), group)
-            start(("back", step, group), src, rows_of(ret, me, group), step)
+            start(("back", step, group), src, compact_of(group), step)
         copy = pltpu.make_async_copy(
-            positions_of(arr, me, group), rows_of(ret, me, group), load.at[13 + group]
+            positions_of(arr, me, group), compact_of(group), load.at[13 + group]
         )
         copy.start()
         kept.append(copy)
@@ -384,62 +393,84 @@
             held[2, channel(step * 8 + j), :] = final[:, block(j)]
         return carry
 
-    lax.fori_loop(0, 4, filter_grads, 0)
-    for n in range(BLOCKS):
-        grad[:, block(n)] = held[2, n * 32 : (n + 1) * 32, :]
-    for group in range(2):
+    def stream_grads(group, chunk, carry):
+        rows = pl.ds(pl.multiple_of(chunk * 128, 128), 128)
+        one, two = ret[group, 0, rows, :].astype(f32), ret[group, 1, rows, :].astype(f32)
+        owners = [
+            cotangent[pl.ds(pl.multiple_of((chunk * 8 + i) * 32 + group * 16, 16), 16), :]
+            for i in range(8)
+        ]
+        factors = (
+            (one, jnp.concatenate(owners, axis=0)),
+            (two, values[group, rows, :]),
+            (two, keys[group, rows, :]),
+        )
+        for p, (value, factor) in enumerate(factors):
+            grads = (value * factor.astype(f32)).astype(bf16)
+            cgx[group * 3 + p, rows, 0:512] = grads
+            columns = pl.ds(pl.multiple_of(p * 256 + chunk * 128, 128), 128)
+            hout[group, :, columns] = grads[:, 0:128].T[0:16, :]
+        return carry
+
+    def tapped(group, p, rows, first, width, kept):
+        x = cgx[group * 3 + p, rows, first : first + width].astype(f32)
+        total = coltaps[group, rows, p : p + 1] * x
+        for j in (1, 2):
+            tap = coltaps[group, rows, 3 * j + p : 3 * j + p + 1]
+            total = total + tap * pltpu.roll(x, width - j, 1)
+        return total[:, :kept].astype(bf16)
+
+    def grad_rows(group, p, chunk):
+        return pl.ds(pl.multiple_of(group * 768 + p * 256 + chunk * 128, 128), 128)
+
+    def front(group, chunk, carry):
+        rows = pl.ds(pl.multiple_of(chunk * 128, 128), 128)
+        for p in range(3):
+            pgc[grad_rows(group, p, chunk), 0:384] = tapped(group, p, rows, 0, 512, 384)
+        return carry
+
+    def rest(group, chunk, carry):
+        rows = pl.ds(pl.multiple_of(chunk * 128, 128), 128)
+        for p in range(3):
+            columns = pl.ds(pl.multiple_of(p * 256 + chunk * 128, 128), 128)
+            edge = hin[group, :, columns].astype(f32)
+            edge = jnp.where(me == N_CTX - 1, jnp.zeros_like(edge), edge)
+            edge = jnp.concatenate([edge, jnp.zeros((112, 128), f32)], axis=0)
+            cgx[group * 3 + p, rows, 512:640] = edge.T.astype(bf16)
+            pgc[grad_rows(group, p, chunk), 384:512] = tapped(group, p, rows, 384, 256, 128)
+        return carry
+
+    def swap(group, part, first, count):
+        places = (pl.ds(group * 768, 768), pl.ds(first, count))
+        start(("grads", group, part), pgc.at[places], pgo.at[places], "twin")
+
+    def to_stream_grads(group, meanwhile):
         arrived(*(("back", step, group) for step in steps))
         kept[2 + group].wait()
-
-    def lanes(p, chunk):
-        return pl.ds(pl.multiple_of(p * 512 + chunk * 128, 128), 128)
-
-    def stream_grads(chunk, carry):
-        rows = pl.ds(pl.multiple_of(chunk * 128, 128), 128)
-        one, two = ret[0, rows, :].astype(f32), ret[1, rows, :].astype(f32)
-        factors = ((one, cotangent), (two, values), (two, keys))
-        for p, (value, factor) in enumerate(factors):
-            grad = (value * factor[rows, :].astype(f32)).astype(bf16)
-            cgx[p, rows, 0:512] = grad
-            hout[:, lanes(p, chunk)] = grad[:, 0:128].T[0:16, :]
+        lax.fori_loop(0, 2, functools.partial(stream_grads, group), 0)
+        start(("halo", group), hout.at[group], hin.at[group], "last")
+        lax.fori_loop(0, 2, functools.partial(front, group), 0)
+        swap(group, 0, 0, 384)
+        meanwhile()
+        arrived(("halo", group))
+        lax.fori_loop(0, 2, functools.partial(rest, group), 0)
+        swap(group, 1, 384, 128)
+
+    def whole_filter_grads():
+        lax.fori_loop(0, 4, filter_grads, 0)
+        for n in range(BLOCKS):
+            grad[:, block(n)] = held[2, n * 32 : (n + 1) * 32, :]
+
+    def by_position(chunk, carry):
+        for p in range(3):
+            pieces = []
+            for i in range(4):
+                for group in range(2):
+                    first = group * 768 + p * 256 + chunk * 64 + i * 16
+                    pieces.append(pgc[pl.ds(pl.multiple_of(first, 16), 16), :])
+            columns = pl.ds(pl.multiple_of(p * 512 + chunk * 128, 128), 128)
+            pgt[:, columns] = jnp.concatenate(pieces, axis=0).T
         return carry
-
-    lax.fori_loop(0, 4, stream_grads, 0)
-    start("halo", hout, hin, "last")
-
-    def tapped(p, rows, first, width, kept):
-        x = cgx[p, rows, first : first + width].astype(f32)
-        total = coltaps[rows, p : p + 1] * x
-        for j in (1, 2):
-            total = total + coltaps[rows, 3 * j + p : 3 * j + p + 1] * pltpu.roll(x, width - j, 1)
-        return total[:, :kept].astype(bf16)
-
-    def front(chunk, carry):
-        rows = pl.ds(pl.multiple_of(chunk * 128, 128), 128)
-        for p in range(3):
-            grad = tapped(p, rows, 0, 512, 384)
-            pgc[lanes(p, chunk), 0:384] = grad
-            pgt[0:384, lanes(p, chunk)] = grad.T
-        return carry
-
-    lax.fori_loop(0, 4, front, 0)
-    start("twin0", pgc.at[:, pl.ds(0, 384)], pgo.at[:, pl.ds(0, 384)], "twin")
-    arrived("halo")
-
-    def rest(chunk, carry):
-        rows = pl.ds(pl.multiple_of(chunk * 128, 128), 128)
-        for p in range(3):
-            first = hin[:, lanes(p, chunk)].astype(f32)
-            first = jnp.where(me == N_CTX - 1, jnp.zeros_like(first), first)
-            first = jnp.concatenate([first, jnp.zeros((112, 128), f32)], axis=0)
-            cgx[p, rows, 512:640] = first.T.astype(bf16)
-            grad = tapped(p, rows, 384, 256, 128)
-            pgc[lanes(p, chunk), 384:512] = grad
-            pgt[384:512, lanes(p, chunk)] = grad.T
-        return carry
-
-    lax.fori_loop(0, 4, rest, 0)
-    start("twin1", pgc.at[:, pl.ds(384, 128)], pgo.at[:, pl.ds(384, 128)], "twin")
 
     def input_tiles(first):
         def tile(step, carry):
@@ -455,22 +486,16 @@
         lax.fori_loop(0, 4, tile, 0)
 
     def acc_rows(slot, row, count):
-        return pl.ds(pl.multiple_of(slot * 1536 + row, 128), count)
-
-    def weight_part(slot, block, own=True, theirs=True):
+        return pl.ds(pl.multiple_of(slot * 768 + row, 16), count)
+
+    def weight_part(slot, group, block, own=True, theirs=True):
         mine = pl.ds(pl.multiple_of((2 * block + core) * 256, 256), 256)
         columns = pl.ds(pl.multiple_of(block * 256, 256), 256)
-
-        def half(step, carry):
-            rows = pl.ds(pl.multiple_of(step * 768, 256), 768)
-            kept = acc_rows(slot, step * 768, 768)
-            value = dot(pgc[rows, :], tok[16:528, mine]) if own else acc[kept, :]
-            if theirs:
-                value = value + dot(pgo[rows, :], oth[:, columns])
-            acc[kept, :] = value
-            return carry
-
-        lax.fori_loop(0, 2, half, 0)
+        rows, kept = slice(group * 768, group * 768 + 768), acc_rows(slot, 0, 768)
+        value = dot(pgc[rows, :], tok[16:528, mine]) if own else acc[kept, :]
+        if theirs:
+            value = value + dot(pgo[rows, :], oth[:, columns])
+        acc[kept, :] = value
 
     def fold(dst, slot, first, last, *terms):
         def chunk(step, carry):
@@ -491,7 +516,7 @@
     ztwo, zp, zm = lax.rem(z + 2, 4), lax.rem(z + 1, 4), lax.rem(z + 3, 4)
     xo = 1 - xh
     sides = (1 - xl, xl)
-    low, high = pl.ds(0, 768), pl.ds(768, 768)
+    low, high = pl.ds(0, 384), pl.ds(384, 384)
     parts = (slice(0, 2048), slice(2048, 4096))
 
     def ig_rows(side, z, first, count):
@@ -535,61 +560,105 @@
         ig_out[:, parts[h]] = ig_add(rows, h, zf.at[h, 1, 0], zf.at[h, 1, 1], xz.at[h])
 
     early = ((y2, xo), (yp, xo), (ym, xo))
-    for slot, place in enumerate(early):
-        weight_part(slot, block_of(*place), theirs=False)
-    arrived("twin0", "twin1")
-    for slot, place in enumerate(early):
-        weight_part(slot, block_of(*place), own=False)
-        fold(part.at[slot], slot, 0, 1536)
-        dst, peer = ((xin, "across"), (rf.at[0, 0], "up"), (rf.at[0, 1], "down"))[slot]
-        start((peer, 0), part.at[slot], dst, peer)
+
+    def first_blocks(group):
+        for n, place in enumerate(early):
+            weight_part(3 * group + n, group, block_of(*place), theirs=False)
+        arrived(("grads", group, 0), ("grads", group, 1))
+        for n, place in enumerate(early):
+            slot = 3 * group + n
+            weight_part(slot, group, block_of(*place), own=False)
+            fold(part.at[group, n], slot, 0, 768)
+            dst = (xin.at[group], rf.at[group, 0, 0], rf.at[group, 0, 1])[n]
+            peer = ("across", "up", "down")[n]
+            start((peer, 0, group), part.at[group, n], dst, peer)
+
+    def second_blocks(group):
+        weight_part(0, group, block_of(y2, xh))
+        arrived(("across", 0, group))
+        fold(part.at[group, 3], 0, 0, 768, (xin.at[group], 0))
+        start(("up", 2, group), part.at[group, 3, low], r2.at[group, 0], "up")
+        start(("down", 2, group), part.at[group, 3, high], r2.at[group, 1], "down")
+
+    def free_halves(group):
+        weight_part(2 * group, group, block_of(yp, xh))
+        fold(part.at[group, 4], 2 * group, 384, 768)
+        start(("upb", 1, group), part.at[group, 4, high], rf.at[group, 1, 0, high], "up")
+        weight_part(2 * group + 1, group, block_of(ym, xh))
+        fold(part.at[group, 5], 2 * group + 1, 0, 384)
+        start(("downa", 1, group), part.at[group, 5, low], rf.at[group, 1, 1, low], "down")
+
+    def side_blocks(group):
+        weight_part(4, group, block_of(y, xo))
+        arrived(("up", 0, group), ("down", 0, group))
+        sent[("across", 0, group)].wait_send()
+        terms = ((rf.at[group, 0, 0], 0), (rf.at[group, 0, 1], 0))
+        fold(part.at[group, 0], 4, 0, 768, *terms)
+        start(("across", 1, group), part.at[group, 0], xr.at[group], "across")
+
+    def bound_halves(group):
+        arrived(("up", 2, group))
+        fold(part.at[group, 4], 2 * group, 0, 384, (r2.at[group, 0], 0))
+        start(("upa", 1, group), part.at[group, 4, low], rf.at[group, 1, 0, low], "up")
+        arrived(("down", 2, group))
+        fold(part.at[group, 5], 2 * group + 1, 384, 768, (r2.at[group, 1], 384))
+        start(("downb", 1, group), part.at[group, 5, high], rf.at[group, 1, 1, high], "down")
+
+    def own_blocks(group):
+        names = (("across", 1), ("upa", 1), ("upb", 1), ("downa", 1), ("downb", 1))
+        arrived(*((*name, group) for name in names))
+
+        def chunk(step, carry):
+            rows = pl.ds(pl.multiple_of(step * 128, 128), 128)
+            place = acc_rows(4 + group, step * 128, 128)
+            total = acc[place, :]
+            for term in (rf.at[group, 1, 0], rf.at[group, 1, 1], xr.at[group]):
+                total = total + term[rows, :].astype(f32)
+            acc[place, :] = total
+            return carry
+
+        lax.fori_loop(0, 6, chunk, 0)
+
+    def last_fold(step, carry):
+        p, chunk = step // 4, lax.rem(step, 4)
+        pieces = []
+        for i in range(4):
+            for group in range(2):
+                pieces.append(acc[acc_rows(4 + group, p * 256 + chunk * 64 + i * 16, 16), :])
+        columns = pl.ds(pl.multiple_of(chunk * 128, 128), 128)
+        wg_out[p, :, columns] = jnp.concatenate(pieces, axis=0).T.astype(bf16)
+        return carry
+
+    to_stream_grads(0, whole_filter_grads)
+    first_blocks(0)
+    to_stream_grads(1, lambda: None)
+    first_blocks(1)
+    lax.fori_loop(0, 4, by_position, 0)
     input_tiles(0)
     z_first(0)
+    second_blocks(0)
     input_tiles(4)
     z_first(1)
+    second_blocks(1)
     z_second(0)
-    weight_part(1, block_of(yp, xh))
-    weight_part(2, block_of(ym, xh))
+    free_halves(0)
+    free_halves(1)
+    side_blocks(0)
+    side_blocks(1)
     z_second(1)
-    weight_part(0, block_of(y2, xh))
-    arrived(("across", 0))
-    fold(part.at[3], 0, 0, 1536, (xin, 0))
-    start("up2", part.at[3, low], r2.at[0], "up")
-    start("down2", part.at[3, high], r2.at[1], "down")
-    weight_part(0, block_of(y, xo))
-    arrived(("up", 0), ("down", 0))
-    sent[("across", 0)].wait_send()
-    fold(part.at[0], 0, 0, 1536, (rf.at[0, 0], 0), (rf.at[0, 1], 0))
-    start("across1", part.at[0], xr, "across")
-    fold(part.at[4], 1, 768, 1536)
-    start("up1b", part.at[4, high], rf.at[1, 0, high], "up")
-    fold(part.at[5], 2, 0, 768)
-    start("down1a", part.at[5, low], rf.at[1, 1, low], "down")
-    weight_part(0, block_of(y, xh))
+    bound_halves(0)
+    bound_halves(1)
+    for group in range(2):
+        weight_part(4 + group, group, block_of(y, xh))
     z_across(0)
     z_across(1)
-    arrived("up2")
-    fold(part.at[4], 1, 0, 768, (r2.at[0], 0))
-    start("up1a", part.at[4, low], rf.at[1, 0, low], "up")
-    arrived("down2")
-    fold(part.at[5], 2, 768, 1536, (r2.at[1], 768))
-    start("down1b", part.at[5, high], rf.at[1, 1, high], "down")
+    own_blocks(0)
     z_last(0)
     z_last(1)
-    arrived("across1", "up1a", "up1b", "down1a", "down1b")
-
-    def last_fold(step, carry):
-        rows = pl.ds(pl.multiple_of(step * 128, 128), 128)
-        total = acc[rows, :]
-        for term in (rf.at[1, 0], rf.at[1, 1], xr):
-            total = total + term[rows, :].astype(f32)
-        columns = pl.ds(pl.multiple_of(lax.rem(step, 4) * 128, 128), 128)
-        wg_out[step // 4, :, columns] = total.T.astype(bf16)
-        return carry
-
+    own_blocks(1)
     lax.fori_loop(0, 12, last_fold, 0)
     for name, copy in sent.items():
-        if name != ("across", 0):
+        if name[:2] != ("across", 0):
             copy.wait_send()
 
 
@@ -612,7 +681,7 @@
             vmem(N_CTX, 256, 1536),
             vmem(512, 512),
             wide(3, 3, 512),
-            wide(512, 16),
+            wide(2, 256, 16),
             wide(32, BLOCKS * LANES),
             wide(1, 32),
             wide(32, LANES),
@@ -621,31 +690,31 @@
             vmem(256, 256),
             vmem(64, 128),
             wide(2, 64, LANES),
-            vmem(512, 512),
-            vmem(512, 512),
+            vmem(2, 256, 512),
+            vmem(2, 256, 512),
             vmem(2, 512, 512),
             vmem(2, 32, BLOCKS * LANES),
             wide(3, 32 * BLOCKS, LANES),
             vmem(32 * BLOCKS, 2 * LANES),
-            vmem(2, 512, 512),
-            vmem(3, 512, 640),
-            vmem(16, 1536),
-            vmem(16, 1536),
+            vmem(2, 2, 256, 512),
+            vmem(6, 256, 640),
+            vmem(2, 16, 768),
+            vmem(2, 16, 768),
             vmem(1536, 512),
             vmem(512, 1536),
             vmem(1536, 512),
             vmem(512, 4096),
             wide(4608, 256),
-            vmem(6, 1536, 256),
-            vmem(1536, 256),
+            vmem(2, 6, 768, 256),
             vmem(2, 768, 256),
-            vmem(2, 2, 1536, 256),
-            vmem(1536, 256),
+            vmem(2, 2, 384, 256),
+            vmem(2, 2, 2, 768, 256),
+            vmem(2, 768, 256),
             vmem(2, 2, 2, 32, 2048),
             vmem(2, 2, 2, 64, 2048),
             vmem(2, 64, 2048),
-            pltpu.SemaphoreType.DMA((125,)),
-            pltpu.SemaphoreType.DMA((125,)),
+            pltpu.SemaphoreType.DMA((136,)),
+            pltpu.SemaphoreType.DMA((136,)),
             pltpu.SemaphoreType.DMA((18,)),
         ],
         compiler_params=pltpu.CompilerParams(
@@ -657,25 +726,28 @@
 
 
 def hand_out_kernel(*refs):
-    count = len(refs) // 2
-    copies = [
-        pltpu.make_async_copy(refs[index], refs[count + index], refs[-1].at[index])
-        for index in range(count)
-    ]
-    for copy in copies:
+    count = (len(refs) - 1) // 3
+    given, results, held, sem = refs[:count], refs[count : 2 * count], refs[2 * count : -1], refs[-1]
+    inward = [pltpu.make_async_copy(given[n], held[n], sem.at[n]) for n in range(count)]
+    outward = [pltpu.make_async_copy(held[n], results[n], sem.at[count + n]) for n in range(count)]
+    for copy in inward:
         copy.start()
-    for copy in copies:
+    for first, then in zip(inward, outward):
+        first.wait()
+        then.start()
+    for copy in outward:
         copy.wait()
 
 
 def hand_out(results):
-    in_hbm = pl.BlockSpec(memory_space=pltpu.HBM)
+    count = len(results)
     return pl.pallas_call(
         hand_out_kernel,
         out_shape=[jax.ShapeDtypeStruct(value.shape, value.dtype) for value in results],
-        in_specs=[in_hbm] * len(results),
-        out_specs=[in_hbm] * len(results),
-        scratch_shapes=[pltpu.SemaphoreType.DMA((len(results),))],
+        in_specs=[ANY] * count,
+        out_specs=[ANY] * count,
+        scratch_shapes=[pltpu.VMEM(value.shape, value.dtype) for value in results]
+        + [pltpu.SemaphoreType.DMA((2 * count,))],
         compiler_params=pltpu.CompilerParams(vmem_limit_bytes=63 * 1024 * 1024),
     )(*results)
 

time: 229 us -> 161 us (0.70)
  Pallas kernels: 228 us -> 159 us
    pallas_call x1, Pallas kernels: 72.6 us -> 2.65 us  [hand_out(): pl.pallas_call(hand_out_kernel, out_shape=[jax.ShapeDtypeStruct(value.sha...]
where the time goes in v8:
time: 161 us; the launch traced here: 160 us
  Pallas kernels  159 us (99%)
    pallas_call x1, Pallas kernels, mixer(): pl.pallas_call(mixer_kernel, out_shape=(jax.ShapeDtypeStruct((64, 4096),...  157 us

profile of v8, /device:TPU:1, one launch (start us, length us, event | category | flops | bytes accessed | tf_op | source)
XLA Modules:
  0.0 160.2 jit_solution(15193403416148401241)
XLA Ops:
  0.6 156.8 %shard_map.130 = (bf16[64,4096]{1,0:T(8,128)(2,1)}, bf16[3,256,512]{2,1,0:T(8,128)(2,1)}, f32[32,8192]{1,0:T(8,128)}) custom-call(bf16[512,4096]{1,0:T(8,128)(2,1)} %tokens.1, bf16[3,256,512]{2,1,0:T(8,128)(2,1)} %bitcast.3, bf16[512,512]{1,0:T(8,128)(2,1)} %cotangent_in.1, f32[3,3,512]{2,1,0:T(4,128)} %taps_in.1, f32[32,8192]{1,0:T(8,128)} %filters_in.1, ...), custom_call_target="tpu_custom_call" | custom-call | tf_op jit(solution)/shard_map/pallas_call | solution.py:669
  157.4 2.6 %shard_map.131 = (bf16[64,4096]{1,0:T(8,128)(2,1)}, bf16[3,256,512]{2,1,0:T(8,128)(2,1)}, f32[32,8192]{1,0:T(8,128)}) custom-call(bf16[64,4096]{1,0:T(8,128)(2,1)} %get-tuple-element.9.refs_0_, bf16[3,256,512]{2,1,0:T(8,128)(2,1)} %get-tuple-element.10.refs_1_, f32[32,8192]{1,0:T(8,128)} %get-tuple-element.11.refs_2_), custom_call_target="tpu_custom_call" | custom-call | tf_op jit(solution)/shard_map/pallas_call | solution.py:744

commit v9 on v8

--- a/solution.py
+++ b/solution.py
@@ -211,37 +211,38 @@
     pass_on("w_on0", below, 0, "up")
     arrived("w_down1")
     pass_on("w_on1", above, 1, "down")
-    pass_on("w_up1", me, 1, "up")
-    pass_on("w_down0", me, 0, "down")
     for one in loads:
         one.wait()
     arrived("w_halo", "w_twin")
     multiply(me, fresh=True)
     arrived("w_across")
+    hand_over("w_twin_side", side)
+    arrived("w_on0")
+    pass_on("w_up1", me, 1, "up")
+    arrived("w_on1")
+    pass_on("w_down0", me, 0, "down")
+    start("w_across_beyond", wall.at[beyond], wall.at[beyond], "across")
     pass_on("w_side_up0", side, 0, "up")
     pass_on("w_side_down1", side, 1, "down")
-    hand_over("w_twin_side", side)
-    arrived("w_on0", "w_on1")
-    start("w_across_beyond", wall.at[beyond], wall.at[beyond], "across")
     hand_over("w_twin_beyond", beyond)
-    pass_on("w_side_up1", side, 1, "up")
-    pass_on("w_side_down0", side, 0, "down")
     arrived("w_twin_side")
     multiply(side)
+    arrived("w_twin_beyond")
+    multiply(beyond)
     arrived("w_up1")
     hand_over("w_twin_below", below)
     arrived("w_down0")
     hand_over("w_twin_above", above)
-    arrived("w_twin_beyond")
-    multiply(beyond)
+    arrived("w_side_up0")
+    pass_on("w_side_up1", side, 1, "up")
+    pass_on("w_twin_sb0", side_below, 0, "twin")
+    arrived("w_side_down1")
+    pass_on("w_side_down0", side, 0, "down")
+    pass_on("w_twin_sa1", side_above, 1, "twin")
     arrived("w_twin_below")
     multiply(below)
     arrived("w_twin_above")
     multiply(above)
-    arrived("w_side_up0")
-    pass_on("w_twin_sb0", side_below, 0, "twin")
-    arrived("w_side_down1")
-    pass_on("w_twin_sa1", side_above, 1, "twin")
     arrived("w_across_beyond")
     hand_over("w_twin_across", side_beyond)
     arrived("w_twin_across")
@@ -299,8 +300,6 @@
         for step in steps:
             if step[0] == s:
                 start_out(step, 0)
-    for step in steps:
-        start_out(step, 1)
     kept = []
     for group in range(2):
         copy = pltpu.make_async_copy(
@@ -363,6 +362,9 @@
 
     for group in range(2):
         arrived(*(("out", step, group) for step in steps))
+        if group == 0:
+            for step in steps:
+                start_out(step, 1)
         kept[group].wait()
         own = slice(group * 16, group * 16 + 16)
         for n in range(BLOCKS):
@@ -444,14 +446,17 @@
         places = (pl.ds(group * 768, 768), pl.ds(first, count))
         start(("grads", group, part), pgc.at[places], pgo.at[places], "twin")
 
-    def to_stream_grads(group, meanwhile):
+    def begin_grads(group):
         arrived(*(("back", step, group) for step in steps))
         kept[2 + group].wait()
         lax.fori_loop(0, 2, functools.partial(stream_grads, group), 0)
         start(("halo", group), hout.at[group], hin.at[group], "last")
+
+    def most_grads(group):
         lax.fori_loop(0, 2, functools.partial(front, group), 0)
         swap(group, 0, 0, 384)
-        meanwhile()
+
+    def last_grads(group):
         arrived(("halo", group))
         lax.fori_loop(0, 2, functools.partial(rest, group), 0)
         swap(group, 1, 384, 128)
@@ -561,9 +566,11 @@
 
     early = ((y2, xo), (yp, xo), (ym, xo))
 
-    def first_blocks(group):
+    def own_halves(group):
         for n, place in enumerate(early):
             weight_part(3 * group + n, group, block_of(*place), theirs=False)
+
+    def first_blocks(group):
         arrived(("grads", group, 0), ("grads", group, 1))
         for n, place in enumerate(early):
             slot = 3 * group + n
@@ -629,13 +636,20 @@
         wg_out[p, :, columns] = jnp.concatenate(pieces, axis=0).T.astype(bf16)
         return carry
 
-    to_stream_grads(0, whole_filter_grads)
+    begin_grads(0)
+    most_grads(0)
+    whole_filter_grads()
+    last_grads(0)
+    own_halves(0)
+    begin_grads(1)
     first_blocks(0)
-    to_stream_grads(1, lambda: None)
-    first_blocks(1)
+    most_grads(1)
+    last_grads(1)
     lax.fori_loop(0, 4, by_position, 0)
     input_tiles(0)
     z_first(0)
+    own_halves(1)
+    first_blocks(1)
     second_blocks(0)
     input_tiles(4)
     z_first(1)

time: 161 us -> 158 us (0.981)
  Pallas kernels: 159 us -> 156 us
    pallas_call x1, Pallas kernels: 157 us -> 154 us  [mixer(): pl.pallas_call(mixer_kernel, out_shape=(jax.ShapeDtypeStruct((64, 4096),...]
where the time goes in v9:
time: 158 us; the launch traced here: 157 us
  Pallas kernels  156 us (99%)
    pallas_call x1, Pallas kernels, mixer(): pl.pallas_call(mixer_kernel, out_shape=(jax.ShapeDtypeStruct((64, 4096),...  154 us

profile of v9, /device:TPU:1, one launch (start us, length us, event | category | flops | bytes accessed | tf_op | source)
XLA Modules:
  0.0 157.3 jit_solution(15311434276766231386)
XLA Ops:
  0.6 153.8 %shard_map.130 = (bf16[64,4096]{1,0:T(8,128)(2,1)}, bf16[3,256,512]{2,1,0:T(8,128)(2,1)}, f32[32,8192]{1,0:T(8,128)}) custom-call(bf16[512,4096]{1,0:T(8,128)(2,1)} %tokens.1, bf16[3,256,512]{2,1,0:T(8,128)(2,1)} %bitcast.3, bf16[512,512]{1,0:T(8,128)(2,1)} %cotangent_in.1, f32[3,3,512]{2,1,0:T(4,128)} %taps_in.1, f32[32,8192]{1,0:T(8,128)} %filters_in.1, ...), custom_call_target="tpu_custom_call" | custom-call | tf_op jit(solution)/shard_map/pallas_call | solution.py:683
  154.5 2.6 %shard_map.131 = (bf16[64,4096]{1,0:T(8,128)(2,1)}, bf16[3,256,512]{2,1,0:T(8,128)(2,1)}, f32[32,8192]{1,0:T(8,128)}) custom-call(bf16[64,4096]{1,0:T(8,128)(2,1)} %get-tuple-element.9.refs_0_, bf16[3,256,512]{2,1,0:T(8,128)(2,1)} %get-tuple-element.10.refs_1_, f32[32,8192]{1,0:T(8,128)} %get-tuple-element.11.refs_2_), custom_call_target="tpu_custom_call" | custom-call | tf_op jit(solution)/shard_map/pallas_call | solution.py:758

commit v10 on v9

--- a/solution.py
+++ b/solution.py
@@ -211,19 +211,20 @@
     pass_on("w_on0", below, 0, "up")
     arrived("w_down1")
     pass_on("w_on1", above, 1, "down")
+    pass_on("w_up1", me, 1, "up")
+    pass_on("w_down0", me, 0, "down")
     for one in loads:
         one.wait()
     arrived("w_halo", "w_twin")
     multiply(me, fresh=True)
     arrived("w_across")
     hand_over("w_twin_side", side)
-    arrived("w_on0")
-    pass_on("w_up1", me, 1, "up")
-    arrived("w_on1")
-    pass_on("w_down0", me, 0, "down")
+    arrived("w_on0", "w_on1")
     start("w_across_beyond", wall.at[beyond], wall.at[beyond], "across")
     pass_on("w_side_up0", side, 0, "up")
     pass_on("w_side_down1", side, 1, "down")
+    pass_on("w_side_up1", side, 1, "up")
+    pass_on("w_side_down0", side, 0, "down")
     hand_over("w_twin_beyond", beyond)
     arrived("w_twin_side")
     multiply(side)
@@ -233,16 +234,14 @@
     hand_over("w_twin_below", below)
     arrived("w_down0")
     hand_over("w_twin_above", above)
-    arrived("w_side_up0")
-    pass_on("w_side_up1", side, 1, "up")
-    pass_on("w_twin_sb0", side_below, 0, "twin")
-    arrived("w_side_down1")
-    pass_on("w_side_down0", side, 0, "down")
-    pass_on("w_twin_sa1", side_above, 1, "twin")
     arrived("w_twin_below")
     multiply(below)
     arrived("w_twin_above")
     multiply(above)
+    arrived("w_side_up0")
+    pass_on("w_twin_sb0", side_below, 0, "twin")
+    arrived("w_side_down1")
+    pass_on("w_twin_sa1", side_above, 1, "twin")
     arrived("w_across_beyond")
     hand_over("w_twin_across", side_beyond)
     arrived("w_twin_across")
@@ -328,6 +327,8 @@
         return carry
 
     lax.fori_loop(0, 4, filter_spectra, 0)
+    for step in steps:
+        start_out(step, 1)
 
     def both_ways(start_at, step, carry):
         index = start_at + step * 4
@@ -362,9 +363,6 @@
 
     for group in range(2):
         arrived(*(("out", step, group) for step in steps))
-        if group == 0:
-            for step in steps:
-                start_out(step, 1)
         kept[group].wait()
         own = slice(group * 16, group * 16 + 16)
         for n in range(BLOCKS):
@@ -653,18 +651,18 @@
     second_blocks(0)
     input_tiles(4)
     z_first(1)
+    z_second(0)
+    side_blocks(0)
     second_blocks(1)
-    z_second(0)
+    z_second(1)
     free_halves(0)
     free_halves(1)
-    side_blocks(0)
     side_blocks(1)
-    z_second(1)
     bound_halves(0)
+    z_across(0)
     bound_halves(1)
     for group in range(2):
         weight_part(4 + group, group, block_of(y, xh))
-    z_across(0)
     z_across(1)
     own_blocks(0)
     z_last(0)

time: 158 us -> 150 us (0.949)
  Pallas kernels: 156 us -> 149 us
    pallas_call x1, Pallas kernels: 154 us -> 146 us  [mixer(): pl.pallas_call(mixer_kernel, out_shape=(jax.ShapeDtypeStruct((64, 4096),...]
where the time goes in v10:
time: 150 us
  Pallas kernels  149 us (99%)
    pallas_call x1, Pallas kernels, mixer(): pl.pallas_call(mixer_kernel, out_shape=(jax.ShapeDtypeStruct((64, 4096),...  146 us

profile of v10, /device:TPU:1, one launch (start us, length us, event | category | flops | bytes accessed | tf_op | source)
XLA Modules:
  0.0 149.8 jit_solution(13015816555872887088)
XLA Ops:
  0.6 146.4 %shard_map.130 = (bf16[64,4096]{1,0:T(8,128)(2,1)}, bf16[3,256,512]{2,1,0:T(8,128)(2,1)}, f32[32,8192]{1,0:T(8,128)}) custom-call(bf16[512,4096]{1,0:T(8,128)(2,1)} %tokens.1, bf16[3,256,512]{2,1,0:T(8,128)(2,1)} %bitcast.3, bf16[512,512]{1,0:T(8,128)(2,1)} %cotangent_in.1, f32[3,3,512]{2,1,0:T(4,128)} %taps_in.1, f32[32,8192]{1,0:T(8,128)} %filters_in.1, ...), custom_call_target="tpu_custom_call" | custom-call | tf_op jit(solution)/shard_map/pallas_call | solution.py:681
  147.0 2.6 %shard_map.131 = (bf16[64,4096]{1,0:T(8,128)(2,1)}, bf16[3,256,512]{2,1,0:T(8,128)(2,1)}, f32[32,8192]{1,0:T(8,128)}) custom-call(bf16[64,4096]{1,0:T(8,128)(2,1)} %get-tuple-element.9.refs_0_, bf16[3,256,512]{2,1,0:T(8,128)(2,1)} %get-tuple-element.10.refs_1_, f32[32,8192]{1,0:T(8,128)} %get-tuple-element.11.refs_2_), custom_call_target="tpu_custom_call" | custom-call | tf_op jit(solution)/shard_map/pallas_call | solution.py:756

commit v11 on v10

--- a/solution.py
+++ b/solution.py
@@ -244,12 +244,12 @@
     pass_on("w_twin_sa1", side_above, 1, "twin")
     arrived("w_across_beyond")
     hand_over("w_twin_across", side_beyond)
-    arrived("w_twin_across")
-    multiply(side_beyond)
     arrived("w_side_up1")
     pass_on("w_twin_sb1", side_below, 1, "twin")
     arrived("w_side_down0")
     pass_on("w_twin_sa0", side_above, 0, "twin")
+    arrived("w_twin_across")
+    multiply(side_beyond)
     arrived("w_twin_sb0", "w_twin_sb1")
     multiply(side_below)
     arrived("w_twin_sa0", "w_twin_sa1")
@@ -538,18 +538,17 @@
             src = ig.at[ig_rows(sides[k], ztwo, 32, 32), parts[h]]
             start(("z2m", h, k), src, z2.at[h, k, 1], "below")
 
-    def z_second(h):
-        for k in range(2):
-            arrived(("z2p", h, k))
-            rows = ig_rows(sides[k], zp, 0, 32)
-            ig[rows, parts[h]] = ig_add(rows, h, z2.at[h, k, 0])
-            src = ig.at[ig_rows(sides[k], zp, 0, 64), parts[h]]
-            start(("zfp", h, k), src, zf.at[h, k, 0], "above")
-            arrived(("z2m", h, k))
-            rows = ig_rows(sides[k], zm, 32, 32)
-            ig[rows, parts[h]] = ig_add(rows, h, z2.at[h, k, 1])
-            src = ig.at[ig_rows(sides[k], zm, 0, 64), parts[h]]
-            start(("zfm", h, k), src, zf.at[h, k, 1], "below")
+    def z_second(h, k):
+        arrived(("z2p", h, k))
+        rows = ig_rows(sides[k], zp, 0, 32)
+        ig[rows, parts[h]] = ig_add(rows, h, z2.at[h, k, 0])
+        src = ig.at[ig_rows(sides[k], zp, 0, 64), parts[h]]
+        start(("zfp", h, k), src, zf.at[h, k, 0], "above")
+        arrived(("z2m", h, k))
+        rows = ig_rows(sides[k], zm, 32, 32)
+        ig[rows, parts[h]] = ig_add(rows, h, z2.at[h, k, 1])
+        src = ig.at[ig_rows(sides[k], zm, 0, 64), parts[h]]
+        start(("zfm", h, k), src, zf.at[h, k, 1], "below")
 
     def z_across(h):
         arrived(("zfp", h, 0), ("zfm", h, 0))
@@ -651,19 +650,21 @@
     second_blocks(0)
     input_tiles(4)
     z_first(1)
-    z_second(0)
+    z_second(0, 0)
     side_blocks(0)
     second_blocks(1)
-    z_second(1)
+    z_second(1, 0)
     free_halves(0)
+    z_second(0, 1)
     free_halves(1)
     side_blocks(1)
     bound_halves(0)
+    z_second(1, 1)
     z_across(0)
     bound_halves(1)
+    z_across(1)
     for group in range(2):
         weight_part(4 + group, group, block_of(y, xh))
-    z_across(1)
     own_blocks(0)
     z_last(0)
     z_last(1)

time: 150 us -> 148 us (0.987)
  Pallas kernels: 149 us -> 147 us
    pallas_call x1, Pallas kernels: 146 us -> 144 us  [mixer(): pl.pallas_call(mixer_kernel, out_shape=(jax.ShapeDtypeStruct((64, 4096),...]
where the time goes in v11:
time: 148 us; the launch traced here: 147 us
  Pallas kernels  147 us (99%)
    pallas_call x1, Pallas kernels, mixer(): pl.pallas_call(mixer_kernel, out_shape=(jax.ShapeDtypeStruct((64, 4096),...  144 us

profile of v11, /device:TPU:1, one launch (start us, length us, event | category | flops | bytes accessed | tf_op | source)
XLA Modules:
  0.0 147.3 jit_solution(17308974852697134062)
XLA Ops:
  0.6 143.9 %shard_map.130 = (bf16[64,4096]{1,0:T(8,128)(2,1)}, bf16[3,256,512]{2,1,0:T(8,128)(2,1)}, f32[32,8192]{1,0:T(8,128)}) custom-call(bf16[512,4096]{1,0:T(8,128)(2,1)} %tokens.1, bf16[3,256,512]{2,1,0:T(8,128)(2,1)} %bitcast.3, bf16[512,512]{1,0:T(8,128)(2,1)} %cotangent_in.1, f32[3,3,512]{2,1,0:T(4,128)} %taps_in.1, f32[32,8192]{1,0:T(8,128)} %filters_in.1, ...), custom_call_target="tpu_custom_call" | custom-call | tf_op jit(solution)/shard_map/pallas_call | solution.py:682
  144.5 2.6 %shard_map.131 = (bf16[64,4096]{1,0:T(8,128)(2,1)}, bf16[3,256,512]{2,1,0:T(8,128)(2,1)}, f32[32,8192]{1,0:T(8,128)}) custom-call(bf16[64,4096]{1,0:T(8,128)(2,1)} %get-tuple-element.9.refs_0_, bf16[3,256,512]{2,1,0:T(8,128)(2,1)} %get-tuple-element.10.refs_1_, f32[32,8192]{1,0:T(8,128)} %get-tuple-element.11.refs_2_), custom_call_target="tpu_custom_call" | custom-call | tf_op jit(solution)/shard_map/pallas_call | solution.py:757

commit v12 on v11

--- a/solution.py
+++ b/solution.py
@@ -211,23 +211,23 @@
     pass_on("w_on0", below, 0, "up")
     arrived("w_down1")
     pass_on("w_on1", above, 1, "down")
-    pass_on("w_up1", me, 1, "up")
-    pass_on("w_down0", me, 0, "down")
     for one in loads:
         one.wait()
     arrived("w_halo", "w_twin")
     multiply(me, fresh=True)
+    pass_on("w_up1", me, 1, "up")
+    pass_on("w_down0", me, 0, "down")
     arrived("w_across")
     hand_over("w_twin_side", side)
     arrived("w_on0", "w_on1")
     start("w_across_beyond", wall.at[beyond], wall.at[beyond], "across")
     pass_on("w_side_up0", side, 0, "up")
     pass_on("w_side_down1", side, 1, "down")
-    pass_on("w_side_up1", side, 1, "up")
-    pass_on("w_side_down0", side, 0, "down")
     hand_over("w_twin_beyond", beyond)
     arrived("w_twin_side")
     multiply(side)
+    pass_on("w_side_up1", side, 1, "up")
+    pass_on("w_side_down0", side, 0, "down")
     arrived("w_twin_beyond")
     multiply(beyond)
     arrived("w_up1")
@@ -561,7 +561,7 @@
         rows = ig_rows(sides[1], z, 0, 64)
         ig_out[:, parts[h]] = ig_add(rows, h, zf.at[h, 1, 0], zf.at[h, 1, 1], xz.at[h])
 
-    early = ((y2, xo), (yp, xo), (ym, xo))
+    early = ((yp, xo), (ym, xo), (y2, xo))
 
     def own_halves(group):
         for n, place in enumerate(early):
@@ -573,8 +573,8 @@
             slot = 3 * group + n
             weight_part(slot, group, block_of(*place), own=False)
             fold(part.at[group, n], slot, 0, 768)
-            dst = (xin.at[group], rf.at[group, 0, 0], rf.at[group, 0, 1])[n]
-            peer = ("across", "up", "down")[n]
+            dst = (rf.at[group, 0, 0], rf.at[group, 0, 1], xin.at[group])[n]
+            peer = ("up", "down", "across")[n]
             start((peer, 0, group), part.at[group, n], dst, peer)
 
     def second_blocks(group):
@@ -597,8 +597,8 @@
         arrived(("up", 0, group), ("down", 0, group))
         sent[("across", 0, group)].wait_send()
         terms = ((rf.at[group, 0, 0], 0), (rf.at[group, 0, 1], 0))
-        fold(part.at[group, 0], 4, 0, 768, *terms)
-        start(("across", 1, group), part.at[group, 0], xr.at[group], "across")
+        fold(part.at[group, 2], 4, 0, 768, *terms)
+        start(("across", 1, group), part.at[group, 2], xr.at[group], "across")
 
     def bound_halves(group):
         arrived(("up", 2, group))

time: 148 us -> 148 us (level)
  no operation moved by 1% of the time
where the time goes in v12:
time: 148 us; the launch traced here: 147 us
  Pallas kernels  147 us (99%)
    pallas_call x1, Pallas kernels, mixer(): pl.pallas_call(mixer_kernel, out_shape=(jax.ShapeDtypeStruct((64, 4096),...  144 us

profile of v12, /device:TPU:1, one launch (start us, length us, event | category | flops | bytes accessed | tf_op | source)
XLA Modules:
  0.0 147.5 jit_solution(11836706318143714775)
XLA Ops:
  0.6 144.0 %shard_map.130 = (bf16[64,4096]{1,0:T(8,128)(2,1)}, bf16[3,256,512]{2,1,0:T(8,128)(2,1)}, f32[32,8192]{1,0:T(8,128)}) custom-call(bf16[512,4096]{1,0:T(8,128)(2,1)} %tokens.1, bf16[3,256,512]{2,1,0:T(8,128)(2,1)} %bitcast.3, bf16[512,512]{1,0:T(8,128)(2,1)} %cotangent_in.1, f32[3,3,512]{2,1,0:T(4,128)} %taps_in.1, f32[32,8192]{1,0:T(8,128)} %filters_in.1, ...), custom_call_target="tpu_custom_call" | custom-call | tf_op jit(solution)/shard_map/pallas_call | solution.py:682
  144.6 2.6 %shard_map.131 = (bf16[64,4096]{1,0:T(8,128)(2,1)}, bf16[3,256,512]{2,1,0:T(8,128)(2,1)}, f32[32,8192]{1,0:T(8,128)}) custom-call(bf16[64,4096]{1,0:T(8,128)(2,1)} %get-tuple-element.9.refs_0_, bf16[3,256,512]{2,1,0:T(8,128)(2,1)} %get-tuple-element.10.refs_1_, f32[32,8192]{1,0:T(8,128)} %get-tuple-element.11.refs_2_), custom_call_target="tpu_custom_call" | custom-call | tf_op jit(solution)/shard_map/pallas_call | solution.py:757

commit v13 on v12

--- a/solution.py
+++ b/solution.py
@@ -107,7 +107,7 @@
     me = lax.axis_index("ctx")
     at["across"] = {"ctx": (y * 2 + 1 - xh) * 2 + core}
     at["next"] = {"ctx": lax.rem(me + 1, N_CTX)}
-    steps = [(s, i) for s in range(4) for i in range(4)][1:]
+    steps = [(s, i) for i in range(4) for s in (1, 3, 2, 0) if (s, i) != (0, 0)]
     fourth = lax.rem(me, 4)
 
     def peer_of(s, i):
@@ -285,7 +285,7 @@
         peer = peer_of(*step)
         start(("out", step, group), rows_of(out, peer, group), positions_of(arr, me, group), step)
 
-    for s in range(4):
+    for s in (1, 3, 2, 0):
         chunk = lax.rem(y + s, 4)
         rows = pl.ds(pl.multiple_of(chunk * 128, 128), 128)
         query, key, value = (filtered(p, chunk) for p in range(3))
@@ -738,11 +738,22 @@
     )
 
 
+def pieces_of(shapes):
+    cuts = []
+    for index, shape in enumerate(shapes):
+        size = max(1, shape[0] // 4)
+        cuts += [(index, pl.ds(first, size)) for first in range(0, shape[0], size)]
+    return cuts
+
+
 def hand_out_kernel(*refs):
     count = (len(refs) - 1) // 3
     given, results, held, sem = refs[:count], refs[count : 2 * count], refs[2 * count : -1], refs[-1]
-    inward = [pltpu.make_async_copy(given[n], held[n], sem.at[n]) for n in range(count)]
-    outward = [pltpu.make_async_copy(held[n], results[n], sem.at[count + n]) for n in range(count)]
+    inward, outward = [], []
+    for place, (n, rows) in enumerate(pieces_of([ref.shape for ref in given])):
+        first, second = sem.at[0, place], sem.at[1, place]
+        inward.append(pltpu.make_async_copy(given[n].at[rows], held[n].at[rows], first))
+        outward.append(pltpu.make_async_copy(held[n].at[rows], results[n].at[rows], second))
     for copy in inward:
         copy.start()
     for first, then in zip(inward, outward):
@@ -760,7 +771,7 @@
         in_specs=[ANY] * count,
         out_specs=[ANY] * count,
         scratch_shapes=[pltpu.VMEM(value.shape, value.dtype) for value in results]
-        + [pltpu.SemaphoreType.DMA((2 * count,))],
+        + [pltpu.SemaphoreType.DMA((2, len(pieces_of([value.shape for value in results]))))],
         compiler_params=pltpu.CompilerParams(vmem_limit_bytes=63 * 1024 * 1024),
     )(*results)
 

time: 148 us -> 147 us (level)
  no operation moved by 1% of the time
where the time goes in v13:
time: 147 us
  Pallas kernels  146 us (99%)
    pallas_call x1, Pallas kernels, mixer(): pl.pallas_call(mixer_kernel, out_shape=(jax.ShapeDtypeStruct((64, 4096),...  143 us

profile of v13, /device:TPU:1, one launch (start us, length us, event | category | flops | bytes accessed | tf_op | source)
XLA Modules:
  0.0 146.6 jit_solution(16866905492146697996)
XLA Ops:
  0.6 143.1 %shard_map.130 = (bf16[64,4096]{1,0:T(8,128)(2,1)}, bf16[3,256,512]{2,1,0:T(8,128)(2,1)}, f32[32,8192]{1,0:T(8,128)}) custom-call(bf16[512,4096]{1,0:T(8,128)(2,1)} %tokens.1, bf16[3,256,512]{2,1,0:T(8,128)(2,1)} %bitcast.3, bf16[512,512]{1,0:T(8,128)(2,1)} %cotangent_in.1, f32[3,3,512]{2,1,0:T(4,128)} %taps_in.1, f32[32,8192]{1,0:T(8,128)} %filters_in.1, ...), custom_call_target="tpu_custom_call" | custom-call | tf_op jit(solution)/shard_map/pallas_call | solution.py:682
  143.8 2.6 %shard_map.131 = (bf16[64,4096]{1,0:T(8,128)(2,1)}, bf16[3,256,512]{2,1,0:T(8,128)(2,1)}, f32[32,8192]{1,0:T(8,128)}) custom-call(bf16[64,4096]{1,0:T(8,128)(2,1)} %get-tuple-element.9.refs_0_, bf16[3,256,512]{2,1,0:T(8,128)(2,1)} %get-tuple-element.10.refs_1_, f32[32,8192]{1,0:T(8,128)} %get-tuple-element.11.refs_2_), custom_call_target="tpu_custom_call" | custom-call | tf_op jit(solution)/shard_map/pallas_call | solution.py:768
